TPU v7x, 256 devices: a whole 4x4x8 slice. The times are simulated.
256 devices in a mesh: inst: 16 (over y_lo, z), samp: 16 (over y_hi, x, core).
Axes of the slice: x: 4, y: 4 (y_hi: 2, y_lo: 2; y = y_hi * 2 + y_lo), z: 8, core: 2. Of those that a mesh axis runs over, the one named last changes fastest.
Arguments:
- prompt_key_values: bfloat16 [16, 4096, 2, 1024], P('inst', 'samp'), may hold values from -6 to 6
- match: int32 [16], replicated, may hold values from 0 to 15, each once
- page_list: int32 [16, 16, 16], P('inst'), may hold values from 0 to 255, as said below
- queries: bfloat16 [16, 128, 12288], P('inst', 'samp'), may hold values from -240 to 240
- sample_key_values: bfloat16 [16, 128, 128, 2, 1024], P('inst', 'samp'), may hold values from -10 to 10
- gen_len: int32 [16, 128], P('inst', 'samp'), may hold values from 1 to 128, 8192 in all within a row
Outputs:
- attended: bfloat16 [16, 128, 12288], P('inst', 'samp')
- prompt_pool: bfloat16 [16, 256, 16, 2, 1024], P('inst', 'samp')
Inputs may be any that keep to these rules, and one draw needn't show every extreme that they name: `match`: each decode instance continues a different prefill instance. `page_list`: each list holds 16 distinct pages and the lists of one instance together hold every page of the prompt once; of the pages p with p // 16 equal to one value, one owner's list holds at most 2, and exactly 2 for some owner.
All inputs are finite; a program needn't handle non-finite values. No bound on the sum of `gen_len` on one device may be relied on, other than what follows from the above.
Results may differ from a plain program's by a relative error of at most 0.0065.
Values may be sent and summed in bfloat16 or wider, within the bound.
No kernel may reach another device: no remote copies, remote signals or barrier semaphores. Data moves between devices by JAX's collectives and lax.ppermute only.
A program may use at most 128 MiB of HBM per device.

v0:
```python
import jax
import jax.numpy as jnp
from jax import lax
from jax.sharding import PartitionSpec as P

QUERY_HEADS = 96
KEY_VALUE_HEADS = 8
HEAD_FEATURES = 128
PAGE_TOKENS = 16


def partial_shared(query_rows, key_rows, value_rows):
    count = query_rows.shape[0]
    group_count = QUERY_HEADS // KEY_VALUE_HEADS
    width = group_count * HEAD_FEATURES
    peaks = []
    sums = []
    numers = []
    for head in range(KEY_VALUE_HEADS):
        block = query_rows[:, head * width : (head + 1) * width].reshape(
            count * group_count, HEAD_FEATURES
        )
        key_block = key_rows[:, head * HEAD_FEATURES : (head + 1) * HEAD_FEATURES]
        value_block = value_rows[:, head * HEAD_FEATURES : (head + 1) * HEAD_FEATURES]
        scores = lax.dot_general(
            block, key_block, (((1,), (1,)), ((), ())), preferred_element_type=jnp.float32
        ) * HEAD_FEATURES ** (-0.5)
        peak = jnp.max(scores, axis=-1)
        weights = jnp.exp(scores - peak[:, None])
        weight_sum = jnp.sum(weights, axis=-1)
        numer = jnp.dot(
            weights.astype(jnp.bfloat16), value_block, preferred_element_type=jnp.float32
        )
        peaks.append(peak.reshape(count, group_count))
        sums.append(weight_sum.reshape(count, group_count))
        numers.append(numer.reshape(count, group_count, HEAD_FEATURES))
    return (jnp.stack(peaks, axis=1), jnp.stack(sums, axis=1), jnp.stack(numers, axis=1))


def partial_own(query_rows, sample_keys, sample_values, live_mask):
    count = query_rows.shape[0]
    group_count = QUERY_HEADS // KEY_VALUE_HEADS
    width = group_count * HEAD_FEATURES
    peaks = []
    sums = []
    numers = []
    for head in range(KEY_VALUE_HEADS):
        block = query_rows[:, head * width : (head + 1) * width].reshape(
            count, group_count, HEAD_FEATURES
        )
        key_block = sample_keys[:, :, head * HEAD_FEATURES : (head + 1) * HEAD_FEATURES]
        value_block = sample_values[:, :, head * HEAD_FEATURES : (head + 1) * HEAD_FEATURES]
        scores = jnp.einsum(
            "sgd,snd->sgn", block, key_block, preferred_element_type=jnp.float32
        ) * HEAD_FEATURES ** (-0.5)
        scores = jnp.where(live_mask[:, None, :], scores, -jnp.inf)
        peak = jnp.max(scores, axis=-1)
        weights = jnp.exp(scores - peak[..., None])
        weight_sum = jnp.sum(weights, axis=-1)
        numer = jnp.einsum(
            "sgn,snd->sgd",
            weights.astype(jnp.bfloat16),
            value_block,
            preferred_element_type=jnp.float32,
        )
        peaks.append(peak)
        sums.append(weight_sum)
        numers.append(numer)
    return (jnp.stack(peaks, axis=1), jnp.stack(sums, axis=1), jnp.stack(numers, axis=1))


def combine(first, second):
    peak = jnp.maximum(first[0], second[0])
    scale_first = jnp.exp(first[0] - peak)
    scale_second = jnp.exp(second[0] - peak)
    weight_sum = first[1] * scale_first + second[1] * scale_second
    numerator = first[2] * scale_first[..., None] + second[2] * scale_second[..., None]
    return (peak, weight_sum, numerator)


def body(prompt_key_values, match, page_list, queries, sample_key_values, gen_len):
    feature_count = KEY_VALUE_HEADS * HEAD_FEATURES
    pieces = lax.all_to_all(prompt_key_values, "inst", split_axis=1, concat_axis=0, tiled=True)
    chosen = jnp.take(pieces, match, axis=0)
    own_shard = lax.all_to_all(chosen, "inst", split_axis=0, concat_axis=1, tiled=True)
    local_total = queries.shape[1]
    local_queries = queries[0]
    sample_keys = sample_key_values[0, :, :, 0, :]
    sample_values = sample_key_values[0, :, :, 1, :]
    live_mask = jnp.arange(sample_keys.shape[1], dtype=jnp.int32)[None, :] < gen_len[0][:, None]
    own_state = partial_own(local_queries, sample_keys, sample_values, live_mask)
    member = lax.axis_index("samp")
    list_table = page_list[0]
    my_list = lax.dynamic_index_in_dim(list_table, member, 0, keepdims=False)
    pages_dev = list_table.shape[1]
    empty_pool = jnp.zeros((pages_dev, PAGE_TOKENS, 2, feature_count), prompt_key_values.dtype)
    page_pool = empty_pool
    running = own_state
    segment_rows = lax.all_gather(own_shard, "samp", axis=1, tiled=True)[0]
    segment_length = segment_rows.shape[0]
    token_index = my_list[:, None] * PAGE_TOKENS + jnp.arange(PAGE_TOKENS, dtype=jnp.int32)[None, :]
    inside = (token_index >= 0) & (token_index < segment_length)
    selected_pages = jnp.take(segment_rows, jnp.clip(token_index, 0, segment_length - 1), axis=0)
    page_pool = jnp.where(inside[:, :, None, None], selected_pages, page_pool)
    running = combine(
        running, partial_shared(local_queries, segment_rows[:, 0, :], segment_rows[:, 1, :])
    )
    page_pool, running = (page_pool, running)
    final_peak, final_sum, final_numer = running
    attended = (
        (final_numer / final_sum[..., None])
        .astype(jnp.bfloat16)
        .reshape(1, local_total, QUERY_HEADS * HEAD_FEATURES)
    )
    return (attended, page_pool[None])


def solution(mesh):
    in_specs = (
        P("inst", "samp", None, None),
        P(),
        P("inst", None, None),
        P("inst", "samp", None),
        P("inst", "samp", None, None, None),
        P("inst", "samp"),
    )
    out_specs = (P("inst", "samp", None), P("inst", "samp", None, None, None))
    return jax.shard_map(body, mesh=mesh, in_specs=in_specs, out_specs=out_specs, check_vma=False)
```

profile of v0, /device:TPU:1, one launch (start us, length us, event | category | flops | bytes accessed | tf_op | source)
XLA Modules:
  0.0 294.2 jit_solution(93938128179282142)
XLA Ops:
  7.2 10.1 %all-to-all-start = ((bf16[1,256,2,1024]{3,2,0,1:T(2,128)(2,1)}), bf16[1,256,2,1024]{3,2,0,1:T(2,128)(2,1)S(1)}, u32[]{:S(2)}, u32[]{:S(2)}) async-start(bf16[1,256,2,1024]{3,2,0,1:T(2,128)(2,1)} %bitcast.112), calls=%async_computation | async-start | bytes 2097152 | tf_op jit(solution)/shard_map/all_to_all | solution.py:83
  17.4 25.6 %all-to-all-done = bf16[1,256,2,1024]{3,2,0,1:T(2,128)(2,1)S(1)} async-done(((bf16[1,256,2,1024]{3,2,0,1:T(2,128)(2,1)}), bf16[1,256,2,1024]{3,2,0,1:T(2,128)(2,1)S(1)}, u32[]{:S(2)}, u32[]{:S(2)}) %all-to-all-start) | async-done | bytes 1048608 | tf_op jit(solution)/shard_map/all_to_all | solution.py:83
  43.0 0.3 copy.60
  43.3 0.6 gather_fusion
  44.1 30.2 %all_to_all.24 = bf16[16,16,2,1024]{3,1,2,0:T(8,128)(2,1)S(1)} all-to-all(bf16[16,16,2,1024]{3,1,2,0:T(8,128)(2,1)S(1)} %broadcast_select_fusion.2), channel_id=1, replica_groups=mesh['inst'=16,'samp'=16] {'inst'}, dimensions={0} | all-to-all | bytes 2097152 | tf_op jit(solution)/shard_map/all_to_all | solution.py:85
  74.4 2.0 copy.62
  76.5 0.7 multiply_bitcast_fusion
  78.1 9.0 %fusion.139 = (bf16[1,8,128,1,1024]{4,3,2,1,0:T(2,128)(2,1)S(1)}, bf16[1,8,128,1,1024]{4,3,2,1,0:T(2,128)(2,1)S(1)}) fusion(bf16[1,8,128,2,1024]{4,3,2,1,0:T(2,128)(2,1)} %param.10), kind=kLoop, calls=%fused_computation.231 | loop fusion | bytes 8388608 | tf_op jit(solution)/shard_map/slice | solution.py:88
  87.0 3.1 %copy_bitcast_fusion.2 = (bf16[8,128,1024]{2,1,0:T(8,128)(2,1)S(1)}, bf16[8,128,1024]{2,1,0:T(8,128)(2,1)}) fusion(bf16[1,8,128,1,1024]{4,3,2,1,0:T(2,128)(2,1)S(1)} %get-tuple-element.8, bf16[1,8,128,1,1024]{4,3,2,1,0:T(2,128)(2,1)S(1)} %get-tuple-element.7), kind=kLoop, calls=%fused_computation.12 | loop fusion | bytes 8388608 | tf_op jit(solution)/shard_map/squeeze | solution.py:89
  90.1 1.3 fusion.155
  91.6 1.3 fusion.154
  93.1 1.3 fusion.153
  94.5 1.3 fusion.152
  96.0 1.3 fusion.151
  97.5 1.3 fusion.150
  98.9 1.3 fusion.149
  100.4 1.3 fusion.148
  104.1 89.4 %all-gather.2.cloned.1.call-done = bf16[1,4096,2,1024]{3,2,0,1:T(2,128)(2,1)} async-done(((bf16[1,256,2,1024]{3,2,0,1:T(2,128)(2,1)}), bf16[1,4096,2,1024]{3,2,0,1:T(2,128)(2,1)}) %all-gather.2.cloned.1.call-update) | async-done | bytes 16777232 | tf_op jit(solution)/shard_map/all_gather | solution.py:99
  193.5 32.5 %fusion.138 = (bf16[4096,1,1024]{2,1,0:T(2,128)(2,1)S(1)}, bf16[4096,1,1024]{2,1,0:T(2,128)(2,1)}) fusion(bf16[4096,2,1024]{2,1,0:T(2,128)(2,1)} %bitcast.107), kind=kLoop, calls=%fused_computation.230 | loop fusion | bytes 33554432 | tf_op jit(solution)/shard_map/slice | solution.py:106
  226.0 16.8 %copy_bitcast_fusion = (bf16[4096,1024]{1,0:T(8,128)(2,1)}, bf16[4096,1024]{1,0:T(8,128)(2,1)}) fusion(bf16[4096,1,1024]{2,1,0:T(2,128)(2,1)} %get-tuple-element.6, bf16[4096,1,1024]{2,1,0:T(2,128)(2,1)S(1)} %get-tuple-element.5), kind=kLoop, calls=%fused_computation.2 | loop fusion | bytes 33554432
  242.7 1.8 fusion.147
  244.6 0.4 fusion.14
  245.0 1.7 fusion.32
  246.6 1.8 fusion.146
  248.4 0.4 fusion.12
  248.8 1.7 fusion.34
  250.6 1.9 fusion.145
  252.4 0.4 fusion.10
  252.8 1.7 fusion.36
  254.6 1.8 fusion.144
  256.4 0.4 fusion.8
  256.8 1.7 fusion.38
  258.5 1.8 fusion.143
  260.3 0.4 fusion.6
  260.7 1.7 fusion.40
  262.4 1.8 fusion.142
  264.2 0.4 fusion.4
  264.6 1.7 fusion.42
  266.4 1.8 fusion.141
  268.2 0.4 fusion.2
  268.6 1.7 fusion.44
  270.2 1.8 fusion.140
  272.0 1.7 fusion.46
  273.7 0.4 fusion
  274.2 8.5 %gather_fusion.1 = bf16[256,2,1024]{2,1,0:T(2,128)(2,1)S(1)} fusion(bf16[4096,2,1024]{2,1,0:T(2,128)(2,1)} %bitcast.108, s32[1024]{0:T(1024)S(1)} %pad_clamp_fusion), kind=kCustom, calls=%fused_computation.1 | custom fusion | bytes 2098176 | tf_op jit(solution)/shard_map/jit(_take)/gather | solution.py:103
  283.8 0.5 divide_convert_fusion
  284.3 0.8 convert_element_type.86
  285.1 2.2 broadcast_select_fusion.1
  (109 shorter events, 6.3 us)
Async XLA Ops:
  7.2 10.2 %copy-start.1 = (s32[16]{0:T(128)S(1)}, s32[16]{0:T(128)}, u32[]{:S(2)}) copy-start(s32[16]{0:T(128)} %param.7) | copy-start | bytes 196
  7.2 35.8 %all-to-all-start = ((bf16[1,256,2,1024]{3,2,0,1:T(2,128)(2,1)}), bf16[1,256,2,1024]{3,2,0,1:T(2,128)(2,1)S(1)}, u32[]{:S(2)}, u32[]{:S(2)}) async-start(bf16[1,256,2,1024]{3,2,0,1:T(2,128)(2,1)} %bitcast.112), calls=%async_computation | async-start | bytes 2097152 | tf_op jit(solution)/shard_map/all_to_all | solution.py:83
  17.3 176.2 %all-gather.2.cloned.1.call-start = ((), (), s32[]{:S(2)}) async-start(), calls=%async_computation.2 | async-start | bytes 17825792 | tf_op jit(solution)/shard_map/all_gather | solution.py:99
  74.4 3.0 %copy-start = (bf16[1,8,12288]{2,1,0:T(8,128)(2,1)S(1)}, bf16[1,8,12288]{2,1,0:T(8,128)(2,1)}, u32[]{:S(2)}) copy-start(bf16[1,8,12288]{2,1,0:T(8,128)(2,1)} %param.9) | copy-start | bytes 589828
  74.4 3.6 %copy-start.2 = (s32[1,8]{1,0:T(1,128)S(1)}, s32[1,8]{1,0:T(1,128)}, u32[]{:S(2)}) copy-start(s32[1,8]{1,0:T(1,128)} %param.11) | copy-start | bytes 100
Sparse Core Ops, SparseCore 0:
  76.6 116.8 all-gather.1
where the time goes:
time: 295 us; the launch traced here: 294 us
  waiting for transfers between devices  115 us (39%)
  local copies, waits for them, and re-layouts  75.7 us (26%)
  matrix products  39.7 us (13%)
  blocking collectives  30.2 us (10%)
  between operations  14.8 us (5%)
  starting transfers between devices  10.2 us (3%)
  other arithmetic  8.6 us (3%)
    all_gather x1, waiting for transfers between devices, body(): segment_rows = lax.all_gather(own_shard, 'samp', axis=1, tiled=True)[0]  89.4 us
    slice x1, local copies, waits for them, and re-layouts, body(): segment_rows[:, 0, :]  32.5 us
    all_to_all x1, blocking collectives, body(): lax.all_to_all(chosen, 'inst', split_axis=0, concat_axis=1, tiled=True)  30.2 us
    all_to_all x1, waiting for transfers between devices, body(): lax.all_to_all(prompt_key_values, 'inst', split_axis=1, concat_axis=0, ti...  25.6 us
    unnamed x42, local copies, waits for them, and re-layouts  16.9 us
    dot_general x8, matrix products, partial_shared(): lax.dot_general(block, key_block, (((1,), (1,)), ((), ())), preferred_ele...  14.5 us
    dot_general x8, matrix products, partial_shared(): jnp.dot(weights.astype(jnp.bfloat16), value_block, preferred_element_type...  13.2 us
    all_to_all x1, starting transfers between devices, body(): lax.all_to_all(prompt_key_values, 'inst', split_axis=1, concat_axis=0, ti...  10.1 us
  transfers between devices with their start and end apart: 2, of which 2 were waited for; matrix products, arithmetic and copies ran while one was open for 9% of the time, Pallas kernels for 0%

commit v1 on v0

v1 whole, which is shorter than its diff:
```python
import functools
import math

import jax
import jax.numpy as jnp
from jax import lax
from jax.experimental import pallas as pl
from jax.experimental.pallas import tpu as pltpu
from jax.sharding import PartitionSpec as P

QUERY_HEADS = 96
KEY_VALUE_HEADS = 8
HEAD_FEATURES = 128
PAGE_TOKENS = 16
GROUP = QUERY_HEADS // KEY_VALUE_HEADS
WIDTH = GROUP * HEAD_FEATURES
SCALE = HEAD_FEATURES ** (-0.5)


def partial_own(query_rows, sample_keys, sample_values, live_mask):
    count = query_rows.shape[0]
    peaks = []
    sums = []
    numers = []
    for head in range(KEY_VALUE_HEADS):
        block = query_rows[:, head * WIDTH : (head + 1) * WIDTH].reshape(
            count, GROUP, HEAD_FEATURES
        )
        key_block = sample_keys[:, :, head * HEAD_FEATURES : (head + 1) * HEAD_FEATURES]
        value_block = sample_values[:, :, head * HEAD_FEATURES : (head + 1) * HEAD_FEATURES]
        scores = jnp.einsum(
            "sgd,snd->sgn", block, key_block, preferred_element_type=jnp.float32
        ) * SCALE
        scores = jnp.where(live_mask[:, None, :], scores, -jnp.inf)
        peak = jnp.max(scores, axis=-1)
        weights = jnp.exp(scores - peak[..., None])
        weight_sum = jnp.sum(weights, axis=-1)
        numer = jnp.einsum(
            "sgn,snd->sgd",
            weights.astype(jnp.bfloat16),
            value_block,
            preferred_element_type=jnp.float32,
        )
        peaks.append(peak)
        sums.append(weight_sum)
        numers.append(numer)
    return (jnp.stack(peaks, axis=1), jnp.stack(sums, axis=1), jnp.stack(numers, axis=1))


def split3(x):
    high = x.astype(jnp.bfloat16)
    rest = x - high.astype(jnp.float32)
    middle = rest.astype(jnp.bfloat16)
    low = (rest - middle.astype(jnp.float32)).astype(jnp.bfloat16)
    return high, middle, low


def shared_kernel(head_ref, query_ref, pair_ref, out_ref, key_ref, value_ref):
    pieces = pair_ref.shape[0]
    samples = query_ref.shape[0]
    row = lax.broadcasted_iota(jnp.int32, (256, 256), 0)
    column = lax.broadcasted_iota(jnp.int32, (256, 256), 1)
    wanted = jnp.where(row < 128, 2 * row, 2 * (row - 128) + 1)
    pick = jnp.where(column == wanted, 1.0, 0.0).astype(jnp.bfloat16)
    for step in range(pieces // 16):
        both = pair_ref[step * 16 : (step + 1) * 16].reshape(256, HEAD_FEATURES)
        apart = jnp.dot(pick, both, preferred_element_type=jnp.float32).astype(jnp.bfloat16)
        key_ref[step * 128 : (step + 1) * 128, :] = apart[:128]
        value_ref[step * 128 : (step + 1) * 128, :] = apart[128:]
    factor = SCALE * math.log2(math.e)
    lane = lax.broadcasted_iota(jnp.int32, (samples, 128), 1)

    def group(g, stats):
        start = pl.multiple_of(g * HEAD_FEATURES, HEAD_FEATURES)
        query = query_ref[:, pl.ds(start, HEAD_FEATURES)]
        scores = lax.dot_general(
            query, key_ref[...], (((1,), (1,)), ((), ())), preferred_element_type=jnp.float32
        )
        top = jnp.max(scores, axis=-1, keepdims=True)
        weights = jnp.exp2((scores - top) * factor)
        total = jnp.sum(weights, axis=-1, keepdims=True)
        numer = jnp.dot(
            weights.astype(jnp.bfloat16), value_ref[...], preferred_element_type=jnp.float32
        )
        out_ref[:, pl.ds(start, HEAD_FEATURES)] = numer.astype(jnp.bfloat16)
        for place, term in enumerate(split3(top * SCALE) + split3(total)):
            stats = jnp.where(
                lane == place * GROUP + g, term.astype(jnp.float32), stats
            )
        return stats

    stats = lax.fori_loop(0, GROUP, group, jnp.zeros((samples, 128), jnp.float32))
    out_ref[:, WIDTH:] = stats.astype(jnp.bfloat16)


def partial_shared(head, query_rows, pairs):
    samples = query_rows.shape[0]
    tokens = pairs.shape[0] * 8
    return pl.pallas_call(
        shared_kernel,
        out_shape=jax.ShapeDtypeStruct((samples, WIDTH + 128), jnp.bfloat16),
        grid_spec=pltpu.PrefetchScalarGridSpec(
            num_scalar_prefetch=1,
            grid=(1,),
            in_specs=[
                pl.BlockSpec((samples, WIDTH), lambda i, head: (0, head[0])),
                pl.BlockSpec(pairs.shape, lambda i, head: (0, 0, 0)),
            ],
            out_specs=pl.BlockSpec((samples, WIDTH + 128), lambda i, head: (0, 0)),
            scratch_shapes=[
                pltpu.VMEM((tokens, HEAD_FEATURES), jnp.bfloat16),
                pltpu.VMEM((tokens, HEAD_FEATURES), jnp.bfloat16),
            ],
        ),
        compiler_params=pltpu.CompilerParams(vmem_limit_bytes=32 * 1024 * 1024),
        cost_estimate=pl.CostEstimate(
            flops=4 * samples * GROUP * tokens * HEAD_FEATURES,
            bytes_accessed=4 * 1024 * 1024,
            transcendentals=samples * GROUP * tokens,
        ),
    )(head, query_rows, pairs)


def body(n_inst, n_samp, prompt_key_values, match, page_list, queries, sample_key_values, gen_len):
    local_total = queries.shape[1]
    pages_dev = page_list.shape[2]
    half = PAGE_TOKENS // 2
    member = lax.axis_index("samp")
    local_queries = queries[0]

    all_queries = lax.all_gather(local_queries, "samp", axis=0, tiled=True)

    pages = lax.all_to_all(prompt_key_values, "inst", split_axis=1, concat_axis=0, tiled=True)

    sample_keys = sample_key_values[0, :, :, 0, :]
    sample_values = sample_key_values[0, :, :, 1, :]
    live_mask = jnp.arange(sample_keys.shape[1], dtype=jnp.int32)[None, :] < gen_len[0][:, None]
    own_peak, own_sum, own_numer = partial_own(local_queries, sample_keys, sample_values, live_mask)

    chosen = jnp.take(pages, match, axis=0)
    chosen = chosen.reshape(n_inst, PAGE_TOKENS, 2, KEY_VALUE_HEADS, HEAD_FEATURES)
    chosen = chosen.transpose(0, 3, 1, 2, 4).reshape(n_inst * n_samp, half * 2, HEAD_FEATURES)
    pairs = lax.all_to_all(chosen, ("inst", "samp"), split_axis=0, concat_axis=0, tiled=True)

    listed = page_list[0].reshape(-1)
    place = (listed % pages_dev) * n_samp + listed // pages_dev
    sent = jnp.take(pairs, place, axis=0)
    came = lax.all_to_all(
        sent.reshape(n_samp, pages_dev, half * 2, HEAD_FEATURES),
        "samp", split_axis=0, concat_axis=0, tiled=True,
    )
    came = came.reshape(KEY_VALUE_HEADS, 2, pages_dev, half, 2, HEAD_FEATURES)
    page_pool = came.transpose(2, 1, 3, 4, 0, 5).reshape(
        1, pages_dev, PAGE_TOKENS, 2, KEY_VALUE_HEADS * HEAD_FEATURES
    )

    part = partial_shared((member // 2).astype(jnp.int32)[None], all_queries, pairs)
    back = lax.all_to_all(
        part.reshape(n_samp, local_total, WIDTH + 128),
        "samp", split_axis=0, concat_axis=0, tiled=True,
    )
    back = back.reshape(KEY_VALUE_HEADS, 2, local_total, WIDTH + 128)
    numer = back[..., :WIDTH].reshape(KEY_VALUE_HEADS, 2, local_total, GROUP, HEAD_FEATURES)
    numer = numer.astype(jnp.float32)
    stats = back[..., WIDTH : WIDTH + 6 * GROUP].astype(jnp.float32)
    stats = stats.reshape(KEY_VALUE_HEADS, 2, local_total, 2, 3, GROUP)
    stats = (stats[..., 0, :] + stats[..., 1, :]) + stats[..., 2, :]
    peaks = stats[..., 0, :]
    sums = stats[..., 1, :]

    own_peak = own_peak.transpose(1, 0, 2)
    own_sum = own_sum.transpose(1, 0, 2)
    own_numer = own_numer.transpose(1, 0, 2, 3)
    peak = jnp.maximum(jnp.max(peaks, axis=1), own_peak)
    scales = jnp.exp(peaks - peak[:, None])
    own_scale = jnp.exp(own_peak - peak)
    weight_sum = jnp.sum(sums * scales, axis=1) + own_sum * own_scale
    total = jnp.sum(numer * scales[..., None], axis=1) + own_numer * own_scale[..., None]
    attended = (total / weight_sum[..., None]).astype(jnp.bfloat16)
    attended = attended.transpose(1, 0, 2, 3).reshape(1, local_total, QUERY_HEADS * HEAD_FEATURES)
    return (attended, page_pool)


def solution(mesh):
    in_specs = (
        P("inst", "samp", None, None),
        P(),
        P("inst", None, None),
        P("inst", "samp", None),
        P("inst", "samp", None, None, None),
        P("inst", "samp"),
    )
    out_specs = (P("inst", "samp", None), P("inst", "samp", None, None, None))
    step = functools.partial(body, mesh.shape["inst"], mesh.shape["samp"])
    return jax.shard_map(step, mesh=mesh, in_specs=in_specs, out_specs=out_specs, check_vma=False)
```

time: 295 us -> 141 us (0.48)
  waiting for transfers between devices: 115 us -> 35.2 us
  local copies, waits for them, and re-layouts: 75.7 us -> 28.9 us
  blocking collectives: 30.2 us -> 0 us
  matrix products: 39.7 us -> 11 us
  starting transfers between devices: 10.2 us -> 30.5 us
  Pallas kernels: 0 us -> 10 us
    all_gather x1, waiting for transfers between devices: 89.4 us -> 0.01 us  [body(): all_queries = lax.all_gather(local_queries, 'samp', axis=0, tiled=True)]
    slice x2, local copies, waits for them, and re-layouts: 41.5 us -> 10 us  [the longest x1 9.95 us: body(): sample_values = sample_key_values[0, :, :, 1, :]]
    all_to_all x1 -> x0, blocking collectives: 30.2 us -> none  [body(): lax.all_to_all(chosen, 'inst', split_axis=0, concat_axis=1, tiled=True)]
    all_to_all x0 -> x3, waiting for transfers between devices: none -> 27.9 us  [the longest x1 19.4 us: body(): lax.all_to_all(chosen, ('inst', 'samp'), split_axis=0, concat_axis=0, til...]
    dot_general x16 -> x0, matrix products: 27.7 us -> none  [the longest x8 14.5 us: partial_shared(): lax.dot_general(block, key_block, (((1,), (1,)), ((), ())), preferred_ele...]
    all_to_all x0 -> x3, starting transfers between devices: none -> 20.4 us  [the longest x1 11.1 us: body(): lax.all_to_all(chosen, ('inst', 'samp'), split_axis=0, concat_axis=0, til...]
    all_to_all x1, waiting for transfers between devices: 25.6 us -> 6.57 us  [body(): lax.all_to_all(prompt_key_values, 'inst', split_axis=1, concat_axis=0, ti...]
    pallas_call x0 -> x1, Pallas kernels: none -> 10 us  [partial_shared(): pl.pallas_call(shared_kernel, out_shape=jax.ShapeDtypeStruct((samples, WI...]
  transfers between devices with their start and end apart: 2 -> 5, of which waited for: 2 -> 4; matrix products, arithmetic and copies ran while one was open for 9% -> 32% of each run, Pallas kernels for 0% -> 7%
where the time goes in v1:
time: 141 us; the launch traced here: 140 us
  waiting for transfers between devices  35.2 us (25%)
  starting transfers between devices  30.5 us (22%)
  local copies, waits for them, and re-layouts  28.9 us (20%)
  between operations  14.5 us (10%)
  matrix products  11 us (8%)
  other arithmetic  10 us (7%)
  Pallas kernels  10 us (7%)
    all_to_all x1, waiting for transfers between devices, body(): lax.all_to_all(chosen, ('inst', 'samp'), split_axis=0, concat_axis=0, til...  19.4 us
    all_to_all x1, starting transfers between devices, body(): lax.all_to_all(chosen, ('inst', 'samp'), split_axis=0, concat_axis=0, til...  11.1 us
    all_to_all x1, starting transfers between devices, body(): lax.all_to_all(prompt_key_values, 'inst', split_axis=1, concat_axis=0, ti...  10.1 us
    pallas_call x1, Pallas kernels, partial_shared(): pl.pallas_call(shared_kernel, out_shape=jax.ShapeDtypeStruct((samples, WI...  10 us
    slice x1, local copies, waits for them, and re-layouts, body(): sample_values = sample_key_values[0, :, :, 1, :]  9.95 us
    unnamed x79, local copies, waits for them, and re-layouts  8.47 us
    dot_general x8, matrix products, partial_own(): jnp.einsum('sgn,snd->sgd', weights.astype(jnp.bfloat16), value_block, pre...  6.9 us
    all_to_all x1, waiting for transfers between devices, body(): lax.all_to_all(prompt_key_values, 'inst', split_axis=1, concat_axis=0, ti...  6.57 us
  transfers between devices with their start and end apart: 5, of which 4 were waited for; matrix products, arithmetic and copies ran while one was open for 32% of the time, Pallas kernels for 7%

profile of v1, /device:TPU:1, one launch (start us, length us, event | category | flops | bytes accessed | tf_op | source)
XLA Modules:
  0.0 140.2 jit_solution(10949508479533256174)
XLA Ops:
  7.2 10.1 %all-to-all-start = ((bf16[1,256,2,1024]{3,2,0,1:T(2,128)(2,1)}), bf16[1,256,2,1024]{3,2,0,1:T(2,128)(2,1)S(1)}, u32[]{:S(2)}, u32[]{:S(2)}) async-start(bf16[1,256,2,1024]{3,2,0,1:T(2,128)(2,1)} %bitcast.184), calls=%async_computation | async-start | bytes 2097152 | tf_op jit(solution)/shard_map/all_to_all | solution.py:133
  17.4 0.7 all-gather.3.cloned.1.call-update
  18.1 9.9 %fusion.86 = (bf16[1,8,128,1,1024]{4,3,2,1,0:T(2,128)(2,1)}, bf16[1,8,128,1,1024]{4,3,2,1,0:T(2,128)(2,1)S(1)}) fusion(bf16[1,8,128,2,1024]{4,3,2,1,0:T(2,128)(2,1)} %param.10), kind=kLoop, calls=%fused_computation.162 | loop fusion | bytes 8388608 | tf_op jit(solution)/shard_map/slice | solution.py:136
  28.0 0.8 copy.125
  28.9 0.6 slice_bitcast_fusion
  29.9 0.3 fusion.88
  30.5 0.3 fusion.90
  31.2 0.3 fusion.92
  31.5 0.3 fusion.93
  31.9 0.3 fusion.94
  32.3 0.6 compare_select_fusion.1
  33.2 0.8 fusion.41
  34.0 0.8 fusion.43
  34.8 0.8 fusion.45
  35.5 0.8 fusion.47
  36.4 6.6 %all-to-all-done = bf16[1,256,2,1024]{3,2,0,1:T(2,128)(2,1)S(1)} async-done(((bf16[1,256,2,1024]{3,2,0,1:T(2,128)(2,1)}), bf16[1,256,2,1024]{3,2,0,1:T(2,128)(2,1)S(1)}, u32[]{:S(2)}, u32[]{:S(2)}) %all-to-all-start) | async-done | bytes 1048608 | tf_op jit(solution)/shard_map/all_to_all | solution.py:133
  43.3 0.6 gather_fusion
  44.4 2.1 %copy.66 = bf16[16,8,16,2,128]{4,3,2,1,0:T(2,128)(2,1)} copy(bf16[16,8,16,2,128]{4,1,2,3,0:T(8,128)(2,1)S(1)} %select_bitcast_fusion) | data formatting | bytes 2097152 | tf_op jit(solution)/shard_map/transpose | solution.py:142
  46.5 11.1 %all-to-all-start.1 = ((bf16[256,16,128]{2,1,0:T(8,128)(2,1)}), bf16[256,16,128]{2,1,0:T(8,128)(2,1)S(1)}, u32[]{:S(2)}, u32[]{:S(2)}) async-start(bf16[256,16,128]{2,1,0:T(8,128)(2,1)} %bitcast.5), calls=%async_computation.1 | async-start | bytes 2097152 | tf_op jit(solution)/shard_map/all_to_all | solution.py:143
  57.6 0.6 pad_clamp_fusion
  58.3 3.4 %copy.124 = bf16[1,8,128,1,1024]{4,2,1,3,0:T(8,128)(2,1)S(1)} copy(bf16[1,8,128,1,1024]{4,3,2,1,0:T(2,128)(2,1)} %get-tuple-element.6) | data formatting | bytes 4194304
  61.7 0.6 constant_dynamic-update-slice_fusion.12
  62.3 0.6 constant_dynamic-update-slice_fusion.11
  62.9 0.6 constant_dynamic-update-slice_fusion.10
  63.5 0.6 compare_and_fusion
  64.1 1.9 %fusion.95 = (f32[8,12]{1,0:T(8,128)}, f32[8,12,128]{2,1,0:T(8,128)S(1)}) fusion(bf16[8,128,1024]{2,1,0:T(8,128)(2,1)} %bitcast.175, bf16[8,12,128]{2,0,1:T(8,128)(2,1)S(1)} %copy-done.9, pred[8,128]{1,0:T(8,128)(4,1)S(1)} %iota_compare_fusion), kind=kOutput, calls=%fused_computation.171 | convolution fusion | flops 3182496 | bytes 337280 | tf_op jit(solution)/shard_map/sgd,snd->sgn/dot_general | solution.py:31
  66.0 0.9 fusion.7
  66.9 0.9 fusion.6
  67.7 0.9 fusion.5
  68.6 0.9 fusion.4
  69.5 19.4 %all-to-all-done.1.pair_ref = bf16[256,16,128]{2,1,0:T(8,128)(2,1)S(1)} async-done(((bf16[256,16,128]{2,1,0:T(8,128)(2,1)}), bf16[256,16,128]{2,1,0:T(8,128)(2,1)S(1)}, u32[]{:S(2)}, u32[]{:S(2)}) %all-to-all-start.1) | async-done | bytes 1048608 | tf_op jit(solution)/shard_map/all_to_all | solution.py:143
  88.9 1.9 %gather_fusion.1 = bf16[256,16,128]{2,1,0:T(8,128)(2,1)} fusion(bf16[256,16,128]{2,1,0:T(8,128)(2,1)S(1)} %all-to-all-done.1.pair_ref, s32[1024]{0:T(1024)} %pad_clamp_fusion), kind=kCustom, calls=%fused_computation.1 | custom fusion | bytes 2098176 | tf_op jit(solution)/shard_map/jit(_take)/gather | solution.py:147
  90.8 2.3 %broadcast_select_fusion = bf16[16,16,16,128]{3,2,1,0:T(8,128)(2,1)} fusion(bf16[16,16,16,128]{3,2,1,0:T(8,128)(2,1)} %bitcast.179, pred[16,16]{1,0:T(8,128)(4,1)S(1)} %copy-done.27), kind=kLoop, calls=%fused_computation.38 | loop fusion | flops 524288 | bytes 2097408 | tf_op jit(solution)/shard_map/jit(_take)/select_n | solution.py:147
  93.1 4.7 %all-to-all-start.3 = ((bf16[16,16,16,128]{3,2,1,0:T(8,128)(2,1)}), bf16[16,16,16,128]{3,2,1,0:T(8,128)(2,1)}, u32[]{:S(2)}, u32[]{:S(2)}) async-start(bf16[16,16,16,128]{3,2,1,0:T(8,128)(2,1)} %broadcast_select_fusion), calls=%async_computation.3 | async-start | bytes 2097152 | tf_op jit(solution)/shard_map/all_to_all | solution.py:148
  98.0 0.9 fusion.3
  98.9 0.9 fusion.2
  99.8 0.9 fusion.1
  100.6 1.9 %copy-done = bf16[1,128,12288]{2,1,0:T(8,128)(2,1)S(1)} copy-done((bf16[1,128,12288]{2,1,0:T(8,128)(2,1)S(1)}, bf16[1,128,12288]{2,1,0:T(8,128)(2,1)}, u32[]{:S(2)}) %copy-start) | copy-done | bytes 3145752
  102.5 10.0 %shard_map.77 = bf16[128,1664]{1,0:T(8,128)(2,1)} custom-call(s32[1]{0:T(128)} %bitcast.head_ref, bf16[128,12288]{1,0:T(8,128)(2,1)S(1)} %bitcast.159, bf16[256,16,128]{2,1,0:T(8,128)(2,1)S(1)} %all-to-all-done.1.pair_ref), custom_call_target="tpu_custom_call" | custom-call | flops 1610612736 | bytes 4194304 | tf_op jit(solution)/shard_map/pallas_call | solution.py:99
  112.6 2.8 %all-to-all-done.3 = bf16[16,16,16,128]{3,2,1,0:T(8,128)(2,1)} async-done(((bf16[16,16,16,128]{3,2,1,0:T(8,128)(2,1)}), bf16[16,16,16,128]{3,2,1,0:T(8,128)(2,1)}, u32[]{:S(2)}, u32[]{:S(2)}) %all-to-all-start.3) | async-done | bytes 1048608 | tf_op jit(solution)/shard_map/all_to_all | solution.py:148
  115.4 4.5 %all-to-all-start.2 = ((bf16[16,8,1664]{2,1,0:T(8,128)(2,1)}), bf16[16,8,1664]{2,1,0:T(8,128)(2,1)S(1)}, u32[]{:S(2)}, u32[]{:S(2)}) async-start(bf16[16,8,1664]{2,1,0:T(8,128)(2,1)} %bitcast.6), calls=%async_computation.2 | async-start | bytes 851968 | tf_op jit(solution)/shard_map/all_to_all | solution.py:158
  119.9 0.9 fusion
  120.7 2.4 %copy.126 = bf16[8,2,16,8,2,128]{5,0,4,3,1,2:T(8,128)(2,1)S(1)} copy(bf16[8,2,16,8,2,128]{5,4,3,2,1,0:T(2,128)(2,1)} %bitcast.56) | data formatting | bytes 2097152 | tf_op jit(solution)/shard_map/reshape | solution.py:152
  123.2 1.1 reshape.239
  124.3 5.7 %all-to-all-done.2 = bf16[16,8,1664]{2,1,0:T(8,128)(2,1)S(1)} async-done(((bf16[16,8,1664]{2,1,0:T(8,128)(2,1)}), bf16[16,8,1664]{2,1,0:T(8,128)(2,1)S(1)}, u32[]{:S(2)}, u32[]{:S(2)}) %all-to-all-start.2) | async-done | bytes 426016 | tf_op jit(solution)/shard_map/all_to_all | solution.py:158
  130.0 0.3 reshape.241
  131.2 1.4 fusion.18
  132.6 0.8 reshape.237
  (99 shorter events, 3.4 us)
Async XLA Ops:
  7.2 35.8 %all-to-all-start = ((bf16[1,256,2,1024]{3,2,0,1:T(2,128)(2,1)}), bf16[1,256,2,1024]{3,2,0,1:T(2,128)(2,1)S(1)}, u32[]{:S(2)}, u32[]{:S(2)}) async-start(bf16[1,256,2,1024]{3,2,0,1:T(2,128)(2,1)} %bitcast.184), calls=%async_computation | async-start | bytes 2097152 | tf_op jit(solution)/shard_map/all_to_all | solution.py:133
  17.3 83.3 %all-gather.3.cloned.1.call-start = ((), (), s32[]{:S(2)}) async-start(), calls=%async_computation.4 | async-start | bytes 3342336 | tf_op jit(solution)/shard_map/all_gather | solution.py:131
  28.0 0.9 copy-start.2
  28.0 1.5 %copy-start.29 = (s32[1,8]{1,0:T(1,128)S(1)}, s32[1,8]{1,0:T(1,128)}, u32[]{:S(2)}) copy-start(s32[1,8]{1,0:T(1,128)} %param.11) | copy-start | bytes 100
  28.8 3.0 %copy-start.1 = (bf16[1,8,128,1,1024]{4,2,1,3,0:T(8,128)(2,1)}, bf16[1,8,128,1,1024]{4,2,1,3,0:T(8,128)(2,1)S(1)}, u32[]{:S(2)}) copy-start(bf16[1,8,128,1,1024]{4,2,1,3,0:T(8,128)(2,1)S(1)} %copy.125) | copy-start | bytes 6291460
  28.8 3.4 %copy-start.30 = (s32[16]{0:T(128)S(1)}, s32[16]{0:T(128)}, u32[]{:S(2)}) copy-start(s32[16]{0:T(128)} %param.7) | copy-start | bytes 196
  28.8 3.4 %copy-start.21 = (s32[1,16,16]{2,1,0:T(8,128)S(1)}, s32[1,16,16]{2,1,0:T(8,128)}, u32[]{:S(2)}) copy-start(s32[1,16,16]{2,1,0:T(8,128)} %param.8) | copy-start | bytes 3076
  29.9 13.1 %copy-start.10 = (f32[8,12]{1,0:T(8,128)}, f32[8,12]{1,0:T(8,128)S(1)}, u32[]{:S(2)}) copy-start(f32[8,12]{1,0:T(8,128)S(1)} %get-tuple-element.20) | copy-start | bytes 1156
  30.3 0.6 copy-start.12
  30.9 12.1 %copy-start.14 = (f32[8,12]{1,0:T(8,128)}, f32[8,12]{1,0:T(8,128)S(1)}, u32[]{:S(2)}) copy-start(f32[8,12]{1,0:T(8,128)S(1)} %get-tuple-element.22) | copy-start | bytes 1156
  30.9 13.1 %copy-start.3 = (f32[8,12,128]{2,1,0:T(8,128)}, f32[8,12,128]{2,1,0:T(8,128)S(1)}, u32[]{:S(2)}) copy-start(f32[8,12,128]{2,1,0:T(8,128)S(1)} %get-tuple-element.23) | copy-start | bytes 147460
  31.2 11.8 %copy-start.5 = (f32[8,12,128]{2,1,0:T(8,128)}, f32[8,12,128]{2,1,0:T(8,128)S(1)}, u32[]{:S(2)}) copy-start(f32[8,12,128]{2,1,0:T(8,128)S(1)} %get-tuple-element.25) | copy-start | bytes 147460
  31.2 11.8 %copy-start.16 = (f32[8,12]{1,0:T(8,128)}, f32[8,12]{1,0:T(8,128)S(1)}, u32[]{:S(2)}) copy-start(f32[8,12]{1,0:T(8,128)S(1)} %get-tuple-element.24) | copy-start | bytes 1156
  36.4 6.6 %copy-start.7 = (f32[8,8,12]{2,0,1:T(8,128)}, f32[8,8,12]{2,0,1:T(8,128)S(1)}, u32[]{:S(2)}) copy-start(f32[8,8,12]{2,0,1:T(8,128)S(1)} %constant_dynamic-update-slice_fusion.1) | copy-start | bytes 9220
  36.4 6.6 %copy-start.19 = (f32[8,8,12]{2,0,1:T(8,128)}, f32[8,8,12]{2,0,1:T(8,128)S(1)}, u32[]{:S(2)}) copy-start(f32[8,8,12]{2,0,1:T(8,128)S(1)} %constant_dynamic-update-slice_fusion.13) | copy-start | bytes 9220
  44.4 13.2 %copy-start.28 = (s32[256,1]{0,1:T(1,128)S(1)}, s32[256,1]{0,1:T(1,128)}, u32[]{:S(2)}) copy-start(s32[256,1]{0,1:T(1,128)} %compare_select_fusion.1) | copy-start | bytes 3076
  46.5 42.4 %all-to-all-start.1 = ((bf16[256,16,128]{2,1,0:T(8,128)(2,1)}), bf16[256,16,128]{2,1,0:T(8,128)(2,1)S(1)}, u32[]{:S(2)}, u32[]{:S(2)}) async-start(bf16[256,16,128]{2,1,0:T(8,128)(2,1)} %bitcast.5), calls=%async_computation.1 | async-start | bytes 2097152 | tf_op jit(solution)/shard_map/all_to_all | solution.py:143
  58.2 3.5 %copy-start.26 = (f32[8,12]{1,0:T(8,128)S(1)}, f32[8,12]{1,0:T(8,128)}, u32[]{:S(2)}) copy-start(f32[8,12]{1,0:T(8,128)} %fusion.41) | copy-start | bytes 1156
  58.2 4.1 %copy-start.25 = (f32[8,12]{1,0:T(8,128)S(1)}, f32[8,12]{1,0:T(8,128)}, u32[]{:S(2)}) copy-start(f32[8,12]{1,0:T(8,128)} %fusion.43) | copy-start | bytes 1156
  58.2 4.7 %copy-start.24 = (f32[8,12]{1,0:T(8,128)S(1)}, f32[8,12]{1,0:T(8,128)}, u32[]{:S(2)}) copy-start(f32[8,12]{1,0:T(8,128)} %fusion.45) | copy-start | bytes 1156
  58.2 5.3 %copy-start.22 = (s32[1,16,16]{2,1,0:T(8,128)S(1)}, s32[1,16,16]{2,1,0:T(8,128)}, u32[]{:S(2)}) copy-start(s32[1,16,16]{2,1,0:T(8,128)} %param.8) | copy-start | bytes 3076
  58.2 5.9 %copy-start.9 = (bf16[8,12,128]{2,0,1:T(8,128)(2,1)S(1)}, bf16[8,12,128]{2,0,1:T(8,128)(2,1)}, u32[]{:S(2)}) copy-start(bf16[8,12,128]{2,0,1:T(8,128)(2,1)} %get-tuple-element.8) | copy-start | bytes 73732
  58.2 7.8 %copy-start.13 = (f32[8,12]{1,0:T(8,128)S(1)}, f32[8,12]{1,0:T(8,128)}, u32[]{:S(2)}) copy-start(f32[8,12]{1,0:T(8,128)} %copy-done.12) | copy-start | bytes 1156
  58.3 8.6 %copy-start.11 = (f32[8,12]{1,0:T(8,128)S(1)}, f32[8,12]{1,0:T(8,128)}, u32[]{:S(2)}) copy-start(f32[8,12]{1,0:T(8,128)} %copy-done.10) | copy-start | bytes 1156
  58.3 9.5 %copy-start.4 = (f32[8,12,128]{2,1,0:T(8,128)S(1)}, f32[8,12,128]{2,1,0:T(8,128)}, u32[]{:S(2)}) copy-start(f32[8,12,128]{2,1,0:T(8,128)} %copy-done.3) | copy-start | bytes 147460
  58.3 9.5 %copy-start.15 = (f32[8,12]{1,0:T(8,128)S(1)}, f32[8,12]{1,0:T(8,128)}, u32[]{:S(2)}) copy-start(f32[8,12]{1,0:T(8,128)} %copy-done.14) | copy-start | bytes 1156
  58.3 10.3 %copy-start.6 = (f32[8,12,128]{2,1,0:T(8,128)S(1)}, f32[8,12,128]{2,1,0:T(8,128)}, u32[]{:S(2)}) copy-start(f32[8,12,128]{2,1,0:T(8,128)} %copy-done.5) | copy-start | bytes 147460
  58.3 10.3 %copy-start.17 = (f32[8,12]{1,0:T(8,128)S(1)}, f32[8,12]{1,0:T(8,128)}, u32[]{:S(2)}) copy-start(f32[8,12]{1,0:T(8,128)} %copy-done.16) | copy-start | bytes 1156
  66.0 24.8 %copy-start.27 = (pred[16,16]{1,0:T(8,128)(4,1)S(1)}, pred[16,16]{1,0:T(8,128)(4,1)}, u32[]{:S(2)}) copy-start(pred[16,16]{1,0:T(8,128)(4,1)} %compare_and_fusion) | copy-start | bytes 772
  90.8 7.0 %copy-start.20 = (f32[8,8,12]{2,0,1:T(8,128)S(1)}, f32[8,8,12]{2,0,1:T(8,128)}, u32[]{:S(2)}) copy-start(f32[8,8,12]{2,0,1:T(8,128)} %constant_dynamic-update-slice_fusion.10) | copy-start | bytes 9220
  90.8 7.0 %copy-start.23 = (f32[8,12]{1,0:T(8,128)S(1)}, f32[8,12]{1,0:T(8,128)}, u32[]{:S(2)}) copy-start(f32[8,12]{1,0:T(8,128)} %fusion.47) | copy-start | bytes 1156
  90.8 7.1 %copy-start.18 = (f32[8,12]{1,0:T(8,128)S(1)}, f32[8,12]{1,0:T(8,128)}, u32[]{:S(2)}) copy-start(f32[8,12]{1,0:T(8,128)} %get-tuple-element.32) | copy-start | bytes 1156
  93.1 22.3 %all-to-all-start.3 = ((bf16[16,16,16,128]{3,2,1,0:T(8,128)(2,1)}), bf16[16,16,16,128]{3,2,1,0:T(8,128)(2,1)}, u32[]{:S(2)}, u32[]{:S(2)}) async-start(bf16[16,16,16,128]{3,2,1,0:T(8,128)(2,1)} %broadcast_select_fusion), calls=%async_computation.3 | async-start | bytes 2097152 | tf_op jit(solution)/shard_map/all_to_all | solution.py:148
  100.6 1.9 %copy-start = (bf16[1,128,12288]{2,1,0:T(8,128)(2,1)S(1)}, bf16[1,128,12288]{2,1,0:T(8,128)(2,1)}, u32[]{:S(2)}) copy-start(bf16[1,128,12288]{2,1,0:T(8,128)(2,1)} %all-gather.3.cloned.1.call-done) | copy-start | bytes 9437188
  102.5 17.3 %copy-start.8 = (f32[8,8,12]{2,0,1:T(8,128)S(1)}, f32[8,8,12]{2,0,1:T(8,128)}, u32[]{:S(2)}) copy-start(f32[8,8,12]{2,0,1:T(8,128)} %copy-done.7) | copy-start | bytes 9220
  115.4 14.6 %all-to-all-start.2 = ((bf16[16,8,1664]{2,1,0:T(8,128)(2,1)}), bf16[16,8,1664]{2,1,0:T(8,128)(2,1)S(1)}, u32[]{:S(2)}, u32[]{:S(2)}) async-start(bf16[16,8,1664]{2,1,0:T(8,128)(2,1)} %bitcast.6), calls=%async_computation.2 | async-start | bytes 851968 | tf_op jit(solution)/shard_map/all_to_all | solution.py:158
Sparse Core Ops, SparseCore 0:
  20.9 67.2 all-gather.2

commit v2 on v1

v2 whole, which is shorter than its diff:
```python
import functools
import math

import jax
import jax.numpy as jnp
from jax import lax
from jax.experimental import pallas as pl
from jax.experimental.pallas import tpu as pltpu
from jax.sharding import PartitionSpec as P

QUERY_HEADS = 96
KEY_VALUE_HEADS = 8
HEAD_FEATURES = 128
PAGE_TOKENS = 16
GROUP = QUERY_HEADS // KEY_VALUE_HEADS
WIDTH = GROUP * HEAD_FEATURES
SCALE = HEAD_FEATURES ** (-0.5)


def partial_own(query_rows, sample_keys, sample_values, live_mask):
    count = query_rows.shape[0]
    peaks = []
    sums = []
    numers = []
    for head in range(KEY_VALUE_HEADS):
        block = query_rows[:, head * WIDTH : (head + 1) * WIDTH].reshape(
            count, GROUP, HEAD_FEATURES
        )
        key_block = sample_keys[:, :, head * HEAD_FEATURES : (head + 1) * HEAD_FEATURES]
        value_block = sample_values[:, :, head * HEAD_FEATURES : (head + 1) * HEAD_FEATURES]
        scores = jnp.einsum(
            "sgd,snd->sgn", block, key_block, preferred_element_type=jnp.float32
        ) * SCALE
        scores = jnp.where(live_mask[:, None, :], scores, -jnp.inf)
        peak = jnp.max(scores, axis=-1)
        weights = jnp.exp(scores - peak[..., None])
        weight_sum = jnp.sum(weights, axis=-1)
        numer = jnp.einsum(
            "sgn,snd->sgd",
            weights.astype(jnp.bfloat16),
            value_block,
            preferred_element_type=jnp.float32,
        )
        peaks.append(peak)
        sums.append(weight_sum)
        numers.append(numer)
    return (jnp.stack(peaks, axis=1), jnp.stack(sums, axis=1), jnp.stack(numers, axis=1))


def split3(x):
    high = x.astype(jnp.bfloat16)
    rest = x - high.astype(jnp.float32)
    middle = rest.astype(jnp.bfloat16)
    low = (rest - middle.astype(jnp.float32)).astype(jnp.bfloat16)
    return high, middle, low


def shared_kernel(place_ref, query_ref, pair_ref, out_ref, key_ref, value_ref):
    pieces = pair_ref.shape[0]
    samples = query_ref.shape[0]
    owners, rows = out_ref.shape[0], pair_ref.shape[1]
    slots = pieces // owners
    local = samples // owners

    def move(n, carry):
        row = pl.multiple_of(lax.rem(n, slots) * rows, rows)
        out_ref[lax.div(n, slots), pl.ds(row, rows), :] = pair_ref[place_ref[n]]
        return carry

    lax.fori_loop(0, pieces, move, 0, unroll=8)

    row = lax.broadcasted_iota(jnp.int32, (256, 256), 0)
    column = lax.broadcasted_iota(jnp.int32, (256, 256), 1)
    wanted = jnp.where(row < 128, 2 * row, 2 * (row - 128) + 1)
    pick = jnp.where(column == wanted, 1.0, 0.0).astype(jnp.bfloat16)
    for step in range(pieces // 16):
        both = pair_ref[step * 16 : (step + 1) * 16].reshape(256, HEAD_FEATURES)
        apart = jnp.dot(pick, both, preferred_element_type=jnp.float32).astype(jnp.bfloat16)
        key_ref[step * 128 : (step + 1) * 128, :] = apart[:128]
        value_ref[step * 128 : (step + 1) * 128, :] = apart[128:]

    factor = SCALE * math.log2(math.e)
    lane = lax.broadcasted_iota(jnp.int32, (samples, 128), 1)
    peaks = jnp.zeros((samples, 128), jnp.float32)
    sums = jnp.zeros((samples, 128), jnp.float32)

    def side_by_side(low, high):
        low = low.reshape(owners, local, HEAD_FEATURES)
        high = high.reshape(owners, local, HEAD_FEATURES)
        return jnp.concatenate([low, high], axis=1).astype(jnp.bfloat16)

    for g in range(0, GROUP, 2):
        query = jnp.concatenate(
            [
                query_ref[:, g * HEAD_FEATURES : (g + 1) * HEAD_FEATURES],
                query_ref[:, (g + 1) * HEAD_FEATURES : (g + 2) * HEAD_FEATURES],
            ],
            axis=0,
        )
        scores = lax.dot_general(
            query, key_ref[...], (((1,), (1,)), ((), ())), preferred_element_type=jnp.float32
        )
        top = jnp.max(scores, axis=-1, keepdims=True)
        weights = jnp.exp2((scores - top) * factor)
        total = jnp.sum(weights, axis=-1, keepdims=True)
        numer = jnp.dot(
            weights.astype(jnp.bfloat16), value_ref[...], preferred_element_type=jnp.float32
        )
        first = slots * rows + g * local
        out_ref[:, first : first + 2 * local, :] = side_by_side(numer[:samples], numer[samples:])
        top = top * SCALE
        peaks = jnp.where(lane == g, top[:samples], peaks)
        peaks = jnp.where(lane == g + 1, top[samples:], peaks)
        sums = jnp.where(lane == g, total[:samples], sums)
        sums = jnp.where(lane == g + 1, total[samples:], sums)

    stats = jnp.zeros((samples, 128), jnp.float32)
    for place, term in enumerate(split3(peaks) + split3(sums)):
        term = term.astype(jnp.float32)
        stats = stats + (pltpu.roll(term, place * GROUP, 1) if place else term)
    first = slots * rows + GROUP * local
    out_ref[:, first:, :] = side_by_side(stats, jnp.zeros_like(stats))


def partial_shared(place, query_rows, pairs, owners):
    samples = query_rows.shape[0]
    pieces, rows, features = pairs.shape
    tokens = pieces * rows // 2
    sent = pieces // owners * rows + (GROUP + 2) * (samples // owners)
    return pl.pallas_call(
        shared_kernel,
        out_shape=jax.ShapeDtypeStruct((owners, sent, features), jnp.bfloat16),
        in_specs=[
            pl.BlockSpec(memory_space=pltpu.SMEM),
            pl.BlockSpec(memory_space=pltpu.VMEM),
            pl.BlockSpec(memory_space=pltpu.VMEM),
        ],
        out_specs=pl.BlockSpec(memory_space=pltpu.VMEM),
        scratch_shapes=[
            pltpu.VMEM((tokens, features), jnp.bfloat16),
            pltpu.VMEM((tokens, features), jnp.bfloat16),
        ],
        compiler_params=pltpu.CompilerParams(vmem_limit_bytes=40 * 1024 * 1024),
        cost_estimate=pl.CostEstimate(
            flops=4 * samples * GROUP * tokens * features,
            bytes_accessed=4 * 1024 * 1024,
            transcendentals=samples * GROUP * tokens,
        ),
    )(place, query_rows, pairs)


def finish_kernel(tile_ref, came_ref, numer_ref, stats_ref, out_ref, pool_ref, sems):
    senders = came_ref.shape[0]
    slots = pool_ref.shape[0]
    local = out_ref.shape[0]
    half = tile_ref.shape[2]
    pool_rows = slots * half * 2
    copies = []
    for sender in range(senders):
        head, part = sender // 2, sender % 2
        copies.append(
            pltpu.make_async_copy(
                tile_ref.at[sender, 0:slots],
                pool_ref.at[
                    :,
                    part * half : (part + 1) * half,
                    :,
                    head * HEAD_FEATURES : (head + 1) * HEAD_FEATURES,
                ],
                sems.at[sender],
            )
        )
        copies[-1].start()

    first = pool_rows + GROUP * local

    def back(x, places):
        return pltpu.roll(x, 128 - places, 1)

    for head in range(KEY_VALUE_HEADS):
        peaks = [stats_ref[head, 0]]
        sums = [stats_ref[head, 1]]
        for part in range(2):
            terms = came_ref[2 * head + part, first : first + 2 * local, :]
            terms = terms.astype(jnp.float32)[:local]
            terms = (terms + back(terms, GROUP)) + back(terms, 2 * GROUP)
            peaks.append(terms)
            sums.append(back(terms, 3 * GROUP))
        peak = jnp.maximum(jnp.maximum(peaks[0], peaks[1]), peaks[2])
        scales = [jnp.exp(p - peak) for p in peaks]
        total = (sums[0] * scales[0] + sums[1] * scales[1]) + sums[2] * scales[2]
        scales = [s / total for s in scales]
        for g in range(0, GROUP, 2):
            rows = slice(g * local, (g + 2) * local)
            numers = [numer_ref[head, rows]] + [
                came_ref[
                    2 * head + part, pool_rows + g * local : pool_rows + (g + 2) * local, :
                ].astype(jnp.float32)
                for part in range(2)
            ]
            for k in range(2):
                mine = [n[k * local : (k + 1) * local] for n in numers]
                by = [s[:, g + k : g + k + 1] for s in scales]
                value = (mine[0] * by[0] + mine[1] * by[1]) + mine[2] * by[2]
                column = (head * GROUP + g + k) * HEAD_FEATURES
                out_ref[:, column : column + HEAD_FEATURES] = value.astype(jnp.bfloat16)

    for copy in copies:
        copy.wait()


def finish(came, numer, stats, local, slots):
    senders, rows, features = came.shape
    half = PAGE_TOKENS // 2
    tiles = came.reshape(senders, rows // (2 * half), half, 2, features)
    return pl.pallas_call(
        finish_kernel,
        out_shape=(
            jax.ShapeDtypeStruct((local, QUERY_HEADS * HEAD_FEATURES), jnp.bfloat16),
            jax.ShapeDtypeStruct(
                (slots, PAGE_TOKENS, 2, KEY_VALUE_HEADS * HEAD_FEATURES), jnp.bfloat16
            ),
        ),
        in_specs=[
            pl.BlockSpec(memory_space=pl.ANY),
            pl.BlockSpec(memory_space=pltpu.VMEM),
            pl.BlockSpec(memory_space=pltpu.VMEM),
            pl.BlockSpec(memory_space=pltpu.VMEM),
        ],
        out_specs=(pl.BlockSpec(memory_space=pltpu.VMEM), pl.BlockSpec(memory_space=pl.ANY)),
        scratch_shapes=[pltpu.SemaphoreType.DMA((senders,))],
        compiler_params=pltpu.CompilerParams(vmem_limit_bytes=32 * 1024 * 1024),
        cost_estimate=pl.CostEstimate(
            flops=6 * local * QUERY_HEADS * HEAD_FEATURES,
            bytes_accessed=4 * 1024 * 1024,
            transcendentals=0,
        ),
    )(tiles, came, numer, stats)


def gather_queries(local_queries, member, n_samp):
    local = local_queries.shape[0]
    held = local_queries.reshape(local, KEY_VALUE_HEADS, WIDTH).transpose(1, 0, 2)
    for step, place in enumerate((3, 2, 1, 0)):
        bit = (member >> place) & 1
        if place:
            half = held.shape[0] // 2
            kept = lax.dynamic_slice_in_dim(held, bit * half, half, 0)
            sent = lax.dynamic_slice_in_dim(held, (1 - bit) * half, half, 0)
        else:
            kept = sent = held
        pairs = [(i, i ^ (1 << place)) for i in range(n_samp)]
        came = lax.ppermute(sent, "samp", pairs)
        held = jnp.stack(
            [jnp.where(bit == 0, kept, came), jnp.where(bit == 0, came, kept)], axis=1 + step
        )
    return held.reshape(n_samp * local, WIDTH)


def body(n_inst, n_samp, prompt_key_values, match, page_list, queries, sample_key_values, gen_len):
    local_total = queries.shape[1]
    pages_dev = page_list.shape[2]
    half = PAGE_TOKENS // 2
    member = lax.axis_index("samp")
    local_queries = queries[0]

    pages = lax.all_to_all(prompt_key_values, "inst", split_axis=1, concat_axis=0, tiled=True)

    head_queries = gather_queries(local_queries, member, n_samp)

    sample_keys = sample_key_values[0, :, :, 0, :]
    sample_values = sample_key_values[0, :, :, 1, :]
    live_mask = jnp.arange(sample_keys.shape[1], dtype=jnp.int32)[None, :] < gen_len[0][:, None]
    own_peak, own_sum, own_numer = partial_own(local_queries, sample_keys, sample_values, live_mask)
    own_stats = jnp.stack([own_peak.transpose(1, 0, 2), own_sum.transpose(1, 0, 2)], axis=1)
    own_stats = jnp.pad(own_stats, ((0, 0), (0, 0), (0, 0), (0, 128 - GROUP)))
    own_numer = own_numer.transpose(1, 2, 0, 3).reshape(
        KEY_VALUE_HEADS, GROUP * local_total, HEAD_FEATURES
    )

    listed = page_list[0].reshape(-1)
    place = (listed % pages_dev) * n_samp + listed // pages_dev

    chosen = pages.at[match].get(mode="promise_in_bounds")
    chosen = chosen.reshape(n_inst, PAGE_TOKENS, 2, KEY_VALUE_HEADS, HEAD_FEATURES)
    chosen = chosen.transpose(0, 3, 1, 2, 4).reshape(n_inst * n_samp, half * 2, HEAD_FEATURES)
    pairs = lax.all_to_all(chosen, ("inst", "samp"), split_axis=0, concat_axis=0, tiled=True)
    pairs, place, head_queries, own_stats, own_numer = lax.optimization_barrier(
        (pairs, place, head_queries, own_stats, own_numer)
    )

    sent = partial_shared(place, head_queries, pairs, n_samp)
    came = lax.all_to_all(sent, "samp", split_axis=0, concat_axis=0, tiled=True)
    attended, page_pool = finish(came, own_numer, own_stats, local_total, pages_dev)
    return (attended[None], page_pool[None])


def solution(mesh):
    in_specs = (
        P("inst", "samp", None, None),
        P(),
        P("inst", None, None),
        P("inst", "samp", None),
        P("inst", "samp", None, None, None),
        P("inst", "samp"),
    )
    out_specs = (P("inst", "samp", None), P("inst", "samp", None, None, None))
    step = functools.partial(body, mesh.shape["inst"], mesh.shape["samp"])
    return jax.shard_map(step, mesh=mesh, in_specs=in_specs, out_specs=out_specs, check_vma=False)
```

time: 141 us -> 120 us (0.85)
  blocking collectives: 0 us -> 25.9 us
  local copies, waits for them, and re-layouts: 28.9 us -> 14.9 us
  between operations: 14.5 us -> 1.18 us
  other arithmetic: 10 us -> 1.78 us
  matrix products: 11 us -> 4.51 us
  waiting for transfers between devices: 35.2 us -> 31.9 us
    all_to_all x0 -> x1, blocking collectives: none -> 25.9 us  [body(): came = lax.all_to_all(sent, 'samp', split_axis=0, concat_axis=0, tiled=True)]
    ppermute x0 -> x4, starting transfers between devices: none -> 11 us  [gather_queries(): came = lax.ppermute(sent, 'samp', pairs)]
    all_to_all x2 -> x0, starting transfers between devices: 9.22 us -> none  [the longest x1 4.75 us: body(): lax.all_to_all(sent.reshape(n_samp, pages_dev, half * 2, HEAD_FEATURES),...]
    all_to_all x2 -> x0, waiting for transfers between devices: 8.5 us -> none  [the longest x1 5.67 us: body(): lax.all_to_all(part.reshape(n_samp, local_total, WIDTH + 128), 'samp', sp...]
    unnamed x79 -> x23, local copies, waits for them, and re-layouts: 8.47 us -> 0.34 us
    dot_general x8, matrix products: 6.9 us -> 1.95 us  [partial_own(): jnp.einsum('sgn,snd->sgd', weights.astype(jnp.bfloat16), value_block, pre...]
    reshape x4 -> x0, local copies, waits for them, and re-layouts: 4.69 us -> none  [the longest x1 2.44 us: body(): came = came.reshape(KEY_VALUE_HEADS, 2, pages_dev, half, 2, HEAD_FEATURES)]
    ppermute x0 -> x4, waiting for transfers between devices: none -> 4.53 us  [gather_queries(): came = lax.ppermute(sent, 'samp', pairs)]
  transfers between devices with their start and end apart: 5 -> 6, of which waited for: 4 -> 4; matrix products, arithmetic and copies ran while one was open for 32% -> 17% of each run, Pallas kernels for 7% -> 0%
where the time goes in v2:
time: 120 us
  waiting for transfers between devices  31.9 us (27%)
  starting transfers between devices  29.9 us (25%)
  blocking collectives  25.9 us (22%)
  local copies, waits for them, and re-layouts  14.9 us (12%)
  Pallas kernels  9.61 us (8%)
  matrix products  4.51 us (4%)
  other arithmetic  1.78 us (1%)
    all_to_all x1, blocking collectives, body(): came = lax.all_to_all(sent, 'samp', split_axis=0, concat_axis=0, tiled=True)  25.9 us
    all_to_all x1, waiting for transfers between devices, body(): lax.all_to_all(chosen, ('inst', 'samp'), split_axis=0, concat_axis=0, til...  22.1 us
    ppermute x4, starting transfers between devices, gather_queries(): came = lax.ppermute(sent, 'samp', pairs)  11 us
    all_to_all x1, starting transfers between devices, body(): lax.all_to_all(chosen, ('inst', 'samp'), split_axis=0, concat_axis=0, til...  10.4 us
    slice x1, local copies, waits for them, and re-layouts, body(): sample_values = sample_key_values[0, :, :, 1, :]  8.78 us
    all_to_all x1, starting transfers between devices, body(): lax.all_to_all(prompt_key_values, 'inst', split_axis=1, concat_axis=0, ti...  8.4 us
    pallas_call x1, Pallas kernels, partial_shared(): pl.pallas_call(shared_kernel, out_shape=jax.ShapeDtypeStruct((owners, sen...  7.43 us
    all_to_all x1, waiting for transfers between devices, body(): lax.all_to_all(prompt_key_values, 'inst', split_axis=1, concat_axis=0, ti...  5.31 us
  transfers between devices with their start and end apart: 6, of which 4 were waited for; matrix products, arithmetic and copies ran while one was open for 17% of the time, Pallas kernels for 0%

profile of v2, /device:TPU:1, one launch (start us, length us, event | category | flops | bytes accessed | tf_op | source)
XLA Modules:
  0.0 119.6 jit_solution(8472187704947924314)
XLA Ops:
  0.6 0.9 dynamic-slice_bitcast_fusion
  1.5 3.7 %collective-permute-start = (bf16[4,8,1536]{2,1,0:T(8,128)(2,1)S(1)}, bf16[4,8,1536]{2,1,0:T(8,128)(2,1)S(1)}, u32[]{:S(2)}, u32[]{:S(2)}) collective-permute-start(bf16[4,8,1536]{2,1,0:T(8,128)(2,1)S(1)} %dynamic-slice_bitcast_fusion), channel_id=1, source_target_pairs={{0,8},{1,9},{2,10},{3,11},{4,12},{5,13},{6,14},{7,15},{8,0},{9,1},... | collective-permute-start | bytes 294920 | tf_op jit(solution)/shard_map/ppermute | solution.py:253
  5.3 8.4 %all-to-all-start = ((bf16[1,256,2,1024]{3,2,0,1:T(2,128)(2,1)}), bf16[1,256,2,1024]{3,2,0,1:T(2,128)(2,1)S(1)}, u32[]{:S(2)}, u32[]{:S(2)}) async-start(bf16[1,256,2,1024]{3,2,0,1:T(2,128)(2,1)} %bitcast.152), calls=%async_computation | async-start | bytes 2097152 | tf_op jit(solution)/shard_map/all_to_all | solution.py:267
  13.7 0.0 copy-start
  13.7 8.8 %fusion.80 = (bf16[1,8,128,1,1024]{4,3,2,1,0:T(2,128)(2,1)S(1)}, bf16[1,8,128,1,1024]{4,3,2,1,0:T(2,128)(2,1)S(1)}) fusion(bf16[1,8,128,2,1024]{4,3,2,1,0:T(2,128)(2,1)} %param.10), kind=kLoop, calls=%fused_computation.153 | loop fusion | bytes 8388608 | tf_op jit(solution)/shard_map/slice | solution.py:272
  22.5 0.1 iota_compare_fusion.1
  22.6 1.7 %copy_bitcast_fusion = (bf16[8,128,1024]{2,1,0:T(8,128)(2,1)S(1)}, bf16[8,128,1024]{2,1,0:T(8,128)(2,1)S(1)}) fusion(bf16[1,8,128,1,1024]{4,3,2,1,0:T(2,128)(2,1)S(1)} %get-tuple-element.16, bf16[1,8,128,1,1024]{4,3,2,1,0:T(2,128)(2,1)S(1)} %get-tuple-element.17), kind=kLoop, calls=%fused_computation.1 | loop fusion | bytes 8388608 | tf_op jit(solution)/shard_map/squeeze | solution.py:272
  24.3 0.3 fusion.81
  24.6 0.2 fusion.39
  24.8 0.2 fusion.7
  25.1 0.3 fusion.82
  25.4 0.2 fusion.41
  25.6 0.2 fusion.6
  25.9 0.3 fusion.83
  26.2 0.2 fusion.43
  26.4 0.2 fusion.5
  26.6 0.3 fusion.84
  26.9 0.2 fusion.45
  27.1 0.2 fusion.4
  27.4 0.3 fusion.85
  27.7 0.3 fusion.86
  28.0 0.3 fusion.87
  28.4 0.3 fusion.88
  28.8 0.2 fusion.47
  28.9 0.2 fusion.49
  29.1 0.2 fusion.51
  29.3 0.2 fusion.53
  29.6 0.2 fusion.3
  29.8 0.2 fusion.2
  30.1 0.2 fusion.1
  30.3 0.2 fusion
  30.6 0.1 copy.124
  30.7 0.1 reshape_squeeze.6
  30.9 2.8 %collective-permute-start.1 = (bf16[2,2,8,1536]{3,2,1,0:T(8,128)(2,1)S(1)}, bf16[2,2,8,1536]{3,2,1,0:T(8,128)(2,1)S(1)}, u32[]{:S(2)}, u32[]{:S(2)}) collective-permute-start(bf16[2,2,8,1536]{3,2,1,0:T(8,128)(2,1)S(1)} %fusion.34), channel_id=1, source_target_pairs={{0,4},{1,5},{2,6},{3,7},{4,0},{5,1},{6,2},{7,3},{8,12},{9,13},{10,... | collective-permute-start | bytes 294920 | tf_op jit(solution)/shard_map/ppermute | solution.py:253
  33.7 5.3 %all-to-all-done = bf16[1,256,2,1024]{3,2,0,1:T(2,128)(2,1)S(1)} async-done(((bf16[1,256,2,1024]{3,2,0,1:T(2,128)(2,1)}), bf16[1,256,2,1024]{3,2,0,1:T(2,128)(2,1)S(1)}, u32[]{:S(2)}, u32[]{:S(2)}) %all-to-all-start) | async-done | bytes 1048608 | tf_op jit(solution)/shard_map/all_to_all | solution.py:267
  39.0 0.3 copy.67
  39.3 0.6 gather_fusion
  39.9 0.3 copy.88
  40.2 2.1 %copy.68 = bf16[16,8,16,2,128]{4,3,2,1,0:T(2,128)(2,1)} copy(bf16[16,8,16,2,128]{4,1,2,3,0:T(8,128)(2,1)S(1)} %bitcast.151) | data formatting | bytes 2097152 | tf_op jit(solution)/shard_map/transpose | solution.py:286
  42.3 10.4 %all-to-all-start.1 = ((bf16[256,16,128]{2,1,0:T(8,128)(2,1)}), bf16[256,16,128]{2,1,0:T(8,128)(2,1)S(1)}, u32[]{:S(2)}, u32[]{:S(2)}) async-start(bf16[256,16,128]{2,1,0:T(8,128)(2,1)} %bitcast.3), calls=%async_computation.1 | async-start | bytes 2097152 | tf_op jit(solution)/shard_map/all_to_all | solution.py:287
  52.8 1.5 %collective-permute-start.2 = (bf16[1,2,2,8,1536]{4,3,2,1,0:T(8,128)(2,1)S(1)}, bf16[1,2,2,8,1536]{4,3,2,1,0:T(8,128)(2,1)S(1)}, u32[]{:S(2)}, u32[]{:S(2)}) collective-permute-start(bf16[1,2,2,8,1536]{4,3,2,1,0:T(8,128)(2,1)S(1)} %fusion.32), channel_id=1, source_target_pairs={{0,2},{1,3},{2,0},{3,1},{4,6},{5,7},{6,4},{7,5},{8,10},{9,11},{10,... | collective-permute-start | bytes 294920 | tf_op jit(solution)/shard_map/ppermute | solution.py:253
  54.3 3.5 %collective-permute-done.2 = bf16[1,2,2,8,1536]{4,3,2,1,0:T(8,128)(2,1)S(1)} collective-permute-done((bf16[1,2,2,8,1536]{4,3,2,1,0:T(8,128)(2,1)S(1)}, bf16[1,2,2,8,1536]{4,3,2,1,0:T(8,128)(2,1)S(1)}, u32[]{:S(2)}, u32[]{:S(2)}) %collective-permute-start.2) | collective-permute-done | bytes 98336 | tf_op jit(solution)/shard_map/ppermute | solution.py:253
  57.8 3.0 %collective-permute-start.3 = (bf16[1,2,2,2,8,1536]{5,4,3,2,1,0:T(8,128)(2,1)S(1)}, bf16[1,2,2,2,8,1536]{5,4,3,2,1,0:T(8,128)(2,1)S(1)}, u32[]{:S(2)}, u32[]{:S(2)}) collective-permute-start(bf16[1,2,2,2,8,1536]{5,4,3,2,1,0:T(8,128)(2,1)S(1)} %pad_maximum_fusion.1), channel_id=1, source_target_pairs={{0,1},{1,0},{2,3},{3,2},{4,5},{5,4},{6,7},{7,6},{8,9},{9,8},{10,11... | collective-permute-start | bytes 589832 | tf_op jit(solution)/shard_map/ppermute | solution.py:253
  60.8 1.1 collective-permute-done.3
  61.9 22.1 %all-to-all-done.1.pair_ref = bf16[256,16,128]{2,1,0:T(8,128)(2,1)S(1)} async-done(((bf16[256,16,128]{2,1,0:T(8,128)(2,1)}), bf16[256,16,128]{2,1,0:T(8,128)(2,1)S(1)}, u32[]{:S(2)}, u32[]{:S(2)}) %all-to-all-start.1) | async-done | bytes 1048608 | tf_op jit(solution)/shard_map/all_to_all | solution.py:287
  84.0 7.4 %shard_map.77 = bf16[16,368,128]{2,1,0:T(8,128)(2,1)S(1)} custom-call(s32[256]{0:T(256)S(1)} %fusion.79.place_ref, bf16[128,1536]{1,0:T(8,128)(2,1)S(1)} %bitcast.148, bf16[256,16,128]{2,1,0:T(8,128)(2,1)S(1)} %all-to-all-done.1.pair_ref), custom_call_target="tpu_custom_call" | custom-call | flops 1610612736 | bytes 4194304 | tf_op jit(solution)/shard_map/pallas_call | solution.py:130
  91.4 25.9 %all_to_all.22.came_ref = bf16[16,368,128]{2,1,0:T(8,128)(2,1)S(1)} all-to-all(bf16[16,368,128]{2,1,0:T(8,128)(2,1)S(1)} %shard_map.77), channel_id=1, replica_groups=mesh['inst'=16,'samp'=16] {'samp'}, dimensions={0} | all-to-all | bytes 3014656 | tf_op jit(solution)/shard_map/all_to_all | solution.py:293
  117.3 2.2 %shard_map.78 = (bf16[8,12288]{1,0:T(8,128)(2,1)}, bf16[16,16,2,1024]{3,2,1,0:T(2,128)(2,1)}) custom-call(bf16[16,23,8,2,128]{4,3,2,1,0:T(2,128)(2,1)S(1)} %bitcast.146, bf16[16,368,128]{2,1,0:T(8,128)(2,1)S(1)} %all_to_all.22.came_ref, f32[8,96,128]{2,1,0:T(8,128)S(1)} %bitcast.147, f32[8,2,8,128]{3,2,1,0:T(8,128)S(1)} %select_maximum_fusion.stats_ref), custom_call_target="tpu_custom_call" | custom-call | flops 589824 | bytes 4194304 | tf_op jit(solution)/shard_map/pallas_call | solution.py:216
  (38 shorter events, 0.3 us)
Async XLA Ops:
  1.5 29.3 %collective-permute-start = (bf16[4,8,1536]{2,1,0:T(8,128)(2,1)S(1)}, bf16[4,8,1536]{2,1,0:T(8,128)(2,1)S(1)}, u32[]{:S(2)}, u32[]{:S(2)}) collective-permute-start(bf16[4,8,1536]{2,1,0:T(8,128)(2,1)S(1)} %dynamic-slice_bitcast_fusion), channel_id=1, source_target_pairs={{0,8},{1,9},{2,10},{3,11},{4,12},{5,13},{6,14},{7,15},{8,0},{9,1},... | collective-permute-start | bytes 294920 | tf_op jit(solution)/shard_map/ppermute | solution.py:253
  5.3 33.7 %all-to-all-start = ((bf16[1,256,2,1024]{3,2,0,1:T(2,128)(2,1)}), bf16[1,256,2,1024]{3,2,0,1:T(2,128)(2,1)S(1)}, u32[]{:S(2)}, u32[]{:S(2)}) async-start(bf16[1,256,2,1024]{3,2,0,1:T(2,128)(2,1)} %bitcast.152), calls=%async_computation | async-start | bytes 2097152 | tf_op jit(solution)/shard_map/all_to_all | solution.py:267
  13.7 8.8 %copy-start = (bf16[1,8,12288]{2,1,0:T(8,128)(2,1)S(1)}, bf16[1,8,12288]{2,1,0:T(8,128)(2,1)}, u32[]{:S(2)}) copy-start(bf16[1,8,12288]{2,1,0:T(8,128)(2,1)} %param.9) | copy-start | bytes 589828
  13.7 8.8 %copy-start.2 = (s32[1,8]{1,0:T(1,128)S(1)}, s32[1,8]{1,0:T(1,128)}, u32[]{:S(2)}) copy-start(s32[1,8]{1,0:T(1,128)} %param.11) | copy-start | bytes 100
  26.6 4.0 %copy-start.3 = (s32[16]{0:T(128)S(1)}, s32[16]{0:T(128)}, u32[]{:S(2)}) copy-start(s32[16]{0:T(128)} %param.7) | copy-start | bytes 196
  27.7 3.0 %copy-start.1 = (s32[1,16,16]{2,1,0:T(8,128)S(1)}, s32[1,16,16]{2,1,0:T(8,128)}, u32[]{:S(2)}) copy-start(s32[1,16,16]{2,1,0:T(8,128)} %param.8) | copy-start | bytes 3076
  30.9 21.8 %collective-permute-start.1 = (bf16[2,2,8,1536]{3,2,1,0:T(8,128)(2,1)S(1)}, bf16[2,2,8,1536]{3,2,1,0:T(8,128)(2,1)S(1)}, u32[]{:S(2)}, u32[]{:S(2)}) collective-permute-start(bf16[2,2,8,1536]{3,2,1,0:T(8,128)(2,1)S(1)} %fusion.34), channel_id=1, source_target_pairs={{0,4},{1,5},{2,6},{3,7},{4,0},{5,1},{6,2},{7,3},{8,12},{9,13},{10,... | collective-permute-start | bytes 294920 | tf_op jit(solution)/shard_map/ppermute | solution.py:253
  42.3 41.7 %all-to-all-start.1 = ((bf16[256,16,128]{2,1,0:T(8,128)(2,1)}), bf16[256,16,128]{2,1,0:T(8,128)(2,1)S(1)}, u32[]{:S(2)}, u32[]{:S(2)}) async-start(bf16[256,16,128]{2,1,0:T(8,128)(2,1)} %bitcast.3), calls=%async_computation.1 | async-start | bytes 2097152 | tf_op jit(solution)/shard_map/all_to_all | solution.py:287
  52.8 4.9 %collective-permute-start.2 = (bf16[1,2,2,8,1536]{4,3,2,1,0:T(8,128)(2,1)S(1)}, bf16[1,2,2,8,1536]{4,3,2,1,0:T(8,128)(2,1)S(1)}, u32[]{:S(2)}, u32[]{:S(2)}) collective-permute-start(bf16[1,2,2,8,1536]{4,3,2,1,0:T(8,128)(2,1)S(1)} %fusion.32), channel_id=1, source_target_pairs={{0,2},{1,3},{2,0},{3,1},{4,6},{5,7},{6,4},{7,5},{8,10},{9,11},{10,... | collective-permute-start | bytes 294920 | tf_op jit(solution)/shard_map/ppermute | solution.py:253
  57.8 4.0 %collective-permute-start.3 = (bf16[1,2,2,2,8,1536]{5,4,3,2,1,0:T(8,128)(2,1)S(1)}, bf16[1,2,2,2,8,1536]{5,4,3,2,1,0:T(8,128)(2,1)S(1)}, u32[]{:S(2)}, u32[]{:S(2)}) collective-permute-start(bf16[1,2,2,2,8,1536]{5,4,3,2,1,0:T(8,128)(2,1)S(1)} %pad_maximum_fusion.1), channel_id=1, source_target_pairs={{0,1},{1,0},{2,3},{3,2},{4,5},{5,4},{6,7},{7,6},{8,9},{9,8},{10,11... | collective-permute-start | bytes 589832 | tf_op jit(solution)/shard_map/ppermute | solution.py:253

commit v3 on v2

--- a/solution.py
+++ b/solution.py
@@ -62,13 +62,6 @@
     slots = pieces // owners
     local = samples // owners
 
-    def move(n, carry):
-        row = pl.multiple_of(lax.rem(n, slots) * rows, rows)
-        out_ref[lax.div(n, slots), pl.ds(row, rows), :] = pair_ref[place_ref[n]]
-        return carry
-
-    lax.fori_loop(0, pieces, move, 0, unroll=8)
-
     row = lax.broadcasted_iota(jnp.int32, (256, 256), 0)
     column = lax.broadcasted_iota(jnp.int32, (256, 256), 1)
     wanted = jnp.where(row < 128, 2 * row, 2 * (row - 128) + 1)
@@ -78,6 +71,9 @@
         apart = jnp.dot(pick, both, preferred_element_type=jnp.float32).astype(jnp.bfloat16)
         key_ref[step * 128 : (step + 1) * 128, :] = apart[:128]
         value_ref[step * 128 : (step + 1) * 128, :] = apart[128:]
+        for n in range(step * 16, (step + 1) * 16):
+            row = n % slots * rows
+            out_ref[n // slots, row : row + rows, :] = pair_ref[place_ref[n]]
 
     factor = SCALE * math.log2(math.e)
     lane = lax.broadcasted_iota(jnp.int32, (samples, 128), 1)
@@ -238,6 +234,34 @@
     )(tiles, came, numer, stats)
 
 
+def choose_kernel(match_ref, page_ref, out_ref):
+    for instance in range(out_ref.shape[0]):
+        page = page_ref[match_ref[instance]]
+        for head in range(KEY_VALUE_HEADS):
+            out_ref[instance, head] = page[
+                :, :, head * HEAD_FEATURES : (head + 1) * HEAD_FEATURES
+            ]
+
+
+def choose(match, pages):
+    instances, tokens = pages.shape[:2]
+    return pl.pallas_call(
+        choose_kernel,
+        out_shape=jax.ShapeDtypeStruct(
+            (instances, KEY_VALUE_HEADS, tokens, 2, HEAD_FEATURES), pages.dtype
+        ),
+        in_specs=[
+            pl.BlockSpec(memory_space=pltpu.SMEM),
+            pl.BlockSpec(memory_space=pltpu.VMEM),
+        ],
+        out_specs=pl.BlockSpec(memory_space=pltpu.VMEM),
+        compiler_params=pltpu.CompilerParams(vmem_limit_bytes=16 * 1024 * 1024),
+        cost_estimate=pl.CostEstimate(
+            flops=0, bytes_accessed=4 * 1024 * 1024, transcendentals=0
+        ),
+    )(match, pages)
+
+
 def gather_queries(local_queries, member, n_samp):
     local = local_queries.shape[0]
     held = local_queries.reshape(local, KEY_VALUE_HEADS, WIDTH).transpose(1, 0, 2)
@@ -266,10 +290,10 @@
 
     pages = lax.all_to_all(prompt_key_values, "inst", split_axis=1, concat_axis=0, tiled=True)
 
-    head_queries = gather_queries(local_queries, member, n_samp)
-
     sample_keys = sample_key_values[0, :, :, 0, :]
     sample_values = sample_key_values[0, :, :, 1, :]
+    sample_keys, sent_queries = lax.optimization_barrier((sample_keys, local_queries))
+    head_queries = gather_queries(sent_queries, member, n_samp)
     live_mask = jnp.arange(sample_keys.shape[1], dtype=jnp.int32)[None, :] < gen_len[0][:, None]
     own_peak, own_sum, own_numer = partial_own(local_queries, sample_keys, sample_values, live_mask)
     own_stats = jnp.stack([own_peak.transpose(1, 0, 2), own_sum.transpose(1, 0, 2)], axis=1)
@@ -281,9 +305,7 @@
     listed = page_list[0].reshape(-1)
     place = (listed % pages_dev) * n_samp + listed // pages_dev
 
-    chosen = pages.at[match].get(mode="promise_in_bounds")
-    chosen = chosen.reshape(n_inst, PAGE_TOKENS, 2, KEY_VALUE_HEADS, HEAD_FEATURES)
-    chosen = chosen.transpose(0, 3, 1, 2, 4).reshape(n_inst * n_samp, half * 2, HEAD_FEATURES)
+    chosen = choose(match, pages).reshape(n_inst * n_samp, half * 2, HEAD_FEATURES)
     pairs = lax.all_to_all(chosen, ("inst", "samp"), split_axis=0, concat_axis=0, tiled=True)
     pairs, place, head_queries, own_stats, own_numer = lax.optimization_barrier(
         (pairs, place, head_queries, own_stats, own_numer)

time: 120 us -> 131 us (1.092)
  local copies, waits for them, and re-layouts: 14.9 us -> 23.3 us
  waiting for transfers between devices: 31.9 us -> 25.8 us
  matrix products: 4.51 us -> 9.87 us
  other arithmetic: 1.78 us -> 3.42 us
    unnamed x23 -> x30, local copies, waits for them, and re-layouts: 0.34 us -> 8.36 us
    all_to_all x1, waiting for transfers between devices: 5.31 us -> 0.01 us  [body(): lax.all_to_all(prompt_key_values, 'inst', split_axis=1, concat_axis=0, ti...]
    dot_general x8, matrix products: 1.95 us -> 5.32 us  [partial_own(): jnp.einsum('sgn,snd->sgd', weights.astype(jnp.bfloat16), value_block, pre...]
    pallas_call x0 -> x1, Pallas kernels: none -> 2.09 us  [choose(): pl.pallas_call(choose_kernel, out_shape=jax.ShapeDtypeStruct((instances,...]
    transpose x1 -> x0, local copies, waits for them, and re-layouts: 2.07 us -> none  [body(): chosen.transpose(0, 3, 1, 2, 4)]
    dot_general x8, matrix products: 2.56 us -> 4.55 us  [partial_own(): jnp.einsum('sgd,snd->sgn', block, key_block, preferred_element_type=jnp.f...]
    pallas_call x1, Pallas kernels: 7.43 us -> 6.02 us  [partial_shared(): pl.pallas_call(shared_kernel, out_shape=jax.ShapeDtypeStruct((owners, sen...]
    squeeze x1, local copies, waits for them, and re-layouts: 1.7 us -> 3.06 us  [body(): sample_values = sample_key_values[0, :, :, 1, :]]
  transfers between devices with their start and end apart: 6 -> 6, of which waited for: 4 -> 3; matrix products, arithmetic and copies ran while one was open for 17% -> 18% of each run, Pallas kernels for 0% -> 2%
where the time goes in v3:
time: 131 us; the launch traced here: 130 us
  starting transfers between devices  30.5 us (23%)
  blocking collectives  25.9 us (20%)
  waiting for transfers between devices  25.8 us (20%)
  local copies, waits for them, and re-layouts  23.3 us (18%)
  Pallas kernels  10.3 us (8%)
  matrix products  9.87 us (8%)
  other arithmetic  3.42 us (3%)
    all_to_all x1, blocking collectives, body(): came = lax.all_to_all(sent, 'samp', split_axis=0, concat_axis=0, tiled=True)  25.9 us
    all_to_all x1, waiting for transfers between devices, body(): lax.all_to_all(chosen, ('inst', 'samp'), split_axis=0, concat_axis=0, til...  22.1 us
    all_to_all x1, starting transfers between devices, body(): lax.all_to_all(chosen, ('inst', 'samp'), split_axis=0, concat_axis=0, til...  11.1 us
    ppermute x4, starting transfers between devices, gather_queries(): came = lax.ppermute(sent, 'samp', pairs)  11 us
    slice x1, local copies, waits for them, and re-layouts, body(): sample_values = sample_key_values[0, :, :, 1, :]  8.81 us
    all_to_all x1, starting transfers between devices, body(): lax.all_to_all(prompt_key_values, 'inst', split_axis=1, concat_axis=0, ti...  8.4 us
    unnamed x30, local copies, waits for them, and re-layouts  8.36 us
    pallas_call x1, Pallas kernels, partial_shared(): pl.pallas_call(shared_kernel, out_shape=jax.ShapeDtypeStruct((owners, sen...  6.02 us
  transfers between devices with their start and end apart: 6, of which 3 were waited for; matrix products, arithmetic and copies ran while one was open for 18% of the time, Pallas kernels for 2%

profile of v3, /device:TPU:1, one launch (start us, length us, event | category | flops | bytes accessed | tf_op | source)
XLA Modules:
  0.0 130.1 jit_solution(2203270198288031420)
XLA Ops:
  0.6 8.8 %fusion.88 = (bf16[1,8,128,1,1024]{4,3,2,1,0:T(2,128)(2,1)S(1)}, bf16[1,8,128,1,1024]{4,3,2,1,0:T(2,128)(2,1)S(1)}) fusion(bf16[1,8,128,2,1024]{4,3,2,1,0:T(2,128)(2,1)} %param.10), kind=kLoop, calls=%fused_computation.158 | loop fusion | bytes 8388608 | tf_op jit(solution)/shard_map/slice | solution.py:294
  9.5 3.1 %copy_bitcast_fusion = (bf16[8,128,1024]{2,1,0:T(8,128)(2,1)S(1)}, bf16[8,128,1024]{2,1,0:T(8,128)(2,1)}) fusion(bf16[1,8,128,1,1024]{4,3,2,1,0:T(2,128)(2,1)S(1)} %get-tuple-element.20, bf16[1,8,128,1,1024]{4,3,2,1,0:T(2,128)(2,1)S(1)} %get-tuple-element.21), kind=kLoop, calls=%fused_computation | loop fusion | bytes 8388608 | tf_op jit(solution)/shard_map/squeeze | solution.py:294
  12.5 0.6 dynamic-slice_bitcast_fusion
  13.2 3.7 %collective-permute-start = (bf16[4,8,1536]{2,1,0:T(8,128)(2,1)}, bf16[4,8,1536]{2,1,0:T(8,128)(2,1)}, u32[]{:S(2)}, u32[]{:S(2)}) collective-permute-start(bf16[4,8,1536]{2,1,0:T(8,128)(2,1)} %dynamic-slice_bitcast_fusion), channel_id=1, source_target_pairs={{0,8},{1,9},{2,10},{3,11},{4,12},{5,13},{6,14},{7,15},{8,0},{9,1},... | collective-permute-start | bytes 294920 | tf_op jit(solution)/shard_map/ppermute | solution.py:277
  16.9 8.4 %all-to-all-start = ((bf16[1,256,2,1024]{3,2,0,1:T(2,128)(2,1)}), bf16[1,256,2,1024]{3,2,0,1:T(2,128)(2,1)S(1)}, u32[]{:S(2)}, u32[]{:S(2)}) async-start(bf16[1,256,2,1024]{3,2,0,1:T(2,128)(2,1)} %bitcast.157), calls=%async_computation | async-start | bytes 2097152 | tf_op jit(solution)/shard_map/all_to_all | solution.py:291
  25.5 1.4 %fusion.89 = (f32[8,12]{1,0:T(8,128)S(1)}, f32[8,12,128]{2,1,0:T(8,128)S(1)}) fusion(bf16[8,12,128]{2,0,1:T(8,128)(2,1)S(1)} %get-tuple-element.37, bf16[8,128,1024]{2,1,0:T(8,128)(2,1)} %get-tuple-element.12, pred[8,128]{1,0:T(8,128)(4,1)S(1)} %iota_compare_fusion.1), kind=kOutput, calls=%fused_computation.159 | convolution fusion | flops 3182496 | bytes 337280 | tf_op jit(solution)/shard_map/sgd,snd->sgn/dot_general | solution.py:31
  26.8 0.6 constant_dynamic-update-slice_fusion.7
  27.9 1.3 fusion.90
  29.6 0.3 fusion.91
  30.1 0.2 fusion.5
  30.4 0.3 fusion.92
  31.1 0.3 fusion.93
  31.4 0.3 fusion.94
  31.8 0.3 fusion.95
  32.1 0.3 fusion.96
  32.5 0.6 constant_dynamic-update-slice_fusion.6
  33.1 0.6 constant_dynamic-update-slice_fusion.5
  33.7 0.6 constant_dynamic-update-slice_fusion.4
  34.3 0.6 constant_dynamic-update-slice_fusion.15
  34.8 0.6 constant_dynamic-update-slice_fusion.3
  35.6 0.6 constant_dynamic-update-slice_fusion.2
  36.4 0.6 constant_dynamic-update-slice_fusion.1
  37.1 0.6 constant_dynamic-update-slice_fusion
  37.7 0.6 constant_dynamic-update-slice_fusion.14
  38.3 0.6 constant_dynamic-update-slice_fusion.13
  38.9 0.6 constant_dynamic-update-slice_fusion.12
  39.5 0.6 constant_dynamic-update-slice_fusion.11
  40.1 0.6 constant_dynamic-update-slice_fusion.10
  40.7 0.6 constant_dynamic-update-slice_fusion.9
  41.3 0.9 fusion.3
  42.2 0.9 fusion.2
  43.0 1.7 %fusion.1 = f32[8,8,12,128]{3,2,0,1:T(8,128)} fusion(f32[8,8,12,128]{3,2,0,1:T(8,128)} %fusion.2, bf16[8,128,1024]{2,1,0:T(8,128)(2,1)S(1)} %get-tuple-element.54, f32[8,12,128]{2,1,0:T(8,128)} %copy-done.4, f32[8,12]{1,0:T(8,128)} %copy-done.5), kind=kOutput, calls=%fused_computation.5 | convolution fusion | flops 3170304 | bytes 397312 | tf_op jit(solution)/shard_map/sgn,snd->sgd/dot_general | solution.py:38
  44.8 0.9 fusion
  45.8 0.9 fusion.45
  46.8 2.8 %collective-permute-start.1 = (bf16[2,2,8,1536]{3,2,1,0:T(8,128)(2,1)S(1)}, bf16[2,2,8,1536]{3,2,1,0:T(8,128)(2,1)S(1)}, u32[]{:S(2)}, u32[]{:S(2)}) collective-permute-start(bf16[2,2,8,1536]{3,2,1,0:T(8,128)(2,1)S(1)} %fusion.42), channel_id=1, source_target_pairs={{0,4},{1,5},{2,6},{3,7},{4,0},{5,1},{6,2},{7,3},{8,12},{9,13},{10,... | collective-permute-start | bytes 294920 | tf_op jit(solution)/shard_map/ppermute | solution.py:277
  49.6 0.6 constant_dynamic-update-slice_fusion.8
  50.2 1.2 copy.83
  51.5 2.1 %shard_map.77 = bf16[16,8,16,2,128]{4,3,2,1,0:T(2,128)(2,1)} custom-call(s32[16]{0:T(128)S(1)} %copy-done, bf16[16,16,2,1024]{3,2,1,0:T(2,128)(2,1)S(1)} %bitcast.154), custom_call_target="tpu_custom_call" | custom-call | bytes 4194304 | tf_op jit(solution)/shard_map/pallas_call | solution.py:248
  53.6 11.1 %all-to-all-start.1 = ((bf16[256,16,128]{2,1,0:T(8,128)(2,1)}), bf16[256,16,128]{2,1,0:T(8,128)(2,1)S(1)}, u32[]{:S(2)}, u32[]{:S(2)}) async-start(bf16[256,16,128]{2,1,0:T(8,128)(2,1)} %bitcast.2), calls=%async_computation.1 | async-start | bytes 2097152 | tf_op jit(solution)/shard_map/all_to_all | solution.py:309
  64.7 1.5 %collective-permute-start.2 = (bf16[1,2,2,8,1536]{4,3,2,1,0:T(8,128)(2,1)S(1)}, bf16[1,2,2,8,1536]{4,3,2,1,0:T(8,128)(2,1)S(1)}, u32[]{:S(2)}, u32[]{:S(2)}) collective-permute-start(bf16[1,2,2,8,1536]{4,3,2,1,0:T(8,128)(2,1)S(1)} %fusion.40), channel_id=1, source_target_pairs={{0,2},{1,3},{2,0},{3,1},{4,6},{5,7},{6,4},{7,5},{8,10},{9,11},{10,... | collective-permute-start | bytes 294920 | tf_op jit(solution)/shard_map/ppermute | solution.py:277
  66.2 0.8 select_maximum_fusion.stats_ref
  67.0 2.7 %collective-permute-done.2 = bf16[1,2,2,8,1536]{4,3,2,1,0:T(8,128)(2,1)S(1)} collective-permute-done((bf16[1,2,2,8,1536]{4,3,2,1,0:T(8,128)(2,1)S(1)}, bf16[1,2,2,8,1536]{4,3,2,1,0:T(8,128)(2,1)S(1)}, u32[]{:S(2)}, u32[]{:S(2)}) %collective-permute-start.2) | collective-permute-done | bytes 98336 | tf_op jit(solution)/shard_map/ppermute | solution.py:277
  69.7 3.0 %collective-permute-start.3 = (bf16[1,2,2,2,8,1536]{5,4,3,2,1,0:T(8,128)(2,1)S(1)}, bf16[1,2,2,2,8,1536]{5,4,3,2,1,0:T(8,128)(2,1)S(1)}, u32[]{:S(2)}, u32[]{:S(2)}) collective-permute-start(bf16[1,2,2,2,8,1536]{5,4,3,2,1,0:T(8,128)(2,1)S(1)} %pad_maximum_fusion.1), channel_id=1, source_target_pairs={{0,1},{1,0},{2,3},{3,2},{4,5},{5,4},{6,7},{7,6},{8,9},{9,8},{10,11... | collective-permute-start | bytes 589832 | tf_op jit(solution)/shard_map/ppermute | solution.py:277
  72.7 1.1 collective-permute-done.3
  73.8 22.1 %all-to-all-done.1.pair_ref = bf16[256,16,128]{2,1,0:T(8,128)(2,1)S(1)} async-done(((bf16[256,16,128]{2,1,0:T(8,128)(2,1)}), bf16[256,16,128]{2,1,0:T(8,128)(2,1)S(1)}, u32[]{:S(2)}, u32[]{:S(2)}) %all-to-all-start.1) | async-done | bytes 1048608 | tf_op jit(solution)/shard_map/all_to_all | solution.py:309
  95.9 6.0 %shard_map.78 = bf16[16,368,128]{2,1,0:T(8,128)(2,1)S(1)} custom-call(s32[256]{0:T(256)S(1)} %fusion.87.place_ref, bf16[128,1536]{1,0:T(8,128)(2,1)S(1)} %bitcast.156, bf16[256,16,128]{2,1,0:T(8,128)(2,1)S(1)} %all-to-all-done.1.pair_ref), custom_call_target="tpu_custom_call" | custom-call | flops 1610612736 | bytes 4194304 | tf_op jit(solution)/shard_map/pallas_call | solution.py:126
  101.9 25.9 %all_to_all.22.came_ref = bf16[16,368,128]{2,1,0:T(8,128)(2,1)S(1)} all-to-all(bf16[16,368,128]{2,1,0:T(8,128)(2,1)S(1)} %shard_map.78), channel_id=1, replica_groups=mesh['inst'=16,'samp'=16] {'samp'}, dimensions={0} | all-to-all | bytes 3014656 | tf_op jit(solution)/shard_map/all_to_all | solution.py:315
  127.8 2.2 %shard_map.79 = (bf16[8,12288]{1,0:T(8,128)(2,1)}, bf16[16,16,2,1024]{3,2,1,0:T(2,128)(2,1)}) custom-call(bf16[16,23,8,2,128]{4,3,2,1,0:T(2,128)(2,1)S(1)} %bitcast.153, bf16[16,368,128]{2,1,0:T(8,128)(2,1)S(1)} %all_to_all.22.came_ref, f32[8,96,128]{2,1,0:T(8,128)S(1)} %bitcast.155, f32[8,2,8,128]{3,2,1,0:T(8,128)S(1)} %select_maximum_fusion.stats_ref), custom_call_target="tpu_custom_call" | custom-call | flops 589824 | bytes 4194304 | tf_op jit(solution)/shard_map/pallas_call | solution.py:212
  (41 shorter events, 2.6 us)
Async XLA Ops:
  9.5 3.1 %copy-start.2 = (bf16[1,8,12288]{2,1,0:T(8,128)(2,1)S(1)}, bf16[1,8,12288]{2,1,0:T(8,128)(2,1)}, u32[]{:S(2)}) copy-start(bf16[1,8,12288]{2,1,0:T(8,128)(2,1)} %param.9) | copy-start | bytes 589828
  12.5 12.8 %copy-start.7 = (s32[1,8]{1,0:T(1,128)S(1)}, s32[1,8]{1,0:T(1,128)}, u32[]{:S(2)}) copy-start(s32[1,8]{1,0:T(1,128)} %param.11) | copy-start | bytes 100
  13.2 32.6 %collective-permute-start = (bf16[4,8,1536]{2,1,0:T(8,128)(2,1)}, bf16[4,8,1536]{2,1,0:T(8,128)(2,1)}, u32[]{:S(2)}, u32[]{:S(2)}) collective-permute-start(bf16[4,8,1536]{2,1,0:T(8,128)(2,1)} %dynamic-slice_bitcast_fusion), channel_id=1, source_target_pairs={{0,8},{1,9},{2,10},{3,11},{4,12},{5,13},{6,14},{7,15},{8,0},{9,1},... | collective-permute-start | bytes 294920 | tf_op jit(solution)/shard_map/ppermute | solution.py:277
  16.9 34.5 %all-to-all-start = ((bf16[1,256,2,1024]{3,2,0,1:T(2,128)(2,1)}), bf16[1,256,2,1024]{3,2,0,1:T(2,128)(2,1)S(1)}, u32[]{:S(2)}, u32[]{:S(2)}) async-start(bf16[1,256,2,1024]{3,2,0,1:T(2,128)(2,1)} %bitcast.157), calls=%async_computation | async-start | bytes 2097152 | tf_op jit(solution)/shard_map/all_to_all | solution.py:291
  25.3 4.3 %copy-start.1 = (bf16[8,128,1024]{2,1,0:T(8,128)(2,1)S(1)}, bf16[8,128,1024]{2,1,0:T(8,128)(2,1)}, u32[]{:S(2)}) copy-start(bf16[8,128,1024]{2,1,0:T(8,128)(2,1)} %get-tuple-element.12) | copy-start | bytes 6291460
  31.1 1.3 %copy-start.3 = (f32[8,8,12,128]{3,2,0,1:T(8,128)}, f32[8,8,12,128]{3,2,0,1:T(8,128)S(1)}, u32[]{:S(2)}) copy-start(f32[8,8,12,128]{3,2,0,1:T(8,128)S(1)} %fusion.4) | copy-start | bytes 1179652
  32.1 4.8 %copy-start.4 = (f32[8,12,128]{2,1,0:T(8,128)}, f32[8,12,128]{2,1,0:T(8,128)S(1)}, u32[]{:S(2)}) copy-start(f32[8,12,128]{2,1,0:T(8,128)S(1)} %get-tuple-element.51) | copy-start | bytes 147460
  32.1 5.0 %copy-start.5 = (f32[8,12]{1,0:T(8,128)}, f32[8,12]{1,0:T(8,128)S(1)}, u32[]{:S(2)}) copy-start(f32[8,12]{1,0:T(8,128)S(1)} %get-tuple-element.50) | copy-start | bytes 1156
  32.1 19.3 %copy-start = (s32[16]{0:T(128)S(1)}, s32[16]{0:T(128)}, u32[]{:S(2)}) copy-start(s32[16]{0:T(128)} %match_ref.1) | copy-start | bytes 196
  42.2 9.2 %copy-start.6 = (s32[1,16,16]{2,1,0:T(8,128)S(1)}, s32[1,16,16]{2,1,0:T(8,128)}, u32[]{:S(2)}) copy-start(s32[1,16,16]{2,1,0:T(8,128)} %param.8) | copy-start | bytes 3076
  46.8 17.9 %collective-permute-start.1 = (bf16[2,2,8,1536]{3,2,1,0:T(8,128)(2,1)S(1)}, bf16[2,2,8,1536]{3,2,1,0:T(8,128)(2,1)S(1)}, u32[]{:S(2)}, u32[]{:S(2)}) collective-permute-start(bf16[2,2,8,1536]{3,2,1,0:T(8,128)(2,1)S(1)} %fusion.42), channel_id=1, source_target_pairs={{0,4},{1,5},{2,6},{3,7},{4,0},{5,1},{6,2},{7,3},{8,12},{9,13},{10,... | collective-permute-start | bytes 294920 | tf_op jit(solution)/shard_map/ppermute | solution.py:277
  53.6 42.4 %all-to-all-start.1 = ((bf16[256,16,128]{2,1,0:T(8,128)(2,1)}), bf16[256,16,128]{2,1,0:T(8,128)(2,1)S(1)}, u32[]{:S(2)}, u32[]{:S(2)}) async-start(bf16[256,16,128]{2,1,0:T(8,128)(2,1)} %bitcast.2), calls=%async_computation.1 | async-start | bytes 2097152 | tf_op jit(solution)/shard_map/all_to_all | solution.py:309
  64.7 4.9 %collective-permute-start.2 = (bf16[1,2,2,8,1536]{4,3,2,1,0:T(8,128)(2,1)S(1)}, bf16[1,2,2,8,1536]{4,3,2,1,0:T(8,128)(2,1)S(1)}, u32[]{:S(2)}, u32[]{:S(2)}) collective-permute-start(bf16[1,2,2,8,1536]{4,3,2,1,0:T(8,128)(2,1)S(1)} %fusion.40), channel_id=1, source_target_pairs={{0,2},{1,3},{2,0},{3,1},{4,6},{5,7},{6,4},{7,5},{8,10},{9,11},{10,... | collective-permute-start | bytes 294920 | tf_op jit(solution)/shard_map/ppermute | solution.py:277
  69.7 4.0 %collective-permute-start.3 = (bf16[1,2,2,2,8,1536]{5,4,3,2,1,0:T(8,128)(2,1)S(1)}, bf16[1,2,2,2,8,1536]{5,4,3,2,1,0:T(8,128)(2,1)S(1)}, u32[]{:S(2)}, u32[]{:S(2)}) collective-permute-start(bf16[1,2,2,2,8,1536]{5,4,3,2,1,0:T(8,128)(2,1)S(1)} %pad_maximum_fusion.1), channel_id=1, source_target_pairs={{0,1},{1,0},{2,3},{3,2},{4,5},{5,4},{6,7},{7,6},{8,9},{9,8},{10,11... | collective-permute-start | bytes 589832 | tf_op jit(solution)/shard_map/ppermute | solution.py:277

commit v4 on v3

--- a/solution.py
+++ b/solution.py
@@ -17,34 +17,65 @@
 SCALE = HEAD_FEATURES ** (-0.5)
 
 
-def partial_own(query_rows, sample_keys, sample_values, live_mask):
-    count = query_rows.shape[0]
-    peaks = []
-    sums = []
-    numers = []
-    for head in range(KEY_VALUE_HEADS):
-        block = query_rows[:, head * WIDTH : (head + 1) * WIDTH].reshape(
-            count, GROUP, HEAD_FEATURES
-        )
-        key_block = sample_keys[:, :, head * HEAD_FEATURES : (head + 1) * HEAD_FEATURES]
-        value_block = sample_values[:, :, head * HEAD_FEATURES : (head + 1) * HEAD_FEATURES]
-        scores = jnp.einsum(
-            "sgd,snd->sgn", block, key_block, preferred_element_type=jnp.float32
-        ) * SCALE
-        scores = jnp.where(live_mask[:, None, :], scores, -jnp.inf)
-        peak = jnp.max(scores, axis=-1)
-        weights = jnp.exp(scores - peak[..., None])
-        weight_sum = jnp.sum(weights, axis=-1)
-        numer = jnp.einsum(
-            "sgn,snd->sgd",
-            weights.astype(jnp.bfloat16),
-            value_block,
-            preferred_element_type=jnp.float32,
-        )
-        peaks.append(peak)
-        sums.append(weight_sum)
-        numers.append(numer)
-    return (jnp.stack(peaks, axis=1), jnp.stack(sums, axis=1), jnp.stack(numers, axis=1))
+def own_kernel(head_at, length_ref, query_ref, cache_ref, numer_ref, stats_ref):
+    samples, positions = cache_ref.shape[:2]
+    factor = SCALE * math.log2(math.e)
+    rows = query_ref.shape[2]
+    column = lax.broadcasted_iota(jnp.int32, (rows, 2 * positions), 1)
+    diagonal = lax.broadcasted_iota(jnp.int32, (rows, 128), 0) == lax.broadcasted_iota(
+        jnp.int32, (rows, 128), 1
+    )
+
+    def across(x):
+        return jnp.sum(jnp.where(diagonal, x, 0.0), axis=0, keepdims=True)
+
+    def one_head(head, carry):
+        start = pl.multiple_of(head * HEAD_FEATURES, HEAD_FEATURES)
+        for sample in range(samples):
+            live = (column % 2 == 0) & (column < 2 * length_ref[sample])
+            both = cache_ref[sample, :, :, pl.ds(start, HEAD_FEATURES)].reshape(
+                2 * positions, HEAD_FEATURES
+            )
+            scores = lax.dot_general(
+                query_ref[sample, head_at + head], both, (((1,), (1,)), ((), ())),
+                preferred_element_type=jnp.float32,
+            )
+            top = jnp.max(jnp.where(live, scores, -jnp.inf), axis=-1, keepdims=True)
+            weights = jnp.where(live, jnp.exp2((scores - top) * factor), 0.0)
+            total = jnp.sum(weights, axis=-1, keepdims=True)
+            onto_values = pltpu.roll(weights, 1, 1).astype(jnp.bfloat16)
+            numer = jnp.dot(onto_values, both, preferred_element_type=jnp.float32)
+            numer_ref[head, :, sample, :] = numer[:GROUP]
+            stats_ref[head, 0, sample : sample + 1, :] = across(top * SCALE)
+            stats_ref[head, 1, sample : sample + 1, :] = across(total)
+        return carry
+
+    lax.fori_loop(0, numer_ref.shape[0], one_head, 0)
+
+
+def partial_own(lengths, grouped, cache, which, parts):
+    samples, positions = cache.shape[:2]
+    heads = KEY_VALUE_HEADS // parts
+    block = (samples, positions, 2, heads * HEAD_FEATURES)
+    return pl.pallas_call(
+        functools.partial(own_kernel, which * heads),
+        grid=(1,),
+        out_shape=(
+            jax.ShapeDtypeStruct((heads, GROUP, samples, HEAD_FEATURES), jnp.float32),
+            jax.ShapeDtypeStruct((heads, 2, samples, 128), jnp.float32),
+        ),
+        in_specs=[
+            pl.BlockSpec(memory_space=pltpu.SMEM),
+            pl.BlockSpec(memory_space=pltpu.VMEM),
+            pl.BlockSpec(block, lambda i: (0, 0, 0, which)),
+        ],
+        out_specs=(
+            pl.BlockSpec(memory_space=pltpu.VMEM),
+            pl.BlockSpec(memory_space=pltpu.VMEM),
+        ),
+        compiler_params=pltpu.CompilerParams(vmem_limit_bytes=24 * 1024 * 1024),
+        cost_estimate=pl.CostEstimate(flops=0, bytes_accessed=65536, transcendentals=0),
+    )(lengths, grouped, cache)
 
 
 def split3(x):
@@ -145,7 +176,8 @@
     )(place, query_rows, pairs)
 
 
-def finish_kernel(tile_ref, came_ref, numer_ref, stats_ref, out_ref, pool_ref, sems):
+def finish_kernel(tile_ref, came_ref, *refs):
+    own_refs, (out_ref, pool_ref, sems) = refs[:-3], refs[-3:]
     senders = came_ref.shape[0]
     slots = pool_ref.shape[0]
     local = out_ref.shape[0]
@@ -174,8 +206,10 @@
         return pltpu.roll(x, 128 - places, 1)
 
     for head in range(KEY_VALUE_HEADS):
-        peaks = [stats_ref[head, 0]]
-        sums = [stats_ref[head, 1]]
+        heads = own_refs[0].shape[0]
+        numer_ref, stats_ref = own_refs[head // heads * 2 : head // heads * 2 + 2]
+        peaks = [stats_ref[head % heads, 0]]
+        sums = [stats_ref[head % heads, 1]]
         for part in range(2):
             terms = came_ref[2 * head + part, first : first + 2 * local, :]
             terms = terms.astype(jnp.float32)[:local]
@@ -188,7 +222,7 @@
         scales = [s / total for s in scales]
         for g in range(0, GROUP, 2):
             rows = slice(g * local, (g + 2) * local)
-            numers = [numer_ref[head, rows]] + [
+            numers = [numer_ref[head % heads, g : g + 2].reshape(2 * local, HEAD_FEATURES)] + [
                 came_ref[
                     2 * head + part, pool_rows + g * local : pool_rows + (g + 2) * local, :
                 ].astype(jnp.float32)
@@ -205,7 +239,7 @@
         copy.wait()
 
 
-def finish(came, numer, stats, local, slots):
+def finish(came, own, local, slots):
     senders, rows, features = came.shape
     half = PAGE_TOKENS // 2
     tiles = came.reshape(senders, rows // (2 * half), half, 2, features)
@@ -219,10 +253,8 @@
         ),
         in_specs=[
             pl.BlockSpec(memory_space=pl.ANY),
-            pl.BlockSpec(memory_space=pltpu.VMEM),
-            pl.BlockSpec(memory_space=pltpu.VMEM),
-            pl.BlockSpec(memory_space=pltpu.VMEM),
-        ],
+        ]
+        + [pl.BlockSpec(memory_space=pltpu.VMEM)] * (1 + len(own)),
         out_specs=(pl.BlockSpec(memory_space=pltpu.VMEM), pl.BlockSpec(memory_space=pl.ANY)),
         scratch_shapes=[pltpu.SemaphoreType.DMA((senders,))],
         compiler_params=pltpu.CompilerParams(vmem_limit_bytes=32 * 1024 * 1024),
@@ -231,7 +263,7 @@
             bytes_accessed=4 * 1024 * 1024,
             transcendentals=0,
         ),
-    )(tiles, came, numer, stats)
+    )(tiles, came, *own)
 
 
 def choose_kernel(match_ref, page_ref, out_ref):
@@ -262,23 +294,18 @@
     )(match, pages)
 
 
-def gather_queries(local_queries, member, n_samp):
-    local = local_queries.shape[0]
-    held = local_queries.reshape(local, KEY_VALUE_HEADS, WIDTH).transpose(1, 0, 2)
-    for step, place in enumerate((3, 2, 1, 0)):
-        bit = (member >> place) & 1
-        if place:
-            half = held.shape[0] // 2
-            kept = lax.dynamic_slice_in_dim(held, bit * half, half, 0)
-            sent = lax.dynamic_slice_in_dim(held, (1 - bit) * half, half, 0)
-        else:
-            kept = sent = held
-        pairs = [(i, i ^ (1 << place)) for i in range(n_samp)]
-        came = lax.ppermute(sent, "samp", pairs)
-        held = jnp.stack(
-            [jnp.where(bit == 0, kept, came), jnp.where(bit == 0, came, kept)], axis=1 + step
-        )
-    return held.reshape(n_samp * local, WIDTH)
+def exchange(held, member, n_samp, place, axis):
+    bit = (member >> place) & 1
+    if place:
+        half = held.shape[0] // 2
+        kept = lax.dynamic_slice_in_dim(held, bit * half, half, 0)
+        sent = lax.dynamic_slice_in_dim(held, (1 - bit) * half, half, 0)
+    else:
+        kept = sent = held
+    came = lax.ppermute(sent, "samp", [(i, i ^ (1 << place)) for i in range(n_samp)])
+    return jnp.stack(
+        [jnp.where(bit == 0, kept, came), jnp.where(bit == 0, came, kept)], axis=axis
+    )
 
 
 def body(n_inst, n_samp, prompt_key_values, match, page_list, queries, sample_key_values, gen_len):
@@ -290,30 +317,31 @@
 
     pages = lax.all_to_all(prompt_key_values, "inst", split_axis=1, concat_axis=0, tiled=True)
 
-    sample_keys = sample_key_values[0, :, :, 0, :]
-    sample_values = sample_key_values[0, :, :, 1, :]
-    sample_keys, sent_queries = lax.optimization_barrier((sample_keys, local_queries))
-    head_queries = gather_queries(sent_queries, member, n_samp)
-    live_mask = jnp.arange(sample_keys.shape[1], dtype=jnp.int32)[None, :] < gen_len[0][:, None]
-    own_peak, own_sum, own_numer = partial_own(local_queries, sample_keys, sample_values, live_mask)
-    own_stats = jnp.stack([own_peak.transpose(1, 0, 2), own_sum.transpose(1, 0, 2)], axis=1)
-    own_stats = jnp.pad(own_stats, ((0, 0), (0, 0), (0, 0), (0, 128 - GROUP)))
-    own_numer = own_numer.transpose(1, 2, 0, 3).reshape(
-        KEY_VALUE_HEADS, GROUP * local_total, HEAD_FEATURES
-    )
+    cache = sample_key_values[0]
+    grouped = local_queries.reshape(local_total, KEY_VALUE_HEADS, GROUP, HEAD_FEATURES)
+    grouped = jnp.pad(grouped, ((0, 0), (0, 0), (0, 16 - GROUP), (0, 0)))
+    own = partial_own(gen_len[0], grouped, cache, 0, 2)
+
+    held = local_queries.reshape(local_total, KEY_VALUE_HEADS, WIDTH).transpose(1, 0, 2)
+    held = exchange(held, member, n_samp, 3, 1)
+    held = exchange(held, member, n_samp, 2, 2)
 
     listed = page_list[0].reshape(-1)
     place = (listed % pages_dev) * n_samp + listed // pages_dev
 
     chosen = choose(match, pages).reshape(n_inst * n_samp, half * 2, HEAD_FEATURES)
+    chosen, held, grouped, own = lax.optimization_barrier((chosen, held, grouped, own))
     pairs = lax.all_to_all(chosen, ("inst", "samp"), split_axis=0, concat_axis=0, tiled=True)
-    pairs, place, head_queries, own_stats, own_numer = lax.optimization_barrier(
-        (pairs, place, head_queries, own_stats, own_numer)
-    )
+
+    own = own + partial_own(gen_len[0], grouped, cache, 1, 2)
+    held = exchange(held, member, n_samp, 1, 3)
+    held = exchange(held, member, n_samp, 0, 4)
+    head_queries = held.reshape(n_samp * local_total, WIDTH)
+    pairs, place, head_queries, own = lax.optimization_barrier((pairs, place, head_queries, own))
 
     sent = partial_shared(place, head_queries, pairs, n_samp)
     came = lax.all_to_all(sent, "samp", split_axis=0, concat_axis=0, tiled=True)
-    attended, page_pool = finish(came, own_numer, own_stats, local_total, pages_dev)
+    attended, page_pool = finish(came, own, local_total, pages_dev)
     return (attended[None], page_pool[None])
 
 

time: 131 us -> 116 us (0.89)
  Pallas kernels: 10.3 us -> 32 us
  local copies, waits for them, and re-layouts: 23.3 us -> 4.7 us
  matrix products: 9.87 us -> 0 us
  waiting for transfers between devices: 25.8 us -> 20.3 us
  other arithmetic: 3.42 us -> 0.22 us
    pallas_call x0 -> x2, Pallas kernels: none -> 21.7 us  [partial_own(): pl.pallas_call(functools.partial(own_kernel, which * heads), grid=(1,), o...]
    all_to_all x1, waiting for transfers between devices: 22.1 us -> 10.1 us  [body(): lax.all_to_all(chosen, ('inst', 'samp'), split_axis=0, concat_axis=0, til...]
    dot_general x16 -> x0, matrix products: 9.87 us -> none  [the longest x8 5.32 us: partial_own(): jnp.einsum('sgn,snd->sgd', weights.astype(jnp.bfloat16), value_block, pre...]
    slice x1 -> x0, local copies, waits for them, and re-layouts: 8.81 us -> none  [body(): sample_values = sample_key_values[0, :, :, 1, :]]
    unnamed x30 -> x12, local copies, waits for them, and re-layouts: 8.36 us -> 4.38 us
    ppermute x4, waiting for transfers between devices: 3.75 us -> 7.45 us  [exchange(): lax.ppermute(sent, 'samp', [(i, i ^ 1 << place) for i in range(n_samp)])]
    squeeze x1 -> x0, local copies, waits for them, and re-layouts: 3.06 us -> none  [body(): sample_values = sample_key_values[0, :, :, 1, :]]
    all_to_all x1, waiting for transfers between devices: 0.01 us -> 2.69 us  [body(): lax.all_to_all(prompt_key_values, 'inst', split_axis=1, concat_axis=0, ti...]
  transfers between devices with their start and end apart: 6 -> 6, of which waited for: 3 -> 4; matrix products, arithmetic and copies ran while one was open for 18% -> 0% of each run, Pallas kernels for 2% -> 19%
where the time goes in v4:
time: 116 us; the launch traced here: 115 us
  Pallas kernels  32 us (28%)
  starting transfers between devices  31.3 us (27%)
  blocking collectives  25.9 us (22%)
  waiting for transfers between devices  20.3 us (18%)
  local copies, waits for them, and re-layouts  4.7 us (4%)
    all_to_all x1, blocking collectives, body(): came = lax.all_to_all(sent, 'samp', split_axis=0, concat_axis=0, tiled=True)  25.9 us
    pallas_call x2, Pallas kernels, partial_own(): pl.pallas_call(functools.partial(own_kernel, which * heads), grid=(1,), o...  21.7 us
    all_to_all x1, starting transfers between devices, body(): lax.all_to_all(chosen, ('inst', 'samp'), split_axis=0, concat_axis=0, til...  11.1 us
    all_to_all x1, starting transfers between devices, body(): lax.all_to_all(prompt_key_values, 'inst', split_axis=1, concat_axis=0, ti...  10.3 us
    all_to_all x1, waiting for transfers between devices, body(): lax.all_to_all(chosen, ('inst', 'samp'), split_axis=0, concat_axis=0, til...  10.1 us
    ppermute x4, starting transfers between devices, exchange(): lax.ppermute(sent, 'samp', [(i, i ^ 1 << place) for i in range(n_samp)])  9.9 us
    ppermute x4, waiting for transfers between devices, exchange(): lax.ppermute(sent, 'samp', [(i, i ^ 1 << place) for i in range(n_samp)])  7.45 us
    pallas_call x1, Pallas kernels, partial_shared(): pl.pallas_call(shared_kernel, out_shape=jax.ShapeDtypeStruct((owners, sen...  5.99 us
  transfers between devices with their start and end apart: 6, of which 4 were waited for; matrix products, arithmetic and copies ran while one was open for 0% of the time, Pallas kernels for 19%

profile of v4, /device:TPU:1, one launch (start us, length us, event | category | flops | bytes accessed | tf_op | source)
XLA Modules:
  0.0 115.3 jit_solution(17874908525133446546)
XLA Ops:
  0.6 0.0 copy-start.4
  0.6 0.0 copy-start.2
  0.6 10.3 %all-to-all-start = ((bf16[1,256,2,1024]{3,2,0,1:T(2,128)(2,1)}), bf16[1,256,2,1024]{3,2,0,1:T(2,128)(2,1)S(1)}, u32[]{:S(2)}, u32[]{:S(2)}) async-start(bf16[1,256,2,1024]{3,2,0,1:T(2,128)(2,1)} %bitcast.50), calls=%async_computation | async-start | bytes 2097152 | tf_op jit(solution)/shard_map/all_to_all | solution.py:318
  10.9 0.0 copy-done.4
  11.0 2.7 %collective-permute-start = (bf16[4,8,1536]{2,1,0:T(8,128)(2,1)S(1)}, bf16[4,8,1536]{2,1,0:T(8,128)(2,1)S(1)}, u32[]{:S(2)}, u32[]{:S(2)}) collective-permute-start(bf16[4,8,1536]{2,1,0:T(8,128)(2,1)S(1)} %dynamic-slice_bitcast_fusion), channel_id=1, source_target_pairs={{0,8},{1,9},{2,10},{3,11},{4,12},{5,13},{6,14},{7,15},{8,0},{9,1},... | collective-permute-start | bytes 294920 | tf_op jit(solution)/shard_map/ppermute | solution.py:305
  13.7 4.0 %collective-permute-done = bf16[4,8,1536]{2,1,0:T(8,128)(2,1)S(1)} collective-permute-done((bf16[4,8,1536]{2,1,0:T(8,128)(2,1)S(1)}, bf16[4,8,1536]{2,1,0:T(8,128)(2,1)S(1)}, u32[]{:S(2)}, u32[]{:S(2)}) %collective-permute-start) | collective-permute-done | bytes 98336 | tf_op jit(solution)/shard_map/ppermute | solution.py:305
  17.7 2.8 %collective-permute-start.1 = (bf16[2,2,8,1536]{3,2,1,0:T(8,128)(2,1)S(1)}, bf16[2,2,8,1536]{3,2,1,0:T(8,128)(2,1)S(1)}, u32[]{:S(2)}, u32[]{:S(2)}) collective-permute-start(bf16[2,2,8,1536]{3,2,1,0:T(8,128)(2,1)S(1)} %fusion), channel_id=1, source_target_pairs={{0,4},{1,5},{2,6},{3,7},{4,0},{5,1},{6,2},{7,3},{8,12},{9,13},{10,... | collective-permute-start | bytes 294920 | tf_op jit(solution)/shard_map/ppermute | solution.py:305
  20.6 0.2 reshape_squeeze.10
  20.7 0.1 pad.4.query_ref
  20.8 0.0 copy-done.2
  20.8 0.0 copy-start
  20.8 2.2 %copy-done = bf16[1,8,128,2,1024]{4,3,2,1,0:T(2,128)(2,1)S(1)} copy-done((bf16[1,8,128,2,1024]{4,3,2,1,0:T(2,128)(2,1)S(1)}, bf16[1,8,128,2,1024]{4,3,2,1,0:T(2,128)(2,1)}, u32[]{:S(2)}) %copy-start) | copy-done | bytes 4194328
  23.0 0.0 copy-start.3
  23.0 10.9 %shard_map.78 = (f32[4,12,8,128]{3,2,1,0:T(8,128)S(1)}, f32[4,2,8,128]{3,2,1,0:T(8,128)S(1)}) custom-call(s32[8]{0:T(128)S(1)} %bitcast.48, bf16[8,8,16,128]{3,2,1,0:T(8,128)(2,1)S(1)} %pad.4.query_ref, bf16[8,128,2,1024]{3,2,1,0:T(2,128)(2,1)S(1)} %bitcast.43), custom_call_target="tpu_custom_call" | custom-call | bytes 65536 | tf_op jit(solution)/shard_map/pallas_call | solution.py:60
  33.9 0.0 collective-permute-done.1
  33.9 2.7 %all-to-all-done = bf16[1,256,2,1024]{3,2,0,1:T(2,128)(2,1)S(1)} async-done(((bf16[1,256,2,1024]{3,2,0,1:T(2,128)(2,1)}), bf16[1,256,2,1024]{3,2,0,1:T(2,128)(2,1)S(1)}, u32[]{:S(2)}, u32[]{:S(2)}) %all-to-all-start) | async-done | bytes 1048608 | tf_op jit(solution)/shard_map/all_to_all | solution.py:318
  36.6 0.0 copy-done.3
  36.6 2.1 %shard_map.77 = bf16[16,8,16,2,128]{4,3,2,1,0:T(2,128)(2,1)} custom-call(s32[16]{0:T(128)S(1)} %copy-done.3, bf16[16,16,2,1024]{3,2,1,0:T(2,128)(2,1)S(1)} %bitcast.46), custom_call_target="tpu_custom_call" | custom-call | bytes 4194304 | tf_op jit(solution)/shard_map/pallas_call | solution.py:280
  38.7 0.0 copy-start.5
  38.7 11.1 %all-to-all-start.1 = ((bf16[256,16,128]{2,1,0:T(8,128)(2,1)}), bf16[256,16,128]{2,1,0:T(8,128)(2,1)S(1)}, u32[]{:S(2)}, u32[]{:S(2)}) async-start(bf16[256,16,128]{2,1,0:T(8,128)(2,1)} %bitcast.2), calls=%async_computation.1 | async-start | bytes 2097152 | tf_op jit(solution)/shard_map/all_to_all | solution.py:334
  49.9 1.5 %collective-permute-start.2 = (bf16[1,2,2,8,1536]{4,3,2,1,0:T(8,128)(2,1)S(1)}, bf16[1,2,2,8,1536]{4,3,2,1,0:T(8,128)(2,1)S(1)}, u32[]{:S(2)}, u32[]{:S(2)}) collective-permute-start(bf16[1,2,2,8,1536]{4,3,2,1,0:T(8,128)(2,1)S(1)} %constant_dynamic-slice_fusion), channel_id=1, source_target_pairs={{0,2},{1,3},{2,0},{3,1},{4,6},{5,7},{6,4},{7,5},{8,10},{9,11},{10,... | collective-permute-start | bytes 294920 | tf_op jit(solution)/shard_map/ppermute | solution.py:305
  51.4 0.0 copy-done.5
  51.4 0.1 reshape_squeeze.11
  51.4 3.4 %collective-permute-done.2 = bf16[1,2,2,8,1536]{4,3,2,1,0:T(8,128)(2,1)S(1)} collective-permute-done((bf16[1,2,2,8,1536]{4,3,2,1,0:T(8,128)(2,1)S(1)}, bf16[1,2,2,8,1536]{4,3,2,1,0:T(8,128)(2,1)S(1)}, u32[]{:S(2)}, u32[]{:S(2)}) %collective-permute-start.2) | collective-permute-done | bytes 98336 | tf_op jit(solution)/shard_map/ppermute | solution.py:305
  54.9 2.9 %collective-permute-start.3 = (bf16[1,2,2,2,8,1536]{5,4,3,2,1,0:T(8,128)(2,1)S(1)}, bf16[1,2,2,2,8,1536]{5,4,3,2,1,0:T(8,128)(2,1)S(1)}, u32[]{:S(2)}, u32[]{:S(2)}) collective-permute-start(bf16[1,2,2,2,8,1536]{5,4,3,2,1,0:T(8,128)(2,1)S(1)} %pad_maximum_fusion.2), channel_id=1, source_target_pairs={{0,1},{1,0},{2,3},{3,2},{4,5},{5,4},{6,7},{7,6},{8,9},{9,8},{10,11... | collective-permute-start | bytes 589832 | tf_op jit(solution)/shard_map/ppermute | solution.py:305
  57.8 0.0 copy-start.1
  57.8 2.2 %copy-done.1 = bf16[1,8,128,2,1024]{4,3,2,1,0:T(2,128)(2,1)S(1)} copy-done((bf16[1,8,128,2,1024]{4,3,2,1,0:T(2,128)(2,1)S(1)}, bf16[1,8,128,2,1024]{4,3,2,1,0:T(2,128)(2,1)}, u32[]{:S(2)}) %copy-start.1) | copy-done | bytes 4194328
  60.0 10.9 %shard_map.79 = (f32[4,12,8,128]{3,2,1,0:T(8,128)S(1)}, f32[4,2,8,128]{3,2,1,0:T(8,128)S(1)}) custom-call(s32[8]{0:T(128)S(1)} %bitcast.49, bf16[8,8,16,128]{3,2,1,0:T(8,128)(2,1)S(1)} %pad.4.query_ref, bf16[8,128,2,1024]{3,2,1,0:T(2,128)(2,1)S(1)} %bitcast.44), custom_call_target="tpu_custom_call" | custom-call | bytes 65536 | tf_op jit(solution)/shard_map/pallas_call | solution.py:60
  70.9 0.0 collective-permute-done.3
  71.0 10.1 %all-to-all-done.1.pair_ref = bf16[256,16,128]{2,1,0:T(8,128)(2,1)S(1)} async-done(((bf16[256,16,128]{2,1,0:T(8,128)(2,1)}), bf16[256,16,128]{2,1,0:T(8,128)(2,1)S(1)}, u32[]{:S(2)}, u32[]{:S(2)}) %all-to-all-start.1) | async-done | bytes 1048608 | tf_op jit(solution)/shard_map/all_to_all | solution.py:334
  81.1 6.0 %shard_map.80 = bf16[16,368,128]{2,1,0:T(8,128)(2,1)S(1)} custom-call(s32[256]{0:T(256)S(1)} %fusion.5.place_ref, bf16[128,1536]{1,0:T(8,128)(2,1)S(1)} %bitcast.47, bf16[256,16,128]{2,1,0:T(8,128)(2,1)S(1)} %all-to-all-done.1.pair_ref), custom_call_target="tpu_custom_call" | custom-call | flops 1610612736 | bytes 4194304 | tf_op jit(solution)/shard_map/pallas_call | solution.py:157
  87.1 25.9 %all_to_all.22.came_ref = bf16[16,368,128]{2,1,0:T(8,128)(2,1)S(1)} all-to-all(bf16[16,368,128]{2,1,0:T(8,128)(2,1)S(1)} %shard_map.80), channel_id=1, replica_groups=mesh['inst'=16,'samp'=16] {'samp'}, dimensions={0} | all-to-all | bytes 3014656 | tf_op jit(solution)/shard_map/all_to_all | solution.py:343
  113.0 2.2 %shard_map.81 = (bf16[8,12288]{1,0:T(8,128)(2,1)}, bf16[16,16,2,1024]{3,2,1,0:T(2,128)(2,1)}) custom-call(bf16[16,23,8,2,128]{4,3,2,1,0:T(2,128)(2,1)S(1)} %bitcast.45, bf16[16,368,128]{2,1,0:T(8,128)(2,1)S(1)} %all_to_all.22.came_ref, f32[4,12,8,128]{3,2,1,0:T(8,128)S(1)} %get-tuple-element.32.refs_0_, f32[4,2,8,128]{3,2,1,0:T(8,128)S(1)} %get-tuple-element.33.refs_1_, ...), custom_call_target="tpu_custom_call" | custom-call | flops 589824 | bytes 4194304 | tf_op jit(solution)/shard_map/pallas_call | solution.py:246
  (11 shorter events, 0.2 us)
Async XLA Ops:
  0.6 10.3 %copy-start.4 = (bf16[1,8,12288]{2,1,0:T(8,128)(2,1)S(1)}, bf16[1,8,12288]{2,1,0:T(8,128)(2,1)}, u32[]{:S(2)}) copy-start(bf16[1,8,12288]{2,1,0:T(8,128)(2,1)} %param.9) | copy-start | bytes 589828
  0.6 20.1 %copy-start.2 = (s32[1,8]{1,0:T(1,128)S(1)}, s32[1,8]{1,0:T(1,128)}, u32[]{:S(2)}) copy-start(s32[1,8]{1,0:T(1,128)} %param.11) | copy-start | bytes 100
  0.6 36.0 %all-to-all-start = ((bf16[1,256,2,1024]{3,2,0,1:T(2,128)(2,1)}), bf16[1,256,2,1024]{3,2,0,1:T(2,128)(2,1)S(1)}, u32[]{:S(2)}, u32[]{:S(2)}) async-start(bf16[1,256,2,1024]{3,2,0,1:T(2,128)(2,1)} %bitcast.50), calls=%async_computation | async-start | bytes 2097152 | tf_op jit(solution)/shard_map/all_to_all | solution.py:318
  11.0 6.7 %collective-permute-start = (bf16[4,8,1536]{2,1,0:T(8,128)(2,1)S(1)}, bf16[4,8,1536]{2,1,0:T(8,128)(2,1)S(1)}, u32[]{:S(2)}, u32[]{:S(2)}) collective-permute-start(bf16[4,8,1536]{2,1,0:T(8,128)(2,1)S(1)} %dynamic-slice_bitcast_fusion), channel_id=1, source_target_pairs={{0,8},{1,9},{2,10},{3,11},{4,12},{5,13},{6,14},{7,15},{8,0},{9,1},... | collective-permute-start | bytes 294920 | tf_op jit(solution)/shard_map/ppermute | solution.py:305
  17.7 16.1 %collective-permute-start.1 = (bf16[2,2,8,1536]{3,2,1,0:T(8,128)(2,1)S(1)}, bf16[2,2,8,1536]{3,2,1,0:T(8,128)(2,1)S(1)}, u32[]{:S(2)}, u32[]{:S(2)}) collective-permute-start(bf16[2,2,8,1536]{3,2,1,0:T(8,128)(2,1)S(1)} %fusion), channel_id=1, source_target_pairs={{0,4},{1,5},{2,6},{3,7},{4,0},{5,1},{6,2},{7,3},{8,12},{9,13},{10,... | collective-permute-start | bytes 294920 | tf_op jit(solution)/shard_map/ppermute | solution.py:305
  20.8 2.2 %copy-start = (bf16[1,8,128,2,1024]{4,3,2,1,0:T(2,128)(2,1)S(1)}, bf16[1,8,128,2,1024]{4,3,2,1,0:T(2,128)(2,1)}, u32[]{:S(2)}) copy-start(bf16[1,8,128,2,1024]{4,3,2,1,0:T(2,128)(2,1)} %param.10) | copy-start | bytes 12582916
  23.0 13.6 %copy-start.3 = (s32[16]{0:T(128)S(1)}, s32[16]{0:T(128)}, u32[]{:S(2)}) copy-start(s32[16]{0:T(128)} %match_ref.1) | copy-start | bytes 196
  38.7 12.6 %copy-start.5 = (s32[1,16,16]{2,1,0:T(8,128)S(1)}, s32[1,16,16]{2,1,0:T(8,128)}, u32[]{:S(2)}) copy-start(s32[1,16,16]{2,1,0:T(8,128)} %param.8) | copy-start | bytes 3076
  38.7 42.4 %all-to-all-start.1 = ((bf16[256,16,128]{2,1,0:T(8,128)(2,1)}), bf16[256,16,128]{2,1,0:T(8,128)(2,1)S(1)}, u32[]{:S(2)}, u32[]{:S(2)}) async-start(bf16[256,16,128]{2,1,0:T(8,128)(2,1)} %bitcast.2), calls=%async_computation.1 | async-start | bytes 2097152 | tf_op jit(solution)/shard_map/all_to_all | solution.py:334
  49.9 5.0 %collective-permute-start.2 = (bf16[1,2,2,8,1536]{4,3,2,1,0:T(8,128)(2,1)S(1)}, bf16[1,2,2,8,1536]{4,3,2,1,0:T(8,128)(2,1)S(1)}, u32[]{:S(2)}, u32[]{:S(2)}) collective-permute-start(bf16[1,2,2,8,1536]{4,3,2,1,0:T(8,128)(2,1)S(1)} %constant_dynamic-slice_fusion), channel_id=1, source_target_pairs={{0,2},{1,3},{2,0},{3,1},{4,6},{5,7},{6,4},{7,5},{8,10},{9,11},{10,... | collective-permute-start | bytes 294920 | tf_op jit(solution)/shard_map/ppermute | solution.py:305
  54.9 16.0 %collective-permute-start.3 = (bf16[1,2,2,2,8,1536]{5,4,3,2,1,0:T(8,128)(2,1)S(1)}, bf16[1,2,2,2,8,1536]{5,4,3,2,1,0:T(8,128)(2,1)S(1)}, u32[]{:S(2)}, u32[]{:S(2)}) collective-permute-start(bf16[1,2,2,2,8,1536]{5,4,3,2,1,0:T(8,128)(2,1)S(1)} %pad_maximum_fusion.2), channel_id=1, source_target_pairs={{0,1},{1,0},{2,3},{3,2},{4,5},{5,4},{6,7},{7,6},{8,9},{9,8},{10,11... | collective-permute-start | bytes 589832 | tf_op jit(solution)/shard_map/ppermute | solution.py:305
  57.8 2.2 %copy-start.1 = (bf16[1,8,128,2,1024]{4,3,2,1,0:T(2,128)(2,1)S(1)}, bf16[1,8,128,2,1024]{4,3,2,1,0:T(2,128)(2,1)}, u32[]{:S(2)}) copy-start(bf16[1,8,128,2,1024]{4,3,2,1,0:T(2,128)(2,1)} %param.10) | copy-start | bytes 12582916

commit v5 on v4

--- a/solution.py
+++ b/solution.py
@@ -116,7 +116,7 @@
         high = high.reshape(owners, local, HEAD_FEATURES)
         return jnp.concatenate([low, high], axis=1).astype(jnp.bfloat16)
 
-    for g in range(0, GROUP, 2):
+    def scores_of(g):
         query = jnp.concatenate(
             [
                 query_ref[:, g * HEAD_FEATURES : (g + 1) * HEAD_FEATURES],
@@ -124,9 +124,15 @@
             ],
             axis=0,
         )
-        scores = lax.dot_general(
+        return lax.dot_general(
             query, key_ref[...], (((1,), (1,)), ((), ())), preferred_element_type=jnp.float32
         )
+
+    later = scores_of(0)
+    for g in range(0, GROUP, 2):
+        scores = later
+        if g + 2 < GROUP:
+            later = scores_of(g + 2)
         top = jnp.max(scores, axis=-1, keepdims=True)
         weights = jnp.exp2((scores - top) * factor)
         total = jnp.sum(weights, axis=-1, keepdims=True)

time: 116 us -> 115 us (level)
  no operation moved by 1% of the time
where the time goes in v5:
time: 115 us; the launch traced here: 114 us
  Pallas kernels  31.2 us (27%)
  starting transfers between devices  31.1 us (27%)
  blocking collectives  25.9 us (23%)
  waiting for transfers between devices  20.4 us (18%)
  local copies, waits for them, and re-layouts  4.7 us (4%)
    all_to_all x1, blocking collectives, body(): came = lax.all_to_all(sent, 'samp', split_axis=0, concat_axis=0, tiled=True)  25.9 us
    pallas_call x2, Pallas kernels, partial_own(): pl.pallas_call(functools.partial(own_kernel, which * heads), grid=(1,), o...  21.7 us
    all_to_all x1, starting transfers between devices, body(): lax.all_to_all(chosen, ('inst', 'samp'), split_axis=0, concat_axis=0, til...  11.1 us
    all_to_all x1, waiting for transfers between devices, body(): lax.all_to_all(chosen, ('inst', 'samp'), split_axis=0, concat_axis=0, til...  10.3 us
    all_to_all x1, starting transfers between devices, body(): lax.all_to_all(prompt_key_values, 'inst', split_axis=1, concat_axis=0, ti...  10.3 us
    ppermute x4, starting transfers between devices, exchange(): lax.ppermute(sent, 'samp', [(i, i ^ 1 << place) for i in range(n_samp)])  9.71 us
    ppermute x4, waiting for transfers between devices, exchange(): lax.ppermute(sent, 'samp', [(i, i ^ 1 << place) for i in range(n_samp)])  7.45 us
    pallas_call x1, Pallas kernels, partial_shared(): pl.pallas_call(shared_kernel, out_shape=jax.ShapeDtypeStruct((owners, sen...  5.17 us
  transfers between devices with their start and end apart: 6, of which 4 were waited for; matrix products, arithmetic and copies ran while one was open for 0% of the time, Pallas kernels for 19%

profile of v5, /device:TPU:1, one launch (start us, length us, event | category | flops | bytes accessed | tf_op | source)
XLA Modules:
  0.0 114.4 jit_solution(15366680335158450388)
XLA Ops:
  0.6 0.0 copy-start.4
  0.6 0.0 copy-start.2
  0.6 10.3 %all-to-all-start = ((bf16[1,256,2,1024]{3,2,0,1:T(2,128)(2,1)}), bf16[1,256,2,1024]{3,2,0,1:T(2,128)(2,1)S(1)}, u32[]{:S(2)}, u32[]{:S(2)}) async-start(bf16[1,256,2,1024]{3,2,0,1:T(2,128)(2,1)} %bitcast.50), calls=%async_computation | async-start | bytes 2097152 | tf_op jit(solution)/shard_map/all_to_all | solution.py:324
  10.9 0.0 copy-done.4
  11.0 2.7 %collective-permute-start = (bf16[4,8,1536]{2,1,0:T(8,128)(2,1)S(1)}, bf16[4,8,1536]{2,1,0:T(8,128)(2,1)S(1)}, u32[]{:S(2)}, u32[]{:S(2)}) collective-permute-start(bf16[4,8,1536]{2,1,0:T(8,128)(2,1)S(1)} %dynamic-slice_bitcast_fusion), channel_id=1, source_target_pairs={{0,8},{1,9},{2,10},{3,11},{4,12},{5,13},{6,14},{7,15},{8,0},{9,1},... | collective-permute-start | bytes 294920 | tf_op jit(solution)/shard_map/ppermute | solution.py:311
  13.7 4.0 %collective-permute-done = bf16[4,8,1536]{2,1,0:T(8,128)(2,1)S(1)} collective-permute-done((bf16[4,8,1536]{2,1,0:T(8,128)(2,1)S(1)}, bf16[4,8,1536]{2,1,0:T(8,128)(2,1)S(1)}, u32[]{:S(2)}, u32[]{:S(2)}) %collective-permute-start) | collective-permute-done | bytes 98336 | tf_op jit(solution)/shard_map/ppermute | solution.py:311
  17.7 2.8 %collective-permute-start.1 = (bf16[2,2,8,1536]{3,2,1,0:T(8,128)(2,1)S(1)}, bf16[2,2,8,1536]{3,2,1,0:T(8,128)(2,1)S(1)}, u32[]{:S(2)}, u32[]{:S(2)}) collective-permute-start(bf16[2,2,8,1536]{3,2,1,0:T(8,128)(2,1)S(1)} %fusion), channel_id=1, source_target_pairs={{0,4},{1,5},{2,6},{3,7},{4,0},{5,1},{6,2},{7,3},{8,12},{9,13},{10,... | collective-permute-start | bytes 294920 | tf_op jit(solution)/shard_map/ppermute | solution.py:311
  20.6 0.2 reshape_squeeze.10
  20.7 0.1 pad.4.query_ref
  20.8 0.0 copy-done.2
  20.8 0.0 copy-start
  20.8 2.2 %copy-done = bf16[1,8,128,2,1024]{4,3,2,1,0:T(2,128)(2,1)S(1)} copy-done((bf16[1,8,128,2,1024]{4,3,2,1,0:T(2,128)(2,1)S(1)}, bf16[1,8,128,2,1024]{4,3,2,1,0:T(2,128)(2,1)}, u32[]{:S(2)}) %copy-start) | copy-done | bytes 4194328
  23.0 0.0 copy-start.3
  23.0 10.9 %shard_map.78 = (f32[4,12,8,128]{3,2,1,0:T(8,128)S(1)}, f32[4,2,8,128]{3,2,1,0:T(8,128)S(1)}) custom-call(s32[8]{0:T(128)S(1)} %bitcast.48, bf16[8,8,16,128]{3,2,1,0:T(8,128)(2,1)S(1)} %pad.4.query_ref, bf16[8,128,2,1024]{3,2,1,0:T(2,128)(2,1)S(1)} %bitcast.43), custom_call_target="tpu_custom_call" | custom-call | bytes 65536 | tf_op jit(solution)/shard_map/pallas_call | solution.py:60
  33.9 0.0 collective-permute-done.1
  33.9 2.7 %all-to-all-done = bf16[1,256,2,1024]{3,2,0,1:T(2,128)(2,1)S(1)} async-done(((bf16[1,256,2,1024]{3,2,0,1:T(2,128)(2,1)}), bf16[1,256,2,1024]{3,2,0,1:T(2,128)(2,1)S(1)}, u32[]{:S(2)}, u32[]{:S(2)}) %all-to-all-start) | async-done | bytes 1048608 | tf_op jit(solution)/shard_map/all_to_all | solution.py:324
  36.6 0.0 copy-done.3
  36.6 2.1 %shard_map.77 = bf16[16,8,16,2,128]{4,3,2,1,0:T(2,128)(2,1)} custom-call(s32[16]{0:T(128)S(1)} %copy-done.3, bf16[16,16,2,1024]{3,2,1,0:T(2,128)(2,1)S(1)} %bitcast.46), custom_call_target="tpu_custom_call" | custom-call | bytes 4194304 | tf_op jit(solution)/shard_map/pallas_call | solution.py:286
  38.7 0.0 copy-start.5
  38.7 11.1 %all-to-all-start.1 = ((bf16[256,16,128]{2,1,0:T(8,128)(2,1)}), bf16[256,16,128]{2,1,0:T(8,128)(2,1)S(1)}, u32[]{:S(2)}, u32[]{:S(2)}) async-start(bf16[256,16,128]{2,1,0:T(8,128)(2,1)} %bitcast.2), calls=%async_computation.1 | async-start | bytes 2097152 | tf_op jit(solution)/shard_map/all_to_all | solution.py:340
  49.9 1.5 %collective-permute-start.2 = (bf16[1,2,2,8,1536]{4,3,2,1,0:T(8,128)(2,1)S(1)}, bf16[1,2,2,8,1536]{4,3,2,1,0:T(8,128)(2,1)S(1)}, u32[]{:S(2)}, u32[]{:S(2)}) collective-permute-start(bf16[1,2,2,8,1536]{4,3,2,1,0:T(8,128)(2,1)S(1)} %constant_dynamic-slice_fusion), channel_id=1, source_target_pairs={{0,2},{1,3},{2,0},{3,1},{4,6},{5,7},{6,4},{7,5},{8,10},{9,11},{10,... | collective-permute-start | bytes 294920 | tf_op jit(solution)/shard_map/ppermute | solution.py:311
  51.4 0.0 copy-done.5
  51.4 0.1 reshape_squeeze.11
  51.4 3.4 %collective-permute-done.2 = bf16[1,2,2,8,1536]{4,3,2,1,0:T(8,128)(2,1)S(1)} collective-permute-done((bf16[1,2,2,8,1536]{4,3,2,1,0:T(8,128)(2,1)S(1)}, bf16[1,2,2,8,1536]{4,3,2,1,0:T(8,128)(2,1)S(1)}, u32[]{:S(2)}, u32[]{:S(2)}) %collective-permute-start.2) | collective-permute-done | bytes 98336 | tf_op jit(solution)/shard_map/ppermute | solution.py:311
  54.9 2.7 %collective-permute-start.3 = (bf16[1,2,2,2,8,1536]{5,4,3,2,1,0:T(8,128)(2,1)S(1)}, bf16[1,2,2,2,8,1536]{5,4,3,2,1,0:T(8,128)(2,1)S(1)}, u32[]{:S(2)}, u32[]{:S(2)}) collective-permute-start(bf16[1,2,2,2,8,1536]{5,4,3,2,1,0:T(8,128)(2,1)S(1)} %pad_maximum_fusion.2), channel_id=1, source_target_pairs={{0,1},{1,0},{2,3},{3,2},{4,5},{5,4},{6,7},{7,6},{8,9},{9,8},{10,11... | collective-permute-start | bytes 589832 | tf_op jit(solution)/shard_map/ppermute | solution.py:311
  57.7 0.0 copy-start.1
  57.7 2.2 %copy-done.1 = bf16[1,8,128,2,1024]{4,3,2,1,0:T(2,128)(2,1)S(1)} copy-done((bf16[1,8,128,2,1024]{4,3,2,1,0:T(2,128)(2,1)S(1)}, bf16[1,8,128,2,1024]{4,3,2,1,0:T(2,128)(2,1)}, u32[]{:S(2)}) %copy-start.1) | copy-done | bytes 4194328
  59.8 10.9 %shard_map.79 = (f32[4,12,8,128]{3,2,1,0:T(8,128)S(1)}, f32[4,2,8,128]{3,2,1,0:T(8,128)S(1)}) custom-call(s32[8]{0:T(128)S(1)} %bitcast.49, bf16[8,8,16,128]{3,2,1,0:T(8,128)(2,1)S(1)} %pad.4.query_ref, bf16[8,128,2,1024]{3,2,1,0:T(2,128)(2,1)S(1)} %bitcast.44), custom_call_target="tpu_custom_call" | custom-call | bytes 65536 | tf_op jit(solution)/shard_map/pallas_call | solution.py:60
  70.7 0.0 collective-permute-done.3
  70.8 10.3 %all-to-all-done.1.pair_ref = bf16[256,16,128]{2,1,0:T(8,128)(2,1)S(1)} async-done(((bf16[256,16,128]{2,1,0:T(8,128)(2,1)}), bf16[256,16,128]{2,1,0:T(8,128)(2,1)S(1)}, u32[]{:S(2)}, u32[]{:S(2)}) %all-to-all-start.1) | async-done | bytes 1048608 | tf_op jit(solution)/shard_map/all_to_all | solution.py:340
  81.1 5.2 %shard_map.80 = bf16[16,368,128]{2,1,0:T(8,128)(2,1)S(1)} custom-call(s32[256]{0:T(256)S(1)} %fusion.5.place_ref, bf16[128,1536]{1,0:T(8,128)(2,1)S(1)} %bitcast.47, bf16[256,16,128]{2,1,0:T(8,128)(2,1)S(1)} %all-to-all-done.1.pair_ref), custom_call_target="tpu_custom_call" | custom-call | flops 1610612736 | bytes 4194304 | tf_op jit(solution)/shard_map/pallas_call | solution.py:163
  86.3 25.9 %all_to_all.22.came_ref = bf16[16,368,128]{2,1,0:T(8,128)(2,1)S(1)} all-to-all(bf16[16,368,128]{2,1,0:T(8,128)(2,1)S(1)} %shard_map.80), channel_id=1, replica_groups=mesh['inst'=16,'samp'=16] {'samp'}, dimensions={0} | all-to-all | bytes 3014656 | tf_op jit(solution)/shard_map/all_to_all | solution.py:349
  112.2 2.2 %shard_map.81 = (bf16[8,12288]{1,0:T(8,128)(2,1)}, bf16[16,16,2,1024]{3,2,1,0:T(2,128)(2,1)}) custom-call(bf16[16,23,8,2,128]{4,3,2,1,0:T(2,128)(2,1)S(1)} %bitcast.45, bf16[16,368,128]{2,1,0:T(8,128)(2,1)S(1)} %all_to_all.22.came_ref, f32[4,12,8,128]{3,2,1,0:T(8,128)S(1)} %get-tuple-element.32.refs_0_, f32[4,2,8,128]{3,2,1,0:T(8,128)S(1)} %get-tuple-element.33.refs_1_, ...), custom_call_target="tpu_custom_call" | custom-call | flops 589824 | bytes 4194304 | tf_op jit(solution)/shard_map/pallas_call | solution.py:252
  (11 shorter events, 0.2 us)
Async XLA Ops:
  0.6 10.3 %copy-start.4 = (bf16[1,8,12288]{2,1,0:T(8,128)(2,1)S(1)}, bf16[1,8,12288]{2,1,0:T(8,128)(2,1)}, u32[]{:S(2)}) copy-start(bf16[1,8,12288]{2,1,0:T(8,128)(2,1)} %param.9) | copy-start | bytes 589828
  0.6 20.1 %copy-start.2 = (s32[1,8]{1,0:T(1,128)S(1)}, s32[1,8]{1,0:T(1,128)}, u32[]{:S(2)}) copy-start(s32[1,8]{1,0:T(1,128)} %param.11) | copy-start | bytes 100
  0.6 36.0 %all-to-all-start = ((bf16[1,256,2,1024]{3,2,0,1:T(2,128)(2,1)}), bf16[1,256,2,1024]{3,2,0,1:T(2,128)(2,1)S(1)}, u32[]{:S(2)}, u32[]{:S(2)}) async-start(bf16[1,256,2,1024]{3,2,0,1:T(2,128)(2,1)} %bitcast.50), calls=%async_computation | async-start | bytes 2097152 | tf_op jit(solution)/shard_map/all_to_all | solution.py:324
  11.0 6.7 %collective-permute-start = (bf16[4,8,1536]{2,1,0:T(8,128)(2,1)S(1)}, bf16[4,8,1536]{2,1,0:T(8,128)(2,1)S(1)}, u32[]{:S(2)}, u32[]{:S(2)}) collective-permute-start(bf16[4,8,1536]{2,1,0:T(8,128)(2,1)S(1)} %dynamic-slice_bitcast_fusion), channel_id=1, source_target_pairs={{0,8},{1,9},{2,10},{3,11},{4,12},{5,13},{6,14},{7,15},{8,0},{9,1},... | collective-permute-start | bytes 294920 | tf_op jit(solution)/shard_map/ppermute | solution.py:311
  17.7 16.1 %collective-permute-start.1 = (bf16[2,2,8,1536]{3,2,1,0:T(8,128)(2,1)S(1)}, bf16[2,2,8,1536]{3,2,1,0:T(8,128)(2,1)S(1)}, u32[]{:S(2)}, u32[]{:S(2)}) collective-permute-start(bf16[2,2,8,1536]{3,2,1,0:T(8,128)(2,1)S(1)} %fusion), channel_id=1, source_target_pairs={{0,4},{1,5},{2,6},{3,7},{4,0},{5,1},{6,2},{7,3},{8,12},{9,13},{10,... | collective-permute-start | bytes 294920 | tf_op jit(solution)/shard_map/ppermute | solution.py:311
  20.8 2.2 %copy-start = (bf16[1,8,128,2,1024]{4,3,2,1,0:T(2,128)(2,1)S(1)}, bf16[1,8,128,2,1024]{4,3,2,1,0:T(2,128)(2,1)}, u32[]{:S(2)}) copy-start(bf16[1,8,128,2,1024]{4,3,2,1,0:T(2,128)(2,1)} %param.10) | copy-start | bytes 12582916
  23.0 13.6 %copy-start.3 = (s32[16]{0:T(128)S(1)}, s32[16]{0:T(128)}, u32[]{:S(2)}) copy-start(s32[16]{0:T(128)} %match_ref.1) | copy-start | bytes 196
  38.7 12.6 %copy-start.5 = (s32[1,16,16]{2,1,0:T(8,128)S(1)}, s32[1,16,16]{2,1,0:T(8,128)}, u32[]{:S(2)}) copy-start(s32[1,16,16]{2,1,0:T(8,128)} %param.8) | copy-start | bytes 3076
  38.7 42.4 %all-to-all-start.1 = ((bf16[256,16,128]{2,1,0:T(8,128)(2,1)}), bf16[256,16,128]{2,1,0:T(8,128)(2,1)S(1)}, u32[]{:S(2)}, u32[]{:S(2)}) async-start(bf16[256,16,128]{2,1,0:T(8,128)(2,1)} %bitcast.2), calls=%async_computation.1 | async-start | bytes 2097152 | tf_op jit(solution)/shard_map/all_to_all | solution.py:340
  49.9 5.0 %collective-permute-start.2 = (bf16[1,2,2,8,1536]{4,3,2,1,0:T(8,128)(2,1)S(1)}, bf16[1,2,2,8,1536]{4,3,2,1,0:T(8,128)(2,1)S(1)}, u32[]{:S(2)}, u32[]{:S(2)}) collective-permute-start(bf16[1,2,2,8,1536]{4,3,2,1,0:T(8,128)(2,1)S(1)} %constant_dynamic-slice_fusion), channel_id=1, source_target_pairs={{0,2},{1,3},{2,0},{3,1},{4,6},{5,7},{6,4},{7,5},{8,10},{9,11},{10,... | collective-permute-start | bytes 294920 | tf_op jit(solution)/shard_map/ppermute | solution.py:311
  54.9 15.8 %collective-permute-start.3 = (bf16[1,2,2,2,8,1536]{5,4,3,2,1,0:T(8,128)(2,1)S(1)}, bf16[1,2,2,2,8,1536]{5,4,3,2,1,0:T(8,128)(2,1)S(1)}, u32[]{:S(2)}, u32[]{:S(2)}) collective-permute-start(bf16[1,2,2,2,8,1536]{5,4,3,2,1,0:T(8,128)(2,1)S(1)} %pad_maximum_fusion.2), channel_id=1, source_target_pairs={{0,1},{1,0},{2,3},{3,2},{4,5},{5,4},{6,7},{7,6},{8,9},{9,8},{10,11... | collective-permute-start | bytes 589832 | tf_op jit(solution)/shard_map/ppermute | solution.py:311
  57.7 2.2 %copy-start.1 = (bf16[1,8,128,2,1024]{4,3,2,1,0:T(2,128)(2,1)S(1)}, bf16[1,8,128,2,1024]{4,3,2,1,0:T(2,128)(2,1)}, u32[]{:S(2)}) copy-start(bf16[1,8,128,2,1024]{4,3,2,1,0:T(2,128)(2,1)} %param.10) | copy-start | bytes 12582916

commit v6 on v5

--- a/solution.py
+++ b/solution.py
@@ -211,21 +211,27 @@
     def back(x, places):
         return pltpu.roll(x, 128 - places, 1)
 
+    heads = own_refs[0].shape[0]
+    stacked = [
+        jnp.concatenate([ref[...].reshape(heads, 2, local, 128)[:, i] for ref in own_refs[1::2]])
+        for i in range(2)
+    ]
+    peaks = [stacked[0].reshape(-1, 128)]
+    sums = [stacked[1].reshape(-1, 128)]
+    for part in range(2):
+        terms = came_ref[part::2, first : first + 2 * local, :].astype(jnp.float32)
+        terms = terms[:, :local].reshape(-1, 128)
+        terms = (terms + back(terms, GROUP)) + back(terms, 2 * GROUP)
+        peaks.append(terms)
+        sums.append(back(terms, 3 * GROUP))
+    peak = jnp.maximum(jnp.maximum(peaks[0], peaks[1]), peaks[2])
+    scales = [jnp.exp(p - peak) for p in peaks]
+    total = (sums[0] * scales[0] + sums[1] * scales[1]) + sums[2] * scales[2]
+    scales = [s / total for s in scales]
+
     for head in range(KEY_VALUE_HEADS):
-        heads = own_refs[0].shape[0]
-        numer_ref, stats_ref = own_refs[head // heads * 2 : head // heads * 2 + 2]
-        peaks = [stats_ref[head % heads, 0]]
-        sums = [stats_ref[head % heads, 1]]
-        for part in range(2):
-            terms = came_ref[2 * head + part, first : first + 2 * local, :]
-            terms = terms.astype(jnp.float32)[:local]
-            terms = (terms + back(terms, GROUP)) + back(terms, 2 * GROUP)
-            peaks.append(terms)
-            sums.append(back(terms, 3 * GROUP))
-        peak = jnp.maximum(jnp.maximum(peaks[0], peaks[1]), peaks[2])
-        scales = [jnp.exp(p - peak) for p in peaks]
-        total = (sums[0] * scales[0] + sums[1] * scales[1]) + sums[2] * scales[2]
-        scales = [s / total for s in scales]
+        numer_ref = own_refs[head // heads * 2]
+        mine_at = slice(head * local, (head + 1) * local)
         for g in range(0, GROUP, 2):
             rows = slice(g * local, (g + 2) * local)
             numers = [numer_ref[head % heads, g : g + 2].reshape(2 * local, HEAD_FEATURES)] + [
@@ -236,7 +242,7 @@
             ]
             for k in range(2):
                 mine = [n[k * local : (k + 1) * local] for n in numers]
-                by = [s[:, g + k : g + k + 1] for s in scales]
+                by = [s[mine_at, g + k : g + k + 1] for s in scales]
                 value = (mine[0] * by[0] + mine[1] * by[1]) + mine[2] * by[2]
                 column = (head * GROUP + g + k) * HEAD_FEATURES
                 out_ref[:, column : column + HEAD_FEATURES] = value.astype(jnp.bfloat16)
@@ -272,27 +278,37 @@
     )(tiles, came, *own)
 
 
-def choose_kernel(match_ref, page_ref, out_ref):
+def choose_kernel(match_ref, page_ref, out_ref, held_ref, sems):
+    copies = []
     for instance in range(out_ref.shape[0]):
         page = page_ref[match_ref[instance]]
         for head in range(KEY_VALUE_HEADS):
-            out_ref[instance, head] = page[
+            held_ref[instance, head] = page[
                 :, :, head * HEAD_FEATURES : (head + 1) * HEAD_FEATURES
             ]
+        copies.append(
+            pltpu.make_async_copy(held_ref.at[instance], out_ref.at[instance], sems.at[instance])
+        )
+        copies[-1].start()
+    for copy in copies:
+        copy.wait()
 
 
 def choose(match, pages):
     instances, tokens = pages.shape[:2]
+    shape = (instances, KEY_VALUE_HEADS, tokens, 2, HEAD_FEATURES)
     return pl.pallas_call(
         choose_kernel,
-        out_shape=jax.ShapeDtypeStruct(
-            (instances, KEY_VALUE_HEADS, tokens, 2, HEAD_FEATURES), pages.dtype
-        ),
+        out_shape=jax.ShapeDtypeStruct(shape, pages.dtype),
         in_specs=[
             pl.BlockSpec(memory_space=pltpu.SMEM),
             pl.BlockSpec(memory_space=pltpu.VMEM),
         ],
-        out_specs=pl.BlockSpec(memory_space=pltpu.VMEM),
+        out_specs=pl.BlockSpec(memory_space=pl.ANY),
+        scratch_shapes=[
+            pltpu.VMEM(shape, pages.dtype),
+            pltpu.SemaphoreType.DMA((instances,)),
+        ],
         compiler_params=pltpu.CompilerParams(vmem_limit_bytes=16 * 1024 * 1024),
         cost_estimate=pl.CostEstimate(
             flops=0, bytes_accessed=4 * 1024 * 1024, transcendentals=0

time: 115 us -> 114 us (level)
  no operation moved by 1% of the time
where the time goes in v6:
time: 114 us
  starting transfers between devices  31.1 us (27%)
  Pallas kernels  30.5 us (27%)
  blocking collectives  25.9 us (23%)
  waiting for transfers between devices  20.4 us (18%)
  local copies, waits for them, and re-layouts  4.7 us (4%)
    all_to_all x1, blocking collectives, body(): came = lax.all_to_all(sent, 'samp', split_axis=0, concat_axis=0, tiled=True)  25.9 us
    pallas_call x2, Pallas kernels, partial_own(): pl.pallas_call(functools.partial(own_kernel, which * heads), grid=(1,), o...  21.7 us
    all_to_all x1, starting transfers between devices, body(): lax.all_to_all(chosen, ('inst', 'samp'), split_axis=0, concat_axis=0, til...  11.1 us
    all_to_all x1, waiting for transfers between devices, body(): lax.all_to_all(chosen, ('inst', 'samp'), split_axis=0, concat_axis=0, til...  10.3 us
    all_to_all x1, starting transfers between devices, body(): lax.all_to_all(prompt_key_values, 'inst', split_axis=1, concat_axis=0, ti...  10.3 us
    ppermute x4, starting transfers between devices, exchange(): lax.ppermute(sent, 'samp', [(i, i ^ 1 << place) for i in range(n_samp)])  9.71 us
    ppermute x4, waiting for transfers between devices, exchange(): lax.ppermute(sent, 'samp', [(i, i ^ 1 << place) for i in range(n_samp)])  7.45 us
    pallas_call x1, Pallas kernels, partial_shared(): pl.pallas_call(shared_kernel, out_shape=jax.ShapeDtypeStruct((owners, sen...  5.17 us
  transfers between devices with their start and end apart: 6, of which 4 were waited for; matrix products, arithmetic and copies ran while one was open for 0% of the time, Pallas kernels for 19%

profile of v6, /device:TPU:1, one launch (start us, length us, event | category | flops | bytes accessed | tf_op | source)
XLA Modules:
  0.0 113.7 jit_solution(9196657978855910345)
XLA Ops:
  0.6 0.0 copy-start.4
  0.6 0.0 copy-start.2
  0.6 10.3 %all-to-all-start = ((bf16[1,256,2,1024]{3,2,0,1:T(2,128)(2,1)}), bf16[1,256,2,1024]{3,2,0,1:T(2,128)(2,1)S(1)}, u32[]{:S(2)}, u32[]{:S(2)}) async-start(bf16[1,256,2,1024]{3,2,0,1:T(2,128)(2,1)} %bitcast.50), calls=%async_computation | async-start | bytes 2097152 | tf_op jit(solution)/shard_map/all_to_all | solution.py:340
  10.9 0.0 copy-done.4
  11.0 2.7 %collective-permute-start = (bf16[4,8,1536]{2,1,0:T(8,128)(2,1)S(1)}, bf16[4,8,1536]{2,1,0:T(8,128)(2,1)S(1)}, u32[]{:S(2)}, u32[]{:S(2)}) collective-permute-start(bf16[4,8,1536]{2,1,0:T(8,128)(2,1)S(1)} %dynamic-slice_bitcast_fusion), channel_id=1, source_target_pairs={{0,8},{1,9},{2,10},{3,11},{4,12},{5,13},{6,14},{7,15},{8,0},{9,1},... | collective-permute-start | bytes 294920 | tf_op jit(solution)/shard_map/ppermute | solution.py:327
  13.7 4.0 %collective-permute-done = bf16[4,8,1536]{2,1,0:T(8,128)(2,1)S(1)} collective-permute-done((bf16[4,8,1536]{2,1,0:T(8,128)(2,1)S(1)}, bf16[4,8,1536]{2,1,0:T(8,128)(2,1)S(1)}, u32[]{:S(2)}, u32[]{:S(2)}) %collective-permute-start) | collective-permute-done | bytes 98336 | tf_op jit(solution)/shard_map/ppermute | solution.py:327
  17.7 2.8 %collective-permute-start.1 = (bf16[2,2,8,1536]{3,2,1,0:T(8,128)(2,1)S(1)}, bf16[2,2,8,1536]{3,2,1,0:T(8,128)(2,1)S(1)}, u32[]{:S(2)}, u32[]{:S(2)}) collective-permute-start(bf16[2,2,8,1536]{3,2,1,0:T(8,128)(2,1)S(1)} %fusion), channel_id=1, source_target_pairs={{0,4},{1,5},{2,6},{3,7},{4,0},{5,1},{6,2},{7,3},{8,12},{9,13},{10,... | collective-permute-start | bytes 294920 | tf_op jit(solution)/shard_map/ppermute | solution.py:327
  20.6 0.2 reshape_squeeze.10
  20.7 0.1 pad.4.query_ref
  20.8 0.0 copy-done.2
  20.8 0.0 copy-start
  20.8 2.2 %copy-done = bf16[1,8,128,2,1024]{4,3,2,1,0:T(2,128)(2,1)S(1)} copy-done((bf16[1,8,128,2,1024]{4,3,2,1,0:T(2,128)(2,1)S(1)}, bf16[1,8,128,2,1024]{4,3,2,1,0:T(2,128)(2,1)}, u32[]{:S(2)}) %copy-start) | copy-done | bytes 4194328
  23.0 0.0 copy-start.3
  23.0 10.9 %shard_map.78 = (f32[4,12,8,128]{3,2,1,0:T(8,128)S(1)}, f32[4,2,8,128]{3,2,1,0:T(8,128)S(1)}) custom-call(s32[8]{0:T(128)S(1)} %bitcast.48, bf16[8,8,16,128]{3,2,1,0:T(8,128)(2,1)S(1)} %pad.4.query_ref, bf16[8,128,2,1024]{3,2,1,0:T(2,128)(2,1)S(1)} %bitcast.43), custom_call_target="tpu_custom_call" | custom-call | bytes 65536 | tf_op jit(solution)/shard_map/pallas_call | solution.py:60
  33.9 0.0 collective-permute-done.1
  33.9 2.7 %all-to-all-done = bf16[1,256,2,1024]{3,2,0,1:T(2,128)(2,1)S(1)} async-done(((bf16[1,256,2,1024]{3,2,0,1:T(2,128)(2,1)}), bf16[1,256,2,1024]{3,2,0,1:T(2,128)(2,1)S(1)}, u32[]{:S(2)}, u32[]{:S(2)}) %all-to-all-start) | async-done | bytes 1048608 | tf_op jit(solution)/shard_map/all_to_all | solution.py:340
  36.6 0.0 copy-done.3
  36.6 1.9 %shard_map.77 = bf16[16,8,16,2,128]{4,3,2,1,0:T(2,128)(2,1)} custom-call(s32[16]{0:T(128)S(1)} %copy-done.3, bf16[16,16,2,1024]{3,2,1,0:T(2,128)(2,1)S(1)} %bitcast.46), custom_call_target="tpu_custom_call" | custom-call | bytes 4194304 | tf_op jit(solution)/shard_map/pallas_call | solution.py:300
  38.5 0.0 copy-start.5
  38.5 11.1 %all-to-all-start.1 = ((bf16[256,16,128]{2,1,0:T(8,128)(2,1)}), bf16[256,16,128]{2,1,0:T(8,128)(2,1)S(1)}, u32[]{:S(2)}, u32[]{:S(2)}) async-start(bf16[256,16,128]{2,1,0:T(8,128)(2,1)} %bitcast.2), calls=%async_computation.1 | async-start | bytes 2097152 | tf_op jit(solution)/shard_map/all_to_all | solution.py:356
  49.7 1.5 %collective-permute-start.2 = (bf16[1,2,2,8,1536]{4,3,2,1,0:T(8,128)(2,1)S(1)}, bf16[1,2,2,8,1536]{4,3,2,1,0:T(8,128)(2,1)S(1)}, u32[]{:S(2)}, u32[]{:S(2)}) collective-permute-start(bf16[1,2,2,8,1536]{4,3,2,1,0:T(8,128)(2,1)S(1)} %constant_dynamic-slice_fusion), channel_id=1, source_target_pairs={{0,2},{1,3},{2,0},{3,1},{4,6},{5,7},{6,4},{7,5},{8,10},{9,11},{10,... | collective-permute-start | bytes 294920 | tf_op jit(solution)/shard_map/ppermute | solution.py:327
  51.2 0.0 copy-done.5
  51.2 0.1 reshape_squeeze.11
  51.2 3.4 %collective-permute-done.2 = bf16[1,2,2,8,1536]{4,3,2,1,0:T(8,128)(2,1)S(1)} collective-permute-done((bf16[1,2,2,8,1536]{4,3,2,1,0:T(8,128)(2,1)S(1)}, bf16[1,2,2,8,1536]{4,3,2,1,0:T(8,128)(2,1)S(1)}, u32[]{:S(2)}, u32[]{:S(2)}) %collective-permute-start.2) | collective-permute-done | bytes 98336 | tf_op jit(solution)/shard_map/ppermute | solution.py:327
  54.7 2.7 %collective-permute-start.3 = (bf16[1,2,2,2,8,1536]{5,4,3,2,1,0:T(8,128)(2,1)S(1)}, bf16[1,2,2,2,8,1536]{5,4,3,2,1,0:T(8,128)(2,1)S(1)}, u32[]{:S(2)}, u32[]{:S(2)}) collective-permute-start(bf16[1,2,2,2,8,1536]{5,4,3,2,1,0:T(8,128)(2,1)S(1)} %pad_maximum_fusion.2), channel_id=1, source_target_pairs={{0,1},{1,0},{2,3},{3,2},{4,5},{5,4},{6,7},{7,6},{8,9},{9,8},{10,11... | collective-permute-start | bytes 589832 | tf_op jit(solution)/shard_map/ppermute | solution.py:327
  57.5 0.0 copy-start.1
  57.5 2.2 %copy-done.1 = bf16[1,8,128,2,1024]{4,3,2,1,0:T(2,128)(2,1)S(1)} copy-done((bf16[1,8,128,2,1024]{4,3,2,1,0:T(2,128)(2,1)S(1)}, bf16[1,8,128,2,1024]{4,3,2,1,0:T(2,128)(2,1)}, u32[]{:S(2)}) %copy-start.1) | copy-done | bytes 4194328
  59.6 10.9 %shard_map.79 = (f32[4,12,8,128]{3,2,1,0:T(8,128)S(1)}, f32[4,2,8,128]{3,2,1,0:T(8,128)S(1)}) custom-call(s32[8]{0:T(128)S(1)} %bitcast.49, bf16[8,8,16,128]{3,2,1,0:T(8,128)(2,1)S(1)} %pad.4.query_ref, bf16[8,128,2,1024]{3,2,1,0:T(2,128)(2,1)S(1)} %bitcast.44), custom_call_target="tpu_custom_call" | custom-call | bytes 65536 | tf_op jit(solution)/shard_map/pallas_call | solution.py:60
  70.5 0.0 collective-permute-done.3
  70.6 10.3 %all-to-all-done.1.pair_ref = bf16[256,16,128]{2,1,0:T(8,128)(2,1)S(1)} async-done(((bf16[256,16,128]{2,1,0:T(8,128)(2,1)}), bf16[256,16,128]{2,1,0:T(8,128)(2,1)S(1)}, u32[]{:S(2)}, u32[]{:S(2)}) %all-to-all-start.1) | async-done | bytes 1048608 | tf_op jit(solution)/shard_map/all_to_all | solution.py:356
  80.9 5.2 %shard_map.80 = bf16[16,368,128]{2,1,0:T(8,128)(2,1)S(1)} custom-call(s32[256]{0:T(256)S(1)} %fusion.5.place_ref, bf16[128,1536]{1,0:T(8,128)(2,1)S(1)} %bitcast.47, bf16[256,16,128]{2,1,0:T(8,128)(2,1)S(1)} %all-to-all-done.1.pair_ref), custom_call_target="tpu_custom_call" | custom-call | flops 1610612736 | bytes 4194304 | tf_op jit(solution)/shard_map/pallas_call | solution.py:163
  86.1 25.9 %all_to_all.22.came_ref = bf16[16,368,128]{2,1,0:T(8,128)(2,1)S(1)} all-to-all(bf16[16,368,128]{2,1,0:T(8,128)(2,1)S(1)} %shard_map.80), channel_id=1, replica_groups=mesh['inst'=16,'samp'=16] {'samp'}, dimensions={0} | all-to-all | bytes 3014656 | tf_op jit(solution)/shard_map/all_to_all | solution.py:365
  112.0 1.8 %shard_map.81 = (bf16[8,12288]{1,0:T(8,128)(2,1)}, bf16[16,16,2,1024]{3,2,1,0:T(2,128)(2,1)}) custom-call(bf16[16,23,8,2,128]{4,3,2,1,0:T(2,128)(2,1)S(1)} %bitcast.45, bf16[16,368,128]{2,1,0:T(8,128)(2,1)S(1)} %all_to_all.22.came_ref, f32[4,12,8,128]{3,2,1,0:T(8,128)S(1)} %get-tuple-element.32.refs_0_, f32[4,2,8,128]{3,2,1,0:T(8,128)S(1)} %get-tuple-element.33.refs_1_, ...), custom_call_target="tpu_custom_call" | custom-call | flops 589824 | bytes 4194304 | tf_op jit(solution)/shard_map/pallas_call | solution.py:258
  (11 shorter events, 0.2 us)
Async XLA Ops:
  0.6 10.3 %copy-start.4 = (bf16[1,8,12288]{2,1,0:T(8,128)(2,1)S(1)}, bf16[1,8,12288]{2,1,0:T(8,128)(2,1)}, u32[]{:S(2)}) copy-start(bf16[1,8,12288]{2,1,0:T(8,128)(2,1)} %param.9) | copy-start | bytes 589828
  0.6 20.1 %copy-start.2 = (s32[1,8]{1,0:T(1,128)S(1)}, s32[1,8]{1,0:T(1,128)}, u32[]{:S(2)}) copy-start(s32[1,8]{1,0:T(1,128)} %param.11) | copy-start | bytes 100
  0.6 36.0 %all-to-all-start = ((bf16[1,256,2,1024]{3,2,0,1:T(2,128)(2,1)}), bf16[1,256,2,1024]{3,2,0,1:T(2,128)(2,1)S(1)}, u32[]{:S(2)}, u32[]{:S(2)}) async-start(bf16[1,256,2,1024]{3,2,0,1:T(2,128)(2,1)} %bitcast.50), calls=%async_computation | async-start | bytes 2097152 | tf_op jit(solution)/shard_map/all_to_all | solution.py:340
  11.0 6.7 %collective-permute-start = (bf16[4,8,1536]{2,1,0:T(8,128)(2,1)S(1)}, bf16[4,8,1536]{2,1,0:T(8,128)(2,1)S(1)}, u32[]{:S(2)}, u32[]{:S(2)}) collective-permute-start(bf16[4,8,1536]{2,1,0:T(8,128)(2,1)S(1)} %dynamic-slice_bitcast_fusion), channel_id=1, source_target_pairs={{0,8},{1,9},{2,10},{3,11},{4,12},{5,13},{6,14},{7,15},{8,0},{9,1},... | collective-permute-start | bytes 294920 | tf_op jit(solution)/shard_map/ppermute | solution.py:327
  17.7 16.1 %collective-permute-start.1 = (bf16[2,2,8,1536]{3,2,1,0:T(8,128)(2,1)S(1)}, bf16[2,2,8,1536]{3,2,1,0:T(8,128)(2,1)S(1)}, u32[]{:S(2)}, u32[]{:S(2)}) collective-permute-start(bf16[2,2,8,1536]{3,2,1,0:T(8,128)(2,1)S(1)} %fusion), channel_id=1, source_target_pairs={{0,4},{1,5},{2,6},{3,7},{4,0},{5,1},{6,2},{7,3},{8,12},{9,13},{10,... | collective-permute-start | bytes 294920 | tf_op jit(solution)/shard_map/ppermute | solution.py:327
  20.8 2.2 %copy-start = (bf16[1,8,128,2,1024]{4,3,2,1,0:T(2,128)(2,1)S(1)}, bf16[1,8,128,2,1024]{4,3,2,1,0:T(2,128)(2,1)}, u32[]{:S(2)}) copy-start(bf16[1,8,128,2,1024]{4,3,2,1,0:T(2,128)(2,1)} %param.10) | copy-start | bytes 12582916
  23.0 13.6 %copy-start.3 = (s32[16]{0:T(128)S(1)}, s32[16]{0:T(128)}, u32[]{:S(2)}) copy-start(s32[16]{0:T(128)} %match_ref.1) | copy-start | bytes 196
  38.5 12.7 %copy-start.5 = (s32[1,16,16]{2,1,0:T(8,128)S(1)}, s32[1,16,16]{2,1,0:T(8,128)}, u32[]{:S(2)}) copy-start(s32[1,16,16]{2,1,0:T(8,128)} %param.8) | copy-start | bytes 3076
  38.5 42.4 %all-to-all-start.1 = ((bf16[256,16,128]{2,1,0:T(8,128)(2,1)}), bf16[256,16,128]{2,1,0:T(8,128)(2,1)S(1)}, u32[]{:S(2)}, u32[]{:S(2)}) async-start(bf16[256,16,128]{2,1,0:T(8,128)(2,1)} %bitcast.2), calls=%async_computation.1 | async-start | bytes 2097152 | tf_op jit(solution)/shard_map/all_to_all | solution.py:356
  49.7 5.0 %collective-permute-start.2 = (bf16[1,2,2,8,1536]{4,3,2,1,0:T(8,128)(2,1)S(1)}, bf16[1,2,2,8,1536]{4,3,2,1,0:T(8,128)(2,1)S(1)}, u32[]{:S(2)}, u32[]{:S(2)}) collective-permute-start(bf16[1,2,2,8,1536]{4,3,2,1,0:T(8,128)(2,1)S(1)} %constant_dynamic-slice_fusion), channel_id=1, source_target_pairs={{0,2},{1,3},{2,0},{3,1},{4,6},{5,7},{6,4},{7,5},{8,10},{9,11},{10,... | collective-permute-start | bytes 294920 | tf_op jit(solution)/shard_map/ppermute | solution.py:327
  54.7 15.8 %collective-permute-start.3 = (bf16[1,2,2,2,8,1536]{5,4,3,2,1,0:T(8,128)(2,1)S(1)}, bf16[1,2,2,2,8,1536]{5,4,3,2,1,0:T(8,128)(2,1)S(1)}, u32[]{:S(2)}, u32[]{:S(2)}) collective-permute-start(bf16[1,2,2,2,8,1536]{5,4,3,2,1,0:T(8,128)(2,1)S(1)} %pad_maximum_fusion.2), channel_id=1, source_target_pairs={{0,1},{1,0},{2,3},{3,2},{4,5},{5,4},{6,7},{7,6},{8,9},{9,8},{10,11... | collective-permute-start | bytes 589832 | tf_op jit(solution)/shard_map/ppermute | solution.py:327
  57.5 2.2 %copy-start.1 = (bf16[1,8,128,2,1024]{4,3,2,1,0:T(2,128)(2,1)S(1)}, bf16[1,8,128,2,1024]{4,3,2,1,0:T(2,128)(2,1)}, u32[]{:S(2)}) copy-start(bf16[1,8,128,2,1024]{4,3,2,1,0:T(2,128)(2,1)} %param.10) | copy-start | bytes 12582916

commit v7 on v6

--- a/solution.py
+++ b/solution.py
@@ -278,42 +278,35 @@
     )(tiles, came, *own)
 
 
-def choose_kernel(match_ref, page_ref, out_ref, held_ref, sems):
+def split_kernel(page_ref, out_ref, held_ref, sems):
     copies = []
-    for instance in range(out_ref.shape[0]):
-        page = page_ref[match_ref[instance]]
+    for page in range(out_ref.shape[0]):
+        rows = page_ref[page]
         for head in range(KEY_VALUE_HEADS):
-            held_ref[instance, head] = page[
-                :, :, head * HEAD_FEATURES : (head + 1) * HEAD_FEATURES
-            ]
-        copies.append(
-            pltpu.make_async_copy(held_ref.at[instance], out_ref.at[instance], sems.at[instance])
-        )
+            held_ref[page, head] = rows[:, :, head * HEAD_FEATURES : (head + 1) * HEAD_FEATURES]
+        copies.append(pltpu.make_async_copy(held_ref.at[page], out_ref.at[page], sems.at[page]))
         copies[-1].start()
     for copy in copies:
         copy.wait()
 
 
-def choose(match, pages):
-    instances, tokens = pages.shape[:2]
-    shape = (instances, KEY_VALUE_HEADS, tokens, 2, HEAD_FEATURES)
+def split_heads(pages):
+    count, tokens = pages.shape[:2]
+    shape = (count, KEY_VALUE_HEADS, tokens, 2, HEAD_FEATURES)
     return pl.pallas_call(
-        choose_kernel,
+        split_kernel,
         out_shape=jax.ShapeDtypeStruct(shape, pages.dtype),
-        in_specs=[
-            pl.BlockSpec(memory_space=pltpu.SMEM),
-            pl.BlockSpec(memory_space=pltpu.VMEM),
-        ],
+        in_specs=[pl.BlockSpec(memory_space=pltpu.VMEM)],
         out_specs=pl.BlockSpec(memory_space=pl.ANY),
         scratch_shapes=[
             pltpu.VMEM(shape, pages.dtype),
-            pltpu.SemaphoreType.DMA((instances,)),
+            pltpu.SemaphoreType.DMA((count,)),
         ],
         compiler_params=pltpu.CompilerParams(vmem_limit_bytes=16 * 1024 * 1024),
         cost_estimate=pl.CostEstimate(
             flops=0, bytes_accessed=4 * 1024 * 1024, transcendentals=0
         ),
-    )(match, pages)
+    )(pages)
 
 
 def exchange(held, member, n_samp, place, axis):
@@ -337,7 +330,11 @@
     member = lax.axis_index("samp")
     local_queries = queries[0]
 
-    pages = lax.all_to_all(prompt_key_values, "inst", split_axis=1, concat_axis=0, tiled=True)
+    pages = prompt_key_values.reshape(
+        n_inst, PAGE_TOKENS, 2, KEY_VALUE_HEADS * HEAD_FEATURES
+    )
+    pieces = split_heads(pages).reshape(n_inst * n_samp, half * 2, HEAD_FEATURES)
+    spread = lax.all_to_all(pieces, ("inst", "samp"), split_axis=0, concat_axis=0, tiled=True)
 
     cache = sample_key_values[0]
     grouped = local_queries.reshape(local_total, KEY_VALUE_HEADS, GROUP, HEAD_FEATURES)
@@ -351,17 +348,20 @@
     listed = page_list[0].reshape(-1)
     place = (listed % pages_dev) * n_samp + listed // pages_dev
 
-    chosen = choose(match, pages).reshape(n_inst * n_samp, half * 2, HEAD_FEATURES)
-    chosen, held, grouped, own = lax.optimization_barrier((chosen, held, grouped, own))
-    pairs = lax.all_to_all(chosen, ("inst", "samp"), split_axis=0, concat_axis=0, tiled=True)
-
-    own = own + partial_own(gen_len[0], grouped, cache, 1, 2)
+    blocks = spread.reshape(n_inst, n_samp * half * 2, HEAD_FEATURES)
+    blocks = blocks.at[match].get(mode="promise_in_bounds")
+    blocks, held, grouped, own = lax.optimization_barrier((blocks, held, grouped, own))
+    pairs = lax.all_to_all(blocks, "inst", split_axis=0, concat_axis=0, tiled=True)
+    pairs = pairs.reshape(n_inst * n_samp, half * 2, HEAD_FEATURES)
+
     held = exchange(held, member, n_samp, 1, 3)
     held = exchange(held, member, n_samp, 0, 4)
     head_queries = held.reshape(n_samp * local_total, WIDTH)
-    pairs, place, head_queries, own = lax.optimization_barrier((pairs, place, head_queries, own))
+    pairs, place, head_queries = lax.optimization_barrier((pairs, place, head_queries))
 
     sent = partial_shared(place, head_queries, pairs, n_samp)
+    sent, grouped = lax.optimization_barrier((sent, grouped))
+    own = own + partial_own(gen_len[0], grouped, cache, 1, 2)
     came = lax.all_to_all(sent, "samp", split_axis=0, concat_axis=0, tiled=True)
     attended, page_pool = finish(came, own, local_total, pages_dev)
     return (attended[None], page_pool[None])

time: 114 us -> 118 us (1.035)
  blocking collectives: 25.9 us -> 0 us
  waiting for transfers between devices: 20.4 us -> 44.1 us
  starting transfers between devices: 31.1 us -> 34 us
  local copies, waits for them, and re-layouts: 4.7 us -> 7.57 us
    all_to_all x1 -> x0, blocking collectives: 25.9 us -> none  [body(): came = lax.all_to_all(sent, 'samp', split_axis=0, concat_axis=0, tiled=True)]
    all_to_all x2 -> x3, waiting for transfers between devices: 13 us -> 36 us  [the longest x1 18.8 us: body(): lax.all_to_all(blocks, 'inst', split_axis=0, concat_axis=0, tiled=True)]
    all_to_all x2 -> x3, starting transfers between devices: 21.4 us -> 25.8 us  [the longest x1 15.7 us: body(): lax.all_to_all(pieces, ('inst', 'samp'), split_axis=0, concat_axis=0, til...]
    gather x0 -> x1, local copies, waits for them, and re-layouts: none -> 1.65 us  [body(): blocks = blocks.at[match].get(mode='promise_in_bounds')]
    ppermute x4, starting transfers between devices: 9.71 us -> 8.22 us  [exchange(): lax.ppermute(sent, 'samp', [(i, i ^ 1 << place) for i in range(n_samp)])]
    pallas_call x1, Pallas kernels: 5.17 us -> 6.46 us  [partial_shared(): pl.pallas_call(shared_kernel, out_shape=jax.ShapeDtypeStruct((owners, sen...]
    unnamed x12 -> x14, local copies, waits for them, and re-layouts: 4.38 us -> 5.61 us
  transfers between devices with their start and end apart: 6 -> 7, of which waited for: 4 -> 6; matrix products, arithmetic and copies ran while one was open for 0% -> 0% of each run, Pallas kernels for 19% -> 18%
where the time goes in v7:
time: 118 us
  waiting for transfers between devices  44.1 us (37%)
  starting transfers between devices  34 us (29%)
  Pallas kernels  31.3 us (27%)
  local copies, waits for them, and re-layouts  7.57 us (6%)
    pallas_call x2, Pallas kernels, partial_own(): pl.pallas_call(functools.partial(own_kernel, which * heads), grid=(1,), o...  21.7 us
    all_to_all x1, waiting for transfers between devices, body(): lax.all_to_all(blocks, 'inst', split_axis=0, concat_axis=0, tiled=True)  18.8 us
    all_to_all x1, starting transfers between devices, body(): lax.all_to_all(pieces, ('inst', 'samp'), split_axis=0, concat_axis=0, til...  15.7 us
    all_to_all x1, waiting for transfers between devices, body(): came = lax.all_to_all(sent, 'samp', split_axis=0, concat_axis=0, tiled=True)  9.21 us
    ppermute x4, starting transfers between devices, exchange(): lax.ppermute(sent, 'samp', [(i, i ^ 1 << place) for i in range(n_samp)])  8.22 us
    all_to_all x1, waiting for transfers between devices, body(): lax.all_to_all(pieces, ('inst', 'samp'), split_axis=0, concat_axis=0, til...  8.02 us
    ppermute x4, waiting for transfers between devices, exchange(): lax.ppermute(sent, 'samp', [(i, i ^ 1 << place) for i in range(n_samp)])  8 us
    pallas_call x1, Pallas kernels, partial_shared(): pl.pallas_call(shared_kernel, out_shape=jax.ShapeDtypeStruct((owners, sen...  6.46 us
  transfers between devices with their start and end apart: 7, of which 6 were waited for; matrix products, arithmetic and copies ran while one was open for 0% of the time, Pallas kernels for 18%

profile of v7, /device:TPU:1, one launch (start us, length us, event | category | flops | bytes accessed | tf_op | source)
XLA Modules:
  0.0 117.9 jit_solution(841287853434183801)
XLA Ops:
  0.6 0.0 copy-start.2
  0.6 1.2 %copy-done.2 = bf16[1,256,2,1024]{3,2,1,0:T(2,128)(2,1)S(1)} copy-done((bf16[1,256,2,1024]{3,2,1,0:T(2,128)(2,1)S(1)}, bf16[1,256,2,1024]{3,2,1,0:T(2,128)(2,1)}, u32[]{:S(2)}) %copy-start.2) | copy-done | bytes 1048600
  1.9 1.3 %shard_map.77 = bf16[16,8,16,2,128]{4,3,2,1,0:T(2,128)(2,1)} custom-call(bf16[16,16,2,1024]{3,2,1,0:T(2,128)(2,1)S(1)} %bitcast.47), custom_call_target="tpu_custom_call" | custom-call | bytes 4194304 | tf_op jit(solution)/shard_map/pallas_call | solution.py:296
  3.2 0.0 copy-start.4
  3.2 0.0 copy-start.6
  3.2 0.0 copy-start.3
  3.2 15.7 %all-to-all-start = ((bf16[256,16,128]{2,1,0:T(8,128)(2,1)}), bf16[256,16,128]{2,1,0:T(8,128)(2,1)S(1)}, u32[]{:S(2)}, u32[]{:S(2)}) async-start(bf16[256,16,128]{2,1,0:T(8,128)(2,1)} %bitcast.1), calls=%async_computation | async-start | bytes 2097152 | tf_op jit(solution)/shard_map/all_to_all | solution.py:337
  18.9 0.0 copy-done.4
  18.9 3.0 %collective-permute-start = (bf16[4,8,1536]{2,1,0:T(8,128)(2,1)S(1)}, bf16[4,8,1536]{2,1,0:T(8,128)(2,1)S(1)}, u32[]{:S(2)}, u32[]{:S(2)}) collective-permute-start(bf16[4,8,1536]{2,1,0:T(8,128)(2,1)S(1)} %dynamic-slice_bitcast_fusion), channel_id=1, source_target_pairs={{0,8},{1,9},{2,10},{3,11},{4,12},{5,13},{6,14},{7,15},{8,0},{9,1},... | collective-permute-start | bytes 294920 | tf_op jit(solution)/shard_map/ppermute | solution.py:320
  21.9 0.0 copy-done.6
  21.9 0.2 reshape_squeeze.10
  22.1 0.1 pad.4.query_ref
  22.1 0.0 copy-done.3
  22.1 0.0 copy-start
  22.2 2.2 %copy-done = bf16[1,8,128,2,1024]{4,3,2,1,0:T(2,128)(2,1)S(1)} copy-done((bf16[1,8,128,2,1024]{4,3,2,1,0:T(2,128)(2,1)S(1)}, bf16[1,8,128,2,1024]{4,3,2,1,0:T(2,128)(2,1)}, u32[]{:S(2)}) %copy-start) | copy-done | bytes 4194328
  24.3 10.9 %shard_map.78 = (f32[4,12,8,128]{3,2,1,0:T(8,128)S(1)}, f32[4,2,8,128]{3,2,1,0:T(8,128)S(1)}) custom-call(s32[8]{0:T(128)S(1)} %bitcast.50, bf16[8,8,16,128]{3,2,1,0:T(8,128)(2,1)S(1)} %pad.4.query_ref, bf16[8,128,2,1024]{3,2,1,0:T(2,128)(2,1)S(1)} %bitcast.44), custom_call_target="tpu_custom_call" | custom-call | bytes 65536 | tf_op jit(solution)/shard_map/pallas_call | solution.py:60
  35.2 0.0 collective-permute-done
  35.3 2.8 %collective-permute-start.1 = (bf16[2,2,8,1536]{3,2,1,0:T(8,128)(2,1)S(1)}, bf16[2,2,8,1536]{3,2,1,0:T(8,128)(2,1)S(1)}, u32[]{:S(2)}, u32[]{:S(2)}) collective-permute-start(bf16[2,2,8,1536]{3,2,1,0:T(8,128)(2,1)S(1)} %fusion), channel_id=1, source_target_pairs={{0,4},{1,5},{2,6},{3,7},{4,0},{5,1},{6,2},{7,3},{8,12},{9,13},{10,... | collective-permute-start | bytes 294920 | tf_op jit(solution)/shard_map/ppermute | solution.py:320
  38.1 4.0 %collective-permute-done.1 = bf16[2,2,8,1536]{3,2,1,0:T(8,128)(2,1)S(1)} collective-permute-done((bf16[2,2,8,1536]{3,2,1,0:T(8,128)(2,1)S(1)}, bf16[2,2,8,1536]{3,2,1,0:T(8,128)(2,1)S(1)}, u32[]{:S(2)}, u32[]{:S(2)}) %collective-permute-start.1) | collective-permute-done | bytes 98336 | tf_op jit(solution)/shard_map/ppermute | solution.py:320
  42.1 8.0 %all-to-all-done = bf16[256,16,128]{2,1,0:T(8,128)(2,1)S(1)} async-done(((bf16[256,16,128]{2,1,0:T(8,128)(2,1)}), bf16[256,16,128]{2,1,0:T(8,128)(2,1)S(1)}, u32[]{:S(2)}, u32[]{:S(2)}) %all-to-all-start) | async-done | bytes 1048608 | tf_op jit(solution)/shard_map/all_to_all | solution.py:337
  50.2 1.6 %gather_fusion = bf16[16,256,128]{2,1,0:T(8,128)(2,1)} fusion(bf16[16,256,128]{2,1,0:T(8,128)(2,1)S(1)} %bitcast.52, s32[1024]{0:T(1024)S(1)} %pad_clamp_fusion), kind=kCustom, calls=%fused_computation | custom fusion | bytes 2097216 | tf_op jit(solution)/shard_map/gather | solution.py:352
  51.8 0.0 copy-start.5
  51.8 3.8 %all-to-all-start.1 = ((bf16[16,256,128]{2,1,0:T(8,128)(2,1)}), bf16[16,256,128]{2,1,0:T(8,128)(2,1)S(1)}, u32[]{:S(2)}, u32[]{:S(2)}) async-start(bf16[16,256,128]{2,1,0:T(8,128)(2,1)} %gather_fusion), calls=%async_computation.1 | async-start | bytes 2097152 | tf_op jit(solution)/shard_map/all_to_all | solution.py:354
  55.6 0.5 collective-permute-start.2
  56.2 0.0 copy-done.5
  56.2 0.1 reshape_squeeze.11
  56.2 2.9 %collective-permute-done.2 = bf16[1,2,2,8,1536]{4,3,2,1,0:T(8,128)(2,1)S(1)} collective-permute-done((bf16[1,2,2,8,1536]{4,3,2,1,0:T(8,128)(2,1)S(1)}, bf16[1,2,2,8,1536]{4,3,2,1,0:T(8,128)(2,1)S(1)}, u32[]{:S(2)}, u32[]{:S(2)}) %collective-permute-start.2) | collective-permute-done | bytes 98336 | tf_op jit(solution)/shard_map/ppermute | solution.py:320
  59.2 1.9 %collective-permute-start.3 = (bf16[1,2,2,2,8,1536]{5,4,3,2,1,0:T(8,128)(2,1)S(1)}, bf16[1,2,2,2,8,1536]{5,4,3,2,1,0:T(8,128)(2,1)S(1)}, u32[]{:S(2)}, u32[]{:S(2)}) collective-permute-start(bf16[1,2,2,2,8,1536]{5,4,3,2,1,0:T(8,128)(2,1)S(1)} %pad_maximum_fusion.2), channel_id=1, source_target_pairs={{0,1},{1,0},{2,3},{3,2},{4,5},{5,4},{6,7},{7,6},{8,9},{9,8},{10,11... | collective-permute-start | bytes 589832 | tf_op jit(solution)/shard_map/ppermute | solution.py:320
  61.2 1.1 collective-permute-done.3
  62.3 18.8 %all-to-all-done.1 = bf16[16,256,128]{2,1,0:T(8,128)(2,1)S(1)} async-done(((bf16[16,256,128]{2,1,0:T(8,128)(2,1)}), bf16[16,256,128]{2,1,0:T(8,128)(2,1)S(1)}, u32[]{:S(2)}, u32[]{:S(2)}) %all-to-all-start.1) | async-done | bytes 1048608 | tf_op jit(solution)/shard_map/all_to_all | solution.py:354
  81.1 6.5 %shard_map.79 = bf16[16,368,128]{2,1,0:T(8,128)(2,1)} custom-call(s32[256]{0:T(256)S(1)} %fusion.5.place_ref, bf16[128,1536]{1,0:T(8,128)(2,1)S(1)} %bitcast.49, bf16[256,16,128]{2,1,0:T(8,128)(2,1)S(1)} %bitcast.48), custom_call_target="tpu_custom_call" | custom-call | flops 1610612736 | bytes 4194304 | tf_op jit(solution)/shard_map/pallas_call | solution.py:163
  87.6 6.3 %all-to-all-start.2 = ((bf16[16,368,128]{2,1,0:T(8,128)(2,1)}), bf16[16,368,128]{2,1,0:T(8,128)(2,1)S(1)}, u32[]{:S(2)}, u32[]{:S(2)}) async-start(bf16[16,368,128]{2,1,0:T(8,128)(2,1)} %shard_map.79), calls=%async_computation.2 | async-start | bytes 3014656 | tf_op jit(solution)/shard_map/all_to_all | solution.py:365
  93.9 0.0 copy-start.1
  93.9 2.2 %copy-done.1 = bf16[1,8,128,2,1024]{4,3,2,1,0:T(2,128)(2,1)S(1)} copy-done((bf16[1,8,128,2,1024]{4,3,2,1,0:T(2,128)(2,1)S(1)}, bf16[1,8,128,2,1024]{4,3,2,1,0:T(2,128)(2,1)}, u32[]{:S(2)}) %copy-start.1) | copy-done | bytes 4194328
  96.1 10.9 %shard_map.80 = (f32[4,12,8,128]{3,2,1,0:T(8,128)S(1)}, f32[4,2,8,128]{3,2,1,0:T(8,128)S(1)}) custom-call(s32[8]{0:T(128)S(1)} %bitcast.51, bf16[8,8,16,128]{3,2,1,0:T(8,128)(2,1)S(1)} %pad.4.query_ref, bf16[8,128,2,1024]{3,2,1,0:T(2,128)(2,1)S(1)} %bitcast.45), custom_call_target="tpu_custom_call" | custom-call | bytes 65536 | tf_op jit(solution)/shard_map/pallas_call | solution.py:60
  107.0 9.2 %all-to-all-done.2.came_ref = bf16[16,368,128]{2,1,0:T(8,128)(2,1)S(1)} async-done(((bf16[16,368,128]{2,1,0:T(8,128)(2,1)}), bf16[16,368,128]{2,1,0:T(8,128)(2,1)S(1)}, u32[]{:S(2)}, u32[]{:S(2)}) %all-to-all-start.2) | async-done | bytes 1507360 | tf_op jit(solution)/shard_map/all_to_all | solution.py:365
  116.2 1.8 %shard_map.81 = (bf16[8,12288]{1,0:T(8,128)(2,1)}, bf16[16,16,2,1024]{3,2,1,0:T(2,128)(2,1)}) custom-call(bf16[16,23,8,2,128]{4,3,2,1,0:T(2,128)(2,1)S(1)} %bitcast.46, bf16[16,368,128]{2,1,0:T(8,128)(2,1)S(1)} %all-to-all-done.2.came_ref, f32[4,12,8,128]{3,2,1,0:T(8,128)S(1)} %get-tuple-element.27.refs_0_, f32[4,2,8,128]{3,2,1,0:T(8,128)S(1)} %get-tuple-element.28.refs_1_, ...), custom_call_target="tpu_custom_call" | custom-call | flops 589824 | bytes 4194304 | tf_op jit(solution)/shard_map/pallas_call | solution.py:258
  (13 shorter events, 0.2 us)
Async XLA Ops:
  0.6 1.2 %copy-start.2 = (bf16[1,256,2,1024]{3,2,1,0:T(2,128)(2,1)S(1)}, bf16[1,256,2,1024]{3,2,1,0:T(2,128)(2,1)}, u32[]{:S(2)}) copy-start(bf16[1,256,2,1024]{3,2,1,0:T(2,128)(2,1)} %param.6) | copy-start | bytes 3145732
  3.2 15.7 %copy-start.4 = (bf16[1,8,12288]{2,1,0:T(8,128)(2,1)S(1)}, bf16[1,8,12288]{2,1,0:T(8,128)(2,1)}, u32[]{:S(2)}) copy-start(bf16[1,8,12288]{2,1,0:T(8,128)(2,1)} %param.9) | copy-start | bytes 589828
  3.2 18.7 %copy-start.6 = (s32[16]{0:T(128)S(1)}, s32[16]{0:T(128)}, u32[]{:S(2)}) copy-start(s32[16]{0:T(128)} %param.7) | copy-start | bytes 196
  3.2 18.9 %copy-start.3 = (s32[1,8]{1,0:T(1,128)S(1)}, s32[1,8]{1,0:T(1,128)}, u32[]{:S(2)}) copy-start(s32[1,8]{1,0:T(1,128)} %param.11) | copy-start | bytes 100
  3.2 46.9 %all-to-all-start = ((bf16[256,16,128]{2,1,0:T(8,128)(2,1)}), bf16[256,16,128]{2,1,0:T(8,128)(2,1)S(1)}, u32[]{:S(2)}, u32[]{:S(2)}) async-start(bf16[256,16,128]{2,1,0:T(8,128)(2,1)} %bitcast.1), calls=%async_computation | async-start | bytes 2097152 | tf_op jit(solution)/shard_map/all_to_all | solution.py:337
  18.9 16.3 %collective-permute-start = (bf16[4,8,1536]{2,1,0:T(8,128)(2,1)S(1)}, bf16[4,8,1536]{2,1,0:T(8,128)(2,1)S(1)}, u32[]{:S(2)}, u32[]{:S(2)}) collective-permute-start(bf16[4,8,1536]{2,1,0:T(8,128)(2,1)S(1)} %dynamic-slice_bitcast_fusion), channel_id=1, source_target_pairs={{0,8},{1,9},{2,10},{3,11},{4,12},{5,13},{6,14},{7,15},{8,0},{9,1},... | collective-permute-start | bytes 294920 | tf_op jit(solution)/shard_map/ppermute | solution.py:320
  22.1 2.2 %copy-start = (bf16[1,8,128,2,1024]{4,3,2,1,0:T(2,128)(2,1)S(1)}, bf16[1,8,128,2,1024]{4,3,2,1,0:T(2,128)(2,1)}, u32[]{:S(2)}) copy-start(bf16[1,8,128,2,1024]{4,3,2,1,0:T(2,128)(2,1)} %param.10) | copy-start | bytes 12582916
  35.3 6.8 %collective-permute-start.1 = (bf16[2,2,8,1536]{3,2,1,0:T(8,128)(2,1)S(1)}, bf16[2,2,8,1536]{3,2,1,0:T(8,128)(2,1)S(1)}, u32[]{:S(2)}, u32[]{:S(2)}) collective-permute-start(bf16[2,2,8,1536]{3,2,1,0:T(8,128)(2,1)S(1)} %fusion), channel_id=1, source_target_pairs={{0,4},{1,5},{2,6},{3,7},{4,0},{5,1},{6,2},{7,3},{8,12},{9,13},{10,... | collective-permute-start | bytes 294920 | tf_op jit(solution)/shard_map/ppermute | solution.py:320
  51.8 4.4 %copy-start.5 = (s32[1,16,16]{2,1,0:T(8,128)S(1)}, s32[1,16,16]{2,1,0:T(8,128)}, u32[]{:S(2)}) copy-start(s32[1,16,16]{2,1,0:T(8,128)} %param.8) | copy-start | bytes 3076
  51.8 29.3 %all-to-all-start.1 = ((bf16[16,256,128]{2,1,0:T(8,128)(2,1)}), bf16[16,256,128]{2,1,0:T(8,128)(2,1)S(1)}, u32[]{:S(2)}, u32[]{:S(2)}) async-start(bf16[16,256,128]{2,1,0:T(8,128)(2,1)} %gather_fusion), calls=%async_computation.1 | async-start | bytes 2097152 | tf_op jit(solution)/shard_map/all_to_all | solution.py:354
  55.6 3.6 %collective-permute-start.2 = (bf16[1,2,2,8,1536]{4,3,2,1,0:T(8,128)(2,1)S(1)}, bf16[1,2,2,8,1536]{4,3,2,1,0:T(8,128)(2,1)S(1)}, u32[]{:S(2)}, u32[]{:S(2)}) collective-permute-start(bf16[1,2,2,8,1536]{4,3,2,1,0:T(8,128)(2,1)S(1)} %constant_dynamic-slice_fusion), channel_id=1, source_target_pairs={{0,2},{1,3},{2,0},{3,1},{4,6},{5,7},{6,4},{7,5},{8,10},{9,11},{10,... | collective-permute-start | bytes 294920 | tf_op jit(solution)/shard_map/ppermute | solution.py:320
  59.2 3.0 %collective-permute-start.3 = (bf16[1,2,2,2,8,1536]{5,4,3,2,1,0:T(8,128)(2,1)S(1)}, bf16[1,2,2,2,8,1536]{5,4,3,2,1,0:T(8,128)(2,1)S(1)}, u32[]{:S(2)}, u32[]{:S(2)}) collective-permute-start(bf16[1,2,2,2,8,1536]{5,4,3,2,1,0:T(8,128)(2,1)S(1)} %pad_maximum_fusion.2), channel_id=1, source_target_pairs={{0,1},{1,0},{2,3},{3,2},{4,5},{5,4},{6,7},{7,6},{8,9},{9,8},{10,11... | collective-permute-start | bytes 589832 | tf_op jit(solution)/shard_map/ppermute | solution.py:320
  87.6 28.6 %all-to-all-start.2 = ((bf16[16,368,128]{2,1,0:T(8,128)(2,1)}), bf16[16,368,128]{2,1,0:T(8,128)(2,1)S(1)}, u32[]{:S(2)}, u32[]{:S(2)}) async-start(bf16[16,368,128]{2,1,0:T(8,128)(2,1)} %shard_map.79), calls=%async_computation.2 | async-start | bytes 3014656 | tf_op jit(solution)/shard_map/all_to_all | solution.py:365
  93.9 2.2 %copy-start.1 = (bf16[1,8,128,2,1024]{4,3,2,1,0:T(2,128)(2,1)S(1)}, bf16[1,8,128,2,1024]{4,3,2,1,0:T(2,128)(2,1)}, u32[]{:S(2)}) copy-start(bf16[1,8,128,2,1024]{4,3,2,1,0:T(2,128)(2,1)} %param.10) | copy-start | bytes 12582916

commit v8 on v6

--- a/solution.py
+++ b/solution.py
@@ -86,26 +86,24 @@
     return high, middle, low
 
 
-def shared_kernel(place_ref, query_ref, pair_ref, out_ref, key_ref, value_ref):
+def shared_kernel(
+    listed_ref, query_ref, pair_ref, out_ref, key_ref, value_ref, wide_ref, place_ref, list_sem
+):
     pieces = pair_ref.shape[0]
     samples = query_ref.shape[0]
     owners, rows = out_ref.shape[0], pair_ref.shape[1]
     slots = pieces // owners
     local = samples // owners
 
-    row = lax.broadcasted_iota(jnp.int32, (256, 256), 0)
-    column = lax.broadcasted_iota(jnp.int32, (256, 256), 1)
-    wanted = jnp.where(row < 128, 2 * row, 2 * (row - 128) + 1)
-    pick = jnp.where(column == wanted, 1.0, 0.0).astype(jnp.bfloat16)
+    fetch = pltpu.make_async_copy(listed_ref, place_ref, list_sem)
+    fetch.start()
     for step in range(pieces // 16):
+        wide = step % wide_ref.shape[0]
         both = pair_ref[step * 16 : (step + 1) * 16].reshape(256, HEAD_FEATURES)
-        apart = jnp.dot(pick, both, preferred_element_type=jnp.float32).astype(jnp.bfloat16)
-        key_ref[step * 128 : (step + 1) * 128, :] = apart[:128]
-        value_ref[step * 128 : (step + 1) * 128, :] = apart[128:]
-        for n in range(step * 16, (step + 1) * 16):
-            row = n % slots * rows
-            out_ref[n // slots, row : row + rows, :] = pair_ref[place_ref[n]]
-
+        wide_ref[wide] = both.astype(jnp.float32)
+        here = slice(step * 128, (step + 1) * 128)
+        key_ref[here, :] = wide_ref[wide, pl.ds(0, 128, stride=2), :].astype(jnp.bfloat16)
+        value_ref[here, :] = wide_ref[wide, pl.ds(1, 128, stride=2), :].astype(jnp.bfloat16)
     factor = SCALE * math.log2(math.e)
     lane = lax.broadcasted_iota(jnp.int32, (samples, 128), 1)
     peaks = jnp.zeros((samples, 128), jnp.float32)
@@ -129,10 +127,14 @@
         )
 
     later = scores_of(0)
+    fetch.wait()
     for g in range(0, GROUP, 2):
         scores = later
         if g + 2 < GROUP:
             later = scores_of(g + 2)
+        for n in range(g * pieces // GROUP, (g + 2) * pieces // GROUP):
+            row = n % slots * rows
+            out_ref[n // slots, row : row + rows, :] = pair_ref[place_ref[n]]
         top = jnp.max(scores, axis=-1, keepdims=True)
         weights = jnp.exp2((scores - top) * factor)
         total = jnp.sum(weights, axis=-1, keepdims=True)
@@ -164,7 +166,7 @@
         shared_kernel,
         out_shape=jax.ShapeDtypeStruct((owners, sent, features), jnp.bfloat16),
         in_specs=[
-            pl.BlockSpec(memory_space=pltpu.SMEM),
+            pl.BlockSpec(memory_space=pl.ANY),
             pl.BlockSpec(memory_space=pltpu.VMEM),
             pl.BlockSpec(memory_space=pltpu.VMEM),
         ],
@@ -172,6 +174,9 @@
         scratch_shapes=[
             pltpu.VMEM((tokens, features), jnp.bfloat16),
             pltpu.VMEM((tokens, features), jnp.bfloat16),
+            pltpu.VMEM((4, 256, features), jnp.float32),
+            pltpu.SMEM((pieces,), jnp.int32),
+            pltpu.SemaphoreType.DMA,
         ],
         compiler_params=pltpu.CompilerParams(vmem_limit_bytes=40 * 1024 * 1024),
         cost_estimate=pl.CostEstimate(
@@ -278,42 +283,56 @@
     )(tiles, came, *own)
 
 
-def choose_kernel(match_ref, page_ref, out_ref, held_ref, sems):
+def choose_kernel(listed_ref, page_ref, out_ref, held_ref, reader_ref, sems, list_sem):
+    fetch = pltpu.make_async_copy(listed_ref, reader_ref, list_sem)
+    fetch.start()
     copies = []
-    for instance in range(out_ref.shape[0]):
-        page = page_ref[match_ref[instance]]
+    sources = page_ref.shape[0]
+    for source in range(sources):
+        page = page_ref[source]
         for head in range(KEY_VALUE_HEADS):
-            held_ref[instance, head] = page[
-                :, :, head * HEAD_FEATURES : (head + 1) * HEAD_FEATURES
-            ]
+            held_ref[source, head] = page[:, :, head * HEAD_FEATURES : (head + 1) * HEAD_FEATURES]
         copies.append(
-            pltpu.make_async_copy(held_ref.at[instance], out_ref.at[instance], sems.at[instance])
+            lambda source=source: pltpu.make_async_copy(
+                held_ref.at[source], out_ref.at[reader_ref[source]], sems.at[source]
+            )
         )
-        copies[-1].start()
+        if source == sources * 5 // 8:
+            fetch.wait()
+            for copy in copies:
+                copy().start()
+        elif source > sources * 5 // 8:
+            copies[-1]().start()
     for copy in copies:
-        copy.wait()
+        copy().wait()
 
 
 def choose(match, pages):
     instances, tokens = pages.shape[:2]
+    sources = jnp.arange(instances, dtype=match.dtype)
+    reader = jnp.sum(
+        jnp.where(match[None, :] == sources[:, None], sources[None, :], 0), axis=1, dtype=match.dtype
+    )
     shape = (instances, KEY_VALUE_HEADS, tokens, 2, HEAD_FEATURES)
     return pl.pallas_call(
         choose_kernel,
         out_shape=jax.ShapeDtypeStruct(shape, pages.dtype),
         in_specs=[
-            pl.BlockSpec(memory_space=pltpu.SMEM),
+            pl.BlockSpec(memory_space=pl.ANY),
             pl.BlockSpec(memory_space=pltpu.VMEM),
         ],
         out_specs=pl.BlockSpec(memory_space=pl.ANY),
         scratch_shapes=[
             pltpu.VMEM(shape, pages.dtype),
+            pltpu.SMEM((instances,), jnp.int32),
             pltpu.SemaphoreType.DMA((instances,)),
+            pltpu.SemaphoreType.DMA,
         ],
         compiler_params=pltpu.CompilerParams(vmem_limit_bytes=16 * 1024 * 1024),
         cost_estimate=pl.CostEstimate(
             flops=0, bytes_accessed=4 * 1024 * 1024, transcendentals=0
         ),
-    )(match, pages)
+    )(reader, pages)
 
 
 def exchange(held, member, n_samp, place, axis):

time: 114 us -> 113 us (level)
    ppermute x4, waiting for transfers between devices: 7.45 us -> 5.86 us  [exchange(): lax.ppermute(sent, 'samp', [(i, i ^ 1 << place) for i in range(n_samp)])]
    all_to_all x1, waiting for transfers between devices: 2.69 us -> 4.16 us  [body(): lax.all_to_all(prompt_key_values, 'inst', split_axis=1, concat_axis=0, ti...]
  transfers between devices with their start and end apart: 6 -> 6, of which waited for: 4 -> 4; matrix products, arithmetic and copies ran while one was open for 0% -> 1% of each run, Pallas kernels for 19% -> 19%
where the time goes in v8:
time: 113 us
  starting transfers between devices  31.1 us (28%)
  Pallas kernels  29.7 us (26%)
  blocking collectives  25.9 us (23%)
  waiting for transfers between devices  20.3 us (18%)
  local copies, waits for them, and re-layouts  4.7 us (4%)
    all_to_all x1, blocking collectives, body(): came = lax.all_to_all(sent, 'samp', split_axis=0, concat_axis=0, tiled=True)  25.9 us
    pallas_call x2, Pallas kernels, partial_own(): pl.pallas_call(functools.partial(own_kernel, which * heads), grid=(1,), o...  21.7 us
    all_to_all x1, starting transfers between devices, body(): lax.all_to_all(chosen, ('inst', 'samp'), split_axis=0, concat_axis=0, til...  11.1 us
    all_to_all x1, waiting for transfers between devices, body(): lax.all_to_all(chosen, ('inst', 'samp'), split_axis=0, concat_axis=0, til...  10.3 us
    all_to_all x1, starting transfers between devices, body(): lax.all_to_all(prompt_key_values, 'inst', split_axis=1, concat_axis=0, ti...  10.3 us
    ppermute x4, starting transfers between devices, exchange(): lax.ppermute(sent, 'samp', [(i, i ^ 1 << place) for i in range(n_samp)])  9.71 us
    ppermute x4, waiting for transfers between devices, exchange(): lax.ppermute(sent, 'samp', [(i, i ^ 1 << place) for i in range(n_samp)])  5.86 us
    pallas_call x1, Pallas kernels, partial_shared(): pl.pallas_call(shared_kernel, out_shape=jax.ShapeDtypeStruct((owners, sen...  4.53 us
  transfers between devices with their start and end apart: 6, of which 4 were waited for; matrix products, arithmetic and copies ran while one was open for 1% of the time, Pallas kernels for 19%

profile of v8, /device:TPU:1, one launch (start us, length us, event | category | flops | bytes accessed | tf_op | source)
XLA Modules:
  0.0 112.9 jit_solution(8238922660666670203)
XLA Ops:
  0.6 0.0 copy-start.3
  0.6 0.0 copy-start.2
  0.6 10.3 %all-to-all-start = ((bf16[1,256,2,1024]{3,2,0,1:T(2,128)(2,1)}), bf16[1,256,2,1024]{3,2,0,1:T(2,128)(2,1)S(1)}, u32[]{:S(2)}, u32[]{:S(2)}) async-start(bf16[1,256,2,1024]{3,2,0,1:T(2,128)(2,1)} %bitcast.50), calls=%async_computation | async-start | bytes 2097152 | tf_op jit(solution)/shard_map/all_to_all | solution.py:359
  10.9 0.0 copy-done.3
  11.0 2.7 %collective-permute-start = (bf16[4,8,1536]{2,1,0:T(8,128)(2,1)S(1)}, bf16[4,8,1536]{2,1,0:T(8,128)(2,1)S(1)}, u32[]{:S(2)}, u32[]{:S(2)}) collective-permute-start(bf16[4,8,1536]{2,1,0:T(8,128)(2,1)S(1)} %dynamic-slice_bitcast_fusion), channel_id=1, source_target_pairs={{0,8},{1,9},{2,10},{3,11},{4,12},{5,13},{6,14},{7,15},{8,0},{9,1},... | collective-permute-start | bytes 294920 | tf_op jit(solution)/shard_map/ppermute | solution.py:346
  13.7 0.2 reshape_squeeze.10
  13.8 0.1 pad.4.query_ref
  13.9 0.0 copy-done.2
  13.9 0.0 copy-start
  13.9 2.2 %copy-done = bf16[1,8,128,2,1024]{4,3,2,1,0:T(2,128)(2,1)S(1)} copy-done((bf16[1,8,128,2,1024]{4,3,2,1,0:T(2,128)(2,1)S(1)}, bf16[1,8,128,2,1024]{4,3,2,1,0:T(2,128)(2,1)}, u32[]{:S(2)}) %copy-start) | copy-done | bytes 4194328
  16.1 0.0 copy-start.5
  16.1 10.9 %shard_map.78 = (f32[4,12,8,128]{3,2,1,0:T(8,128)S(1)}, f32[4,2,8,128]{3,2,1,0:T(8,128)S(1)}) custom-call(s32[8]{0:T(128)S(1)} %bitcast.48, bf16[8,8,16,128]{3,2,1,0:T(8,128)(2,1)S(1)} %pad.4.query_ref, bf16[8,128,2,1024]{3,2,1,0:T(2,128)(2,1)S(1)} %bitcast.43), custom_call_target="tpu_custom_call" | custom-call | bytes 65536 | tf_op jit(solution)/shard_map/pallas_call | solution.py:60
  27.0 0.0 collective-permute-done
  27.1 2.8 %collective-permute-start.1 = (bf16[2,2,8,1536]{3,2,1,0:T(8,128)(2,1)S(1)}, bf16[2,2,8,1536]{3,2,1,0:T(8,128)(2,1)S(1)}, u32[]{:S(2)}, u32[]{:S(2)}) collective-permute-start(bf16[2,2,8,1536]{3,2,1,0:T(8,128)(2,1)S(1)} %fusion), channel_id=1, source_target_pairs={{0,4},{1,5},{2,6},{3,7},{4,0},{5,1},{6,2},{7,3},{8,12},{9,13},{10,... | collective-permute-start | bytes 294920 | tf_op jit(solution)/shard_map/ppermute | solution.py:346
  29.9 0.0 copy-done.5
  29.9 0.1 select_reduce_fusion.listed_ref
  30.0 2.4 %collective-permute-done.1 = bf16[2,2,8,1536]{3,2,1,0:T(8,128)(2,1)S(1)} collective-permute-done((bf16[2,2,8,1536]{3,2,1,0:T(8,128)(2,1)S(1)}, bf16[2,2,8,1536]{3,2,1,0:T(8,128)(2,1)S(1)}, u32[]{:S(2)}, u32[]{:S(2)}) %collective-permute-start.1) | collective-permute-done | bytes 98336 | tf_op jit(solution)/shard_map/ppermute | solution.py:346
  32.5 4.2 %all-to-all-done = bf16[1,256,2,1024]{3,2,0,1:T(2,128)(2,1)S(1)} async-done(((bf16[1,256,2,1024]{3,2,0,1:T(2,128)(2,1)}), bf16[1,256,2,1024]{3,2,0,1:T(2,128)(2,1)S(1)}, u32[]{:S(2)}, u32[]{:S(2)}) %all-to-all-start) | async-done | bytes 1048608 | tf_op jit(solution)/shard_map/all_to_all | solution.py:359
  36.6 1.6 %shard_map.77 = bf16[16,8,16,2,128]{4,3,2,1,0:T(2,128)(2,1)} custom-call(s32[16]{0:T(128)S(1)} %select_reduce_fusion.listed_ref, bf16[16,16,2,1024]{3,2,1,0:T(2,128)(2,1)S(1)} %bitcast.46), custom_call_target="tpu_custom_call" | custom-call | bytes 4194304 | tf_op jit(solution)/shard_map/pallas_call | solution.py:317
  38.3 0.0 copy-start.4
  38.3 11.1 %all-to-all-start.1 = ((bf16[256,16,128]{2,1,0:T(8,128)(2,1)}), bf16[256,16,128]{2,1,0:T(8,128)(2,1)S(1)}, u32[]{:S(2)}, u32[]{:S(2)}) async-start(bf16[256,16,128]{2,1,0:T(8,128)(2,1)} %bitcast.2), calls=%async_computation.1 | async-start | bytes 2097152 | tf_op jit(solution)/shard_map/all_to_all | solution.py:375
  49.5 1.5 %collective-permute-start.2 = (bf16[1,2,2,8,1536]{4,3,2,1,0:T(8,128)(2,1)S(1)}, bf16[1,2,2,8,1536]{4,3,2,1,0:T(8,128)(2,1)S(1)}, u32[]{:S(2)}, u32[]{:S(2)}) collective-permute-start(bf16[1,2,2,8,1536]{4,3,2,1,0:T(8,128)(2,1)S(1)} %constant_dynamic-slice_fusion), channel_id=1, source_target_pairs={{0,2},{1,3},{2,0},{3,1},{4,6},{5,7},{6,4},{7,5},{8,10},{9,11},{10,... | collective-permute-start | bytes 294920 | tf_op jit(solution)/shard_map/ppermute | solution.py:346
  50.9 0.0 copy-done.4
  50.9 0.1 reshape_squeeze.11
  51.0 3.4 %collective-permute-done.2 = bf16[1,2,2,8,1536]{4,3,2,1,0:T(8,128)(2,1)S(1)} collective-permute-done((bf16[1,2,2,8,1536]{4,3,2,1,0:T(8,128)(2,1)S(1)}, bf16[1,2,2,8,1536]{4,3,2,1,0:T(8,128)(2,1)S(1)}, u32[]{:S(2)}, u32[]{:S(2)}) %collective-permute-start.2) | collective-permute-done | bytes 98336 | tf_op jit(solution)/shard_map/ppermute | solution.py:346
  54.5 2.7 %collective-permute-start.3 = (bf16[1,2,2,2,8,1536]{5,4,3,2,1,0:T(8,128)(2,1)S(1)}, bf16[1,2,2,2,8,1536]{5,4,3,2,1,0:T(8,128)(2,1)S(1)}, u32[]{:S(2)}, u32[]{:S(2)}) collective-permute-start(bf16[1,2,2,2,8,1536]{5,4,3,2,1,0:T(8,128)(2,1)S(1)} %pad_maximum_fusion.2), channel_id=1, source_target_pairs={{0,1},{1,0},{2,3},{3,2},{4,5},{5,4},{6,7},{7,6},{8,9},{9,8},{10,11... | collective-permute-start | bytes 589832 | tf_op jit(solution)/shard_map/ppermute | solution.py:346
  57.2 0.0 copy-start.1
  57.2 2.2 %copy-done.1 = bf16[1,8,128,2,1024]{4,3,2,1,0:T(2,128)(2,1)S(1)} copy-done((bf16[1,8,128,2,1024]{4,3,2,1,0:T(2,128)(2,1)S(1)}, bf16[1,8,128,2,1024]{4,3,2,1,0:T(2,128)(2,1)}, u32[]{:S(2)}) %copy-start.1) | copy-done | bytes 4194328
  59.4 10.9 %shard_map.79 = (f32[4,12,8,128]{3,2,1,0:T(8,128)S(1)}, f32[4,2,8,128]{3,2,1,0:T(8,128)S(1)}) custom-call(s32[8]{0:T(128)S(1)} %bitcast.49, bf16[8,8,16,128]{3,2,1,0:T(8,128)(2,1)S(1)} %pad.4.query_ref, bf16[8,128,2,1024]{3,2,1,0:T(2,128)(2,1)S(1)} %bitcast.44), custom_call_target="tpu_custom_call" | custom-call | bytes 65536 | tf_op jit(solution)/shard_map/pallas_call | solution.py:60
  70.3 0.0 collective-permute-done.3
  70.4 10.3 %all-to-all-done.1.pair_ref = bf16[256,16,128]{2,1,0:T(8,128)(2,1)S(1)} async-done(((bf16[256,16,128]{2,1,0:T(8,128)(2,1)}), bf16[256,16,128]{2,1,0:T(8,128)(2,1)S(1)}, u32[]{:S(2)}, u32[]{:S(2)}) %all-to-all-start.1) | async-done | bytes 1048608 | tf_op jit(solution)/shard_map/all_to_all | solution.py:375
  80.7 4.5 %shard_map.80 = bf16[16,368,128]{2,1,0:T(8,128)(2,1)S(1)} custom-call(s32[256]{0:T(256)S(1)} %fusion.5.listed_ref, bf16[128,1536]{1,0:T(8,128)(2,1)S(1)} %bitcast.47, bf16[256,16,128]{2,1,0:T(8,128)(2,1)S(1)} %all-to-all-done.1.pair_ref), custom_call_target="tpu_custom_call" | custom-call | flops 1610612736 | bytes 4194304 | tf_op jit(solution)/shard_map/pallas_call | solution.py:165
  85.2 25.9 %all_to_all.22.came_ref = bf16[16,368,128]{2,1,0:T(8,128)(2,1)S(1)} all-to-all(bf16[16,368,128]{2,1,0:T(8,128)(2,1)S(1)} %shard_map.80), channel_id=1, replica_groups=mesh['inst'=16,'samp'=16] {'samp'}, dimensions={0} | all-to-all | bytes 3014656 | tf_op jit(solution)/shard_map/all_to_all | solution.py:384
  111.1 1.8 %shard_map.81 = (bf16[8,12288]{1,0:T(8,128)(2,1)}, bf16[16,16,2,1024]{3,2,1,0:T(2,128)(2,1)}) custom-call(bf16[16,23,8,2,128]{4,3,2,1,0:T(2,128)(2,1)S(1)} %bitcast.45, bf16[16,368,128]{2,1,0:T(8,128)(2,1)S(1)} %all_to_all.22.came_ref, f32[4,12,8,128]{3,2,1,0:T(8,128)S(1)} %get-tuple-element.32.refs_0_, f32[4,2,8,128]{3,2,1,0:T(8,128)S(1)} %get-tuple-element.33.refs_1_, ...), custom_call_target="tpu_custom_call" | custom-call | flops 589824 | bytes 4194304 | tf_op jit(solution)/shard_map/pallas_call | solution.py:263
  (11 shorter events, 0.2 us)
Async XLA Ops:
  0.6 10.3 %copy-start.3 = (bf16[1,8,12288]{2,1,0:T(8,128)(2,1)S(1)}, bf16[1,8,12288]{2,1,0:T(8,128)(2,1)}, u32[]{:S(2)}) copy-start(bf16[1,8,12288]{2,1,0:T(8,128)(2,1)} %param.9) | copy-start | bytes 589828
  0.6 13.3 %copy-start.2 = (s32[1,8]{1,0:T(1,128)S(1)}, s32[1,8]{1,0:T(1,128)}, u32[]{:S(2)}) copy-start(s32[1,8]{1,0:T(1,128)} %param.11) | copy-start | bytes 100
  0.6 36.0 %all-to-all-start = ((bf16[1,256,2,1024]{3,2,0,1:T(2,128)(2,1)}), bf16[1,256,2,1024]{3,2,0,1:T(2,128)(2,1)S(1)}, u32[]{:S(2)}, u32[]{:S(2)}) async-start(bf16[1,256,2,1024]{3,2,0,1:T(2,128)(2,1)} %bitcast.50), calls=%async_computation | async-start | bytes 2097152 | tf_op jit(solution)/shard_map/all_to_all | solution.py:359
  11.0 16.0 %collective-permute-start = (bf16[4,8,1536]{2,1,0:T(8,128)(2,1)S(1)}, bf16[4,8,1536]{2,1,0:T(8,128)(2,1)S(1)}, u32[]{:S(2)}, u32[]{:S(2)}) collective-permute-start(bf16[4,8,1536]{2,1,0:T(8,128)(2,1)S(1)} %dynamic-slice_bitcast_fusion), channel_id=1, source_target_pairs={{0,8},{1,9},{2,10},{3,11},{4,12},{5,13},{6,14},{7,15},{8,0},{9,1},... | collective-permute-start | bytes 294920 | tf_op jit(solution)/shard_map/ppermute | solution.py:346
  13.9 2.2 %copy-start = (bf16[1,8,128,2,1024]{4,3,2,1,0:T(2,128)(2,1)S(1)}, bf16[1,8,128,2,1024]{4,3,2,1,0:T(2,128)(2,1)}, u32[]{:S(2)}) copy-start(bf16[1,8,128,2,1024]{4,3,2,1,0:T(2,128)(2,1)} %param.10) | copy-start | bytes 12582916
  16.1 13.8 %copy-start.5 = (s32[16]{0:T(128)S(1)}, s32[16]{0:T(128)}, u32[]{:S(2)}) copy-start(s32[16]{0:T(128)} %param.7) | copy-start | bytes 196
  27.1 5.4 %collective-permute-start.1 = (bf16[2,2,8,1536]{3,2,1,0:T(8,128)(2,1)S(1)}, bf16[2,2,8,1536]{3,2,1,0:T(8,128)(2,1)S(1)}, u32[]{:S(2)}, u32[]{:S(2)}) collective-permute-start(bf16[2,2,8,1536]{3,2,1,0:T(8,128)(2,1)S(1)} %fusion), channel_id=1, source_target_pairs={{0,4},{1,5},{2,6},{3,7},{4,0},{5,1},{6,2},{7,3},{8,12},{9,13},{10,... | collective-permute-start | bytes 294920 | tf_op jit(solution)/shard_map/ppermute | solution.py:346
  38.3 12.7 %copy-start.4 = (s32[1,16,16]{2,1,0:T(8,128)S(1)}, s32[1,16,16]{2,1,0:T(8,128)}, u32[]{:S(2)}) copy-start(s32[1,16,16]{2,1,0:T(8,128)} %param.8) | copy-start | bytes 3076
  38.3 42.4 %all-to-all-start.1 = ((bf16[256,16,128]{2,1,0:T(8,128)(2,1)}), bf16[256,16,128]{2,1,0:T(8,128)(2,1)S(1)}, u32[]{:S(2)}, u32[]{:S(2)}) async-start(bf16[256,16,128]{2,1,0:T(8,128)(2,1)} %bitcast.2), calls=%async_computation.1 | async-start | bytes 2097152 | tf_op jit(solution)/shard_map/all_to_all | solution.py:375
  49.5 5.0 %collective-permute-start.2 = (bf16[1,2,2,8,1536]{4,3,2,1,0:T(8,128)(2,1)S(1)}, bf16[1,2,2,8,1536]{4,3,2,1,0:T(8,128)(2,1)S(1)}, u32[]{:S(2)}, u32[]{:S(2)}) collective-permute-start(bf16[1,2,2,8,1536]{4,3,2,1,0:T(8,128)(2,1)S(1)} %constant_dynamic-slice_fusion), channel_id=1, source_target_pairs={{0,2},{1,3},{2,0},{3,1},{4,6},{5,7},{6,4},{7,5},{8,10},{9,11},{10,... | collective-permute-start | bytes 294920 | tf_op jit(solution)/shard_map/ppermute | solution.py:346
  54.5 15.8 %collective-permute-start.3 = (bf16[1,2,2,2,8,1536]{5,4,3,2,1,0:T(8,128)(2,1)S(1)}, bf16[1,2,2,2,8,1536]{5,4,3,2,1,0:T(8,128)(2,1)S(1)}, u32[]{:S(2)}, u32[]{:S(2)}) collective-permute-start(bf16[1,2,2,2,8,1536]{5,4,3,2,1,0:T(8,128)(2,1)S(1)} %pad_maximum_fusion.2), channel_id=1, source_target_pairs={{0,1},{1,0},{2,3},{3,2},{4,5},{5,4},{6,7},{7,6},{8,9},{9,8},{10,11... | collective-permute-start | bytes 589832 | tf_op jit(solution)/shard_map/ppermute | solution.py:346
  57.2 2.2 %copy-start.1 = (bf16[1,8,128,2,1024]{4,3,2,1,0:T(2,128)(2,1)S(1)}, bf16[1,8,128,2,1024]{4,3,2,1,0:T(2,128)(2,1)}, u32[]{:S(2)}) copy-start(bf16[1,8,128,2,1024]{4,3,2,1,0:T(2,128)(2,1)} %param.10) | copy-start | bytes 12582916

commit v9 on v8

--- a/solution.py
+++ b/solution.py
@@ -283,56 +283,31 @@
     )(tiles, came, *own)
 
 
-def choose_kernel(listed_ref, page_ref, out_ref, held_ref, reader_ref, sems, list_sem):
-    fetch = pltpu.make_async_copy(listed_ref, reader_ref, list_sem)
-    fetch.start()
-    copies = []
-    sources = page_ref.shape[0]
-    for source in range(sources):
-        page = page_ref[source]
+def choose_kernel(match_ref, page_ref, out_ref):
+    for instance in range(out_ref.shape[0]):
+        page = page_ref[match_ref[instance]]
         for head in range(KEY_VALUE_HEADS):
-            held_ref[source, head] = page[:, :, head * HEAD_FEATURES : (head + 1) * HEAD_FEATURES]
-        copies.append(
-            lambda source=source: pltpu.make_async_copy(
-                held_ref.at[source], out_ref.at[reader_ref[source]], sems.at[source]
-            )
-        )
-        if source == sources * 5 // 8:
-            fetch.wait()
-            for copy in copies:
-                copy().start()
-        elif source > sources * 5 // 8:
-            copies[-1]().start()
-    for copy in copies:
-        copy().wait()
+            out_ref[instance, head] = page[
+                :, :, head * HEAD_FEATURES : (head + 1) * HEAD_FEATURES
+            ]
 
 
 def choose(match, pages):
     instances, tokens = pages.shape[:2]
-    sources = jnp.arange(instances, dtype=match.dtype)
-    reader = jnp.sum(
-        jnp.where(match[None, :] == sources[:, None], sources[None, :], 0), axis=1, dtype=match.dtype
-    )
     shape = (instances, KEY_VALUE_HEADS, tokens, 2, HEAD_FEATURES)
     return pl.pallas_call(
         choose_kernel,
-        out_shape=jax.ShapeDtypeStruct(shape, pages.dtype),
+        out_shape=pltpu.VMEM(shape, pages.dtype),
         in_specs=[
-            pl.BlockSpec(memory_space=pl.ANY),
+            pl.BlockSpec(memory_space=pltpu.SMEM),
             pl.BlockSpec(memory_space=pltpu.VMEM),
         ],
-        out_specs=pl.BlockSpec(memory_space=pl.ANY),
-        scratch_shapes=[
-            pltpu.VMEM(shape, pages.dtype),
-            pltpu.SMEM((instances,), jnp.int32),
-            pltpu.SemaphoreType.DMA((instances,)),
-            pltpu.SemaphoreType.DMA,
-        ],
+        out_specs=pl.BlockSpec(memory_space=pltpu.VMEM),
         compiler_params=pltpu.CompilerParams(vmem_limit_bytes=16 * 1024 * 1024),
         cost_estimate=pl.CostEstimate(
             flops=0, bytes_accessed=4 * 1024 * 1024, transcendentals=0
         ),
-    )(reader, pages)
+    )(match, pages)
 
 
 def exchange(held, member, n_samp, place, axis):

time: 113 us -> 114 us (level)
    ppermute x4, waiting for transfers between devices: 5.86 us -> 7.45 us  [exchange(): lax.ppermute(sent, 'samp', [(i, i ^ 1 << place) for i in range(n_samp)])]
    all_to_all x1, waiting for transfers between devices: 4.16 us -> 2.69 us  [body(): lax.all_to_all(prompt_key_values, 'inst', split_axis=1, concat_axis=0, ti...]
  transfers between devices with their start and end apart: 6 -> 6, of which waited for: 4 -> 4; matrix products, arithmetic and copies ran while one was open for 1% -> 0% of each run, Pallas kernels for 19% -> 19%
where the time goes in v9:
time: 114 us; the launch traced here: 113 us
  starting transfers between devices  31.1 us (27%)
  Pallas kernels  30.1 us (26%)
  blocking collectives  25.9 us (23%)
  waiting for transfers between devices  20.4 us (18%)
  local copies, waits for them, and re-layouts  4.7 us (4%)
    all_to_all x1, blocking collectives, body(): came = lax.all_to_all(sent, 'samp', split_axis=0, concat_axis=0, tiled=True)  25.9 us
    pallas_call x2, Pallas kernels, partial_own(): pl.pallas_call(functools.partial(own_kernel, which * heads), grid=(1,), o...  21.7 us
    all_to_all x1, starting transfers between devices, body(): lax.all_to_all(chosen, ('inst', 'samp'), split_axis=0, concat_axis=0, til...  11.1 us
    all_to_all x1, waiting for transfers between devices, body(): lax.all_to_all(chosen, ('inst', 'samp'), split_axis=0, concat_axis=0, til...  10.3 us
    all_to_all x1, starting transfers between devices, body(): lax.all_to_all(prompt_key_values, 'inst', split_axis=1, concat_axis=0, ti...  10.3 us
    ppermute x4, starting transfers between devices, exchange(): lax.ppermute(sent, 'samp', [(i, i ^ 1 << place) for i in range(n_samp)])  9.71 us
    ppermute x4, waiting for transfers between devices, exchange(): lax.ppermute(sent, 'samp', [(i, i ^ 1 << place) for i in range(n_samp)])  7.45 us
    pallas_call x1, Pallas kernels, partial_shared(): pl.pallas_call(shared_kernel, out_shape=jax.ShapeDtypeStruct((owners, sen...  4.54 us
  transfers between devices with their start and end apart: 6, of which 4 were waited for; matrix products, arithmetic and copies ran while one was open for 0% of the time, Pallas kernels for 19%

profile of v9, /device:TPU:1, one launch (start us, length us, event | category | flops | bytes accessed | tf_op | source)
XLA Modules:
  0.0 113.3 jit_solution(3489494085311321424)
XLA Ops:
  0.6 0.0 copy-start.4
  0.6 0.0 copy-start.2
  0.6 10.3 %all-to-all-start = ((bf16[1,256,2,1024]{3,2,0,1:T(2,128)(2,1)}), bf16[1,256,2,1024]{3,2,0,1:T(2,128)(2,1)S(1)}, u32[]{:S(2)}, u32[]{:S(2)}) async-start(bf16[1,256,2,1024]{3,2,0,1:T(2,128)(2,1)} %bitcast.50), calls=%async_computation | async-start | bytes 2097152 | tf_op jit(solution)/shard_map/all_to_all | solution.py:334
  10.9 0.0 copy-done.4
  11.0 2.7 %collective-permute-start = (bf16[4,8,1536]{2,1,0:T(8,128)(2,1)S(1)}, bf16[4,8,1536]{2,1,0:T(8,128)(2,1)S(1)}, u32[]{:S(2)}, u32[]{:S(2)}) collective-permute-start(bf16[4,8,1536]{2,1,0:T(8,128)(2,1)S(1)} %dynamic-slice_bitcast_fusion), channel_id=1, source_target_pairs={{0,8},{1,9},{2,10},{3,11},{4,12},{5,13},{6,14},{7,15},{8,0},{9,1},... | collective-permute-start | bytes 294920 | tf_op jit(solution)/shard_map/ppermute | solution.py:321
  13.7 4.0 %collective-permute-done = bf16[4,8,1536]{2,1,0:T(8,128)(2,1)S(1)} collective-permute-done((bf16[4,8,1536]{2,1,0:T(8,128)(2,1)S(1)}, bf16[4,8,1536]{2,1,0:T(8,128)(2,1)S(1)}, u32[]{:S(2)}, u32[]{:S(2)}) %collective-permute-start) | collective-permute-done | bytes 98336 | tf_op jit(solution)/shard_map/ppermute | solution.py:321
  17.7 2.8 %collective-permute-start.1 = (bf16[2,2,8,1536]{3,2,1,0:T(8,128)(2,1)S(1)}, bf16[2,2,8,1536]{3,2,1,0:T(8,128)(2,1)S(1)}, u32[]{:S(2)}, u32[]{:S(2)}) collective-permute-start(bf16[2,2,8,1536]{3,2,1,0:T(8,128)(2,1)S(1)} %fusion), channel_id=1, source_target_pairs={{0,4},{1,5},{2,6},{3,7},{4,0},{5,1},{6,2},{7,3},{8,12},{9,13},{10,... | collective-permute-start | bytes 294920 | tf_op jit(solution)/shard_map/ppermute | solution.py:321
  20.6 0.2 reshape_squeeze.10
  20.7 0.1 pad.4.query_ref
  20.8 0.0 copy-done.2
  20.8 0.0 copy-start
  20.8 2.2 %copy-done = bf16[1,8,128,2,1024]{4,3,2,1,0:T(2,128)(2,1)S(1)} copy-done((bf16[1,8,128,2,1024]{4,3,2,1,0:T(2,128)(2,1)S(1)}, bf16[1,8,128,2,1024]{4,3,2,1,0:T(2,128)(2,1)}, u32[]{:S(2)}) %copy-start) | copy-done | bytes 4194328
  23.0 0.0 copy-start.3
  23.0 10.9 %shard_map.78 = (f32[4,12,8,128]{3,2,1,0:T(8,128)S(1)}, f32[4,2,8,128]{3,2,1,0:T(8,128)S(1)}) custom-call(s32[8]{0:T(128)S(1)} %bitcast.48, bf16[8,8,16,128]{3,2,1,0:T(8,128)(2,1)S(1)} %pad.4.query_ref, bf16[8,128,2,1024]{3,2,1,0:T(2,128)(2,1)S(1)} %bitcast.43), custom_call_target="tpu_custom_call" | custom-call | bytes 65536 | tf_op jit(solution)/shard_map/pallas_call | solution.py:60
  33.9 0.0 collective-permute-done.1
  33.9 2.7 %all-to-all-done = bf16[1,256,2,1024]{3,2,0,1:T(2,128)(2,1)S(1)} async-done(((bf16[1,256,2,1024]{3,2,0,1:T(2,128)(2,1)}), bf16[1,256,2,1024]{3,2,0,1:T(2,128)(2,1)S(1)}, u32[]{:S(2)}, u32[]{:S(2)}) %all-to-all-start) | async-done | bytes 1048608 | tf_op jit(solution)/shard_map/all_to_all | solution.py:334
  36.6 0.0 copy-done.3
  36.6 2.1 %shard_map.77 = bf16[16,8,16,2,128]{4,3,2,1,0:T(2,128)(2,1)} custom-call(s32[16]{0:T(128)S(1)} %copy-done.3, bf16[16,16,2,1024]{3,2,1,0:T(2,128)(2,1)S(1)} %bitcast.46), custom_call_target="tpu_custom_call" | custom-call | bytes 4194304 | tf_op jit(solution)/shard_map/pallas_call | solution.py:298
  38.7 0.0 copy-start.5
  38.7 11.1 %all-to-all-start.1 = ((bf16[256,16,128]{2,1,0:T(8,128)(2,1)}), bf16[256,16,128]{2,1,0:T(8,128)(2,1)S(1)}, u32[]{:S(2)}, u32[]{:S(2)}) async-start(bf16[256,16,128]{2,1,0:T(8,128)(2,1)} %bitcast.2), calls=%async_computation.1 | async-start | bytes 2097152 | tf_op jit(solution)/shard_map/all_to_all | solution.py:350
  49.9 1.5 %collective-permute-start.2 = (bf16[1,2,2,8,1536]{4,3,2,1,0:T(8,128)(2,1)S(1)}, bf16[1,2,2,8,1536]{4,3,2,1,0:T(8,128)(2,1)S(1)}, u32[]{:S(2)}, u32[]{:S(2)}) collective-permute-start(bf16[1,2,2,8,1536]{4,3,2,1,0:T(8,128)(2,1)S(1)} %constant_dynamic-slice_fusion), channel_id=1, source_target_pairs={{0,2},{1,3},{2,0},{3,1},{4,6},{5,7},{6,4},{7,5},{8,10},{9,11},{10,... | collective-permute-start | bytes 294920 | tf_op jit(solution)/shard_map/ppermute | solution.py:321
  51.4 0.0 copy-done.5
  51.4 0.1 reshape_squeeze.11
  51.4 3.4 %collective-permute-done.2 = bf16[1,2,2,8,1536]{4,3,2,1,0:T(8,128)(2,1)S(1)} collective-permute-done((bf16[1,2,2,8,1536]{4,3,2,1,0:T(8,128)(2,1)S(1)}, bf16[1,2,2,8,1536]{4,3,2,1,0:T(8,128)(2,1)S(1)}, u32[]{:S(2)}, u32[]{:S(2)}) %collective-permute-start.2) | collective-permute-done | bytes 98336 | tf_op jit(solution)/shard_map/ppermute | solution.py:321
  54.9 2.7 %collective-permute-start.3 = (bf16[1,2,2,2,8,1536]{5,4,3,2,1,0:T(8,128)(2,1)S(1)}, bf16[1,2,2,2,8,1536]{5,4,3,2,1,0:T(8,128)(2,1)S(1)}, u32[]{:S(2)}, u32[]{:S(2)}) collective-permute-start(bf16[1,2,2,2,8,1536]{5,4,3,2,1,0:T(8,128)(2,1)S(1)} %pad_maximum_fusion.2), channel_id=1, source_target_pairs={{0,1},{1,0},{2,3},{3,2},{4,5},{5,4},{6,7},{7,6},{8,9},{9,8},{10,11... | collective-permute-start | bytes 589832 | tf_op jit(solution)/shard_map/ppermute | solution.py:321
  57.7 0.0 copy-start.1
  57.7 2.2 %copy-done.1 = bf16[1,8,128,2,1024]{4,3,2,1,0:T(2,128)(2,1)S(1)} copy-done((bf16[1,8,128,2,1024]{4,3,2,1,0:T(2,128)(2,1)S(1)}, bf16[1,8,128,2,1024]{4,3,2,1,0:T(2,128)(2,1)}, u32[]{:S(2)}) %copy-start.1) | copy-done | bytes 4194328
  59.8 10.9 %shard_map.79 = (f32[4,12,8,128]{3,2,1,0:T(8,128)S(1)}, f32[4,2,8,128]{3,2,1,0:T(8,128)S(1)}) custom-call(s32[8]{0:T(128)S(1)} %bitcast.49, bf16[8,8,16,128]{3,2,1,0:T(8,128)(2,1)S(1)} %pad.4.query_ref, bf16[8,128,2,1024]{3,2,1,0:T(2,128)(2,1)S(1)} %bitcast.44), custom_call_target="tpu_custom_call" | custom-call | bytes 65536 | tf_op jit(solution)/shard_map/pallas_call | solution.py:60
  70.7 0.0 collective-permute-done.3
  70.8 10.3 %all-to-all-done.1.pair_ref = bf16[256,16,128]{2,1,0:T(8,128)(2,1)S(1)} async-done(((bf16[256,16,128]{2,1,0:T(8,128)(2,1)}), bf16[256,16,128]{2,1,0:T(8,128)(2,1)S(1)}, u32[]{:S(2)}, u32[]{:S(2)}) %all-to-all-start.1) | async-done | bytes 1048608 | tf_op jit(solution)/shard_map/all_to_all | solution.py:350
  81.1 4.5 %shard_map.80 = bf16[16,368,128]{2,1,0:T(8,128)(2,1)S(1)} custom-call(s32[256]{0:T(256)S(1)} %fusion.5.listed_ref, bf16[128,1536]{1,0:T(8,128)(2,1)S(1)} %bitcast.47, bf16[256,16,128]{2,1,0:T(8,128)(2,1)S(1)} %all-to-all-done.1.pair_ref), custom_call_target="tpu_custom_call" | custom-call | flops 1610612736 | bytes 4194304 | tf_op jit(solution)/shard_map/pallas_call | solution.py:165
  85.7 25.9 %all_to_all.22.came_ref = bf16[16,368,128]{2,1,0:T(8,128)(2,1)S(1)} all-to-all(bf16[16,368,128]{2,1,0:T(8,128)(2,1)S(1)} %shard_map.80), channel_id=1, replica_groups=mesh['inst'=16,'samp'=16] {'samp'}, dimensions={0} | all-to-all | bytes 3014656 | tf_op jit(solution)/shard_map/all_to_all | solution.py:359
  111.5 1.8 %shard_map.81 = (bf16[8,12288]{1,0:T(8,128)(2,1)}, bf16[16,16,2,1024]{3,2,1,0:T(2,128)(2,1)}) custom-call(bf16[16,23,8,2,128]{4,3,2,1,0:T(2,128)(2,1)S(1)} %bitcast.45, bf16[16,368,128]{2,1,0:T(8,128)(2,1)S(1)} %all_to_all.22.came_ref, f32[4,12,8,128]{3,2,1,0:T(8,128)S(1)} %get-tuple-element.32.refs_0_, f32[4,2,8,128]{3,2,1,0:T(8,128)S(1)} %get-tuple-element.33.refs_1_, ...), custom_call_target="tpu_custom_call" | custom-call | flops 589824 | bytes 4194304 | tf_op jit(solution)/shard_map/pallas_call | solution.py:263
  (11 shorter events, 0.2 us)
Async XLA Ops:
  0.6 10.3 %copy-start.4 = (bf16[1,8,12288]{2,1,0:T(8,128)(2,1)S(1)}, bf16[1,8,12288]{2,1,0:T(8,128)(2,1)}, u32[]{:S(2)}) copy-start(bf16[1,8,12288]{2,1,0:T(8,128)(2,1)} %param.9) | copy-start | bytes 589828
  0.6 20.1 %copy-start.2 = (s32[1,8]{1,0:T(1,128)S(1)}, s32[1,8]{1,0:T(1,128)}, u32[]{:S(2)}) copy-start(s32[1,8]{1,0:T(1,128)} %param.11) | copy-start | bytes 100
  0.6 36.0 %all-to-all-start = ((bf16[1,256,2,1024]{3,2,0,1:T(2,128)(2,1)}), bf16[1,256,2,1024]{3,2,0,1:T(2,128)(2,1)S(1)}, u32[]{:S(2)}, u32[]{:S(2)}) async-start(bf16[1,256,2,1024]{3,2,0,1:T(2,128)(2,1)} %bitcast.50), calls=%async_computation | async-start | bytes 2097152 | tf_op jit(solution)/shard_map/all_to_all | solution.py:334
  11.0 6.7 %collective-permute-start = (bf16[4,8,1536]{2,1,0:T(8,128)(2,1)S(1)}, bf16[4,8,1536]{2,1,0:T(8,128)(2,1)S(1)}, u32[]{:S(2)}, u32[]{:S(2)}) collective-permute-start(bf16[4,8,1536]{2,1,0:T(8,128)(2,1)S(1)} %dynamic-slice_bitcast_fusion), channel_id=1, source_target_pairs={{0,8},{1,9},{2,10},{3,11},{4,12},{5,13},{6,14},{7,15},{8,0},{9,1},... | collective-permute-start | bytes 294920 | tf_op jit(solution)/shard_map/ppermute | solution.py:321
  17.7 16.1 %collective-permute-start.1 = (bf16[2,2,8,1536]{3,2,1,0:T(8,128)(2,1)S(1)}, bf16[2,2,8,1536]{3,2,1,0:T(8,128)(2,1)S(1)}, u32[]{:S(2)}, u32[]{:S(2)}) collective-permute-start(bf16[2,2,8,1536]{3,2,1,0:T(8,128)(2,1)S(1)} %fusion), channel_id=1, source_target_pairs={{0,4},{1,5},{2,6},{3,7},{4,0},{5,1},{6,2},{7,3},{8,12},{9,13},{10,... | collective-permute-start | bytes 294920 | tf_op jit(solution)/shard_map/ppermute | solution.py:321
  20.8 2.2 %copy-start = (bf16[1,8,128,2,1024]{4,3,2,1,0:T(2,128)(2,1)S(1)}, bf16[1,8,128,2,1024]{4,3,2,1,0:T(2,128)(2,1)}, u32[]{:S(2)}) copy-start(bf16[1,8,128,2,1024]{4,3,2,1,0:T(2,128)(2,1)} %param.10) | copy-start | bytes 12582916
  23.0 13.6 %copy-start.3 = (s32[16]{0:T(128)S(1)}, s32[16]{0:T(128)}, u32[]{:S(2)}) copy-start(s32[16]{0:T(128)} %match_ref.1) | copy-start | bytes 196
  38.7 12.6 %copy-start.5 = (s32[1,16,16]{2,1,0:T(8,128)S(1)}, s32[1,16,16]{2,1,0:T(8,128)}, u32[]{:S(2)}) copy-start(s32[1,16,16]{2,1,0:T(8,128)} %param.8) | copy-start | bytes 3076
  38.7 42.4 %all-to-all-start.1 = ((bf16[256,16,128]{2,1,0:T(8,128)(2,1)}), bf16[256,16,128]{2,1,0:T(8,128)(2,1)S(1)}, u32[]{:S(2)}, u32[]{:S(2)}) async-start(bf16[256,16,128]{2,1,0:T(8,128)(2,1)} %bitcast.2), calls=%async_computation.1 | async-start | bytes 2097152 | tf_op jit(solution)/shard_map/all_to_all | solution.py:350
  49.9 5.0 %collective-permute-start.2 = (bf16[1,2,2,8,1536]{4,3,2,1,0:T(8,128)(2,1)S(1)}, bf16[1,2,2,8,1536]{4,3,2,1,0:T(8,128)(2,1)S(1)}, u32[]{:S(2)}, u32[]{:S(2)}) collective-permute-start(bf16[1,2,2,8,1536]{4,3,2,1,0:T(8,128)(2,1)S(1)} %constant_dynamic-slice_fusion), channel_id=1, source_target_pairs={{0,2},{1,3},{2,0},{3,1},{4,6},{5,7},{6,4},{7,5},{8,10},{9,11},{10,... | collective-permute-start | bytes 294920 | tf_op jit(solution)/shard_map/ppermute | solution.py:321
  54.9 15.8 %collective-permute-start.3 = (bf16[1,2,2,2,8,1536]{5,4,3,2,1,0:T(8,128)(2,1)S(1)}, bf16[1,2,2,2,8,1536]{5,4,3,2,1,0:T(8,128)(2,1)S(1)}, u32[]{:S(2)}, u32[]{:S(2)}) collective-permute-start(bf16[1,2,2,2,8,1536]{5,4,3,2,1,0:T(8,128)(2,1)S(1)} %pad_maximum_fusion.2), channel_id=1, source_target_pairs={{0,1},{1,0},{2,3},{3,2},{4,5},{5,4},{6,7},{7,6},{8,9},{9,8},{10,11... | collective-permute-start | bytes 589832 | tf_op jit(solution)/shard_map/ppermute | solution.py:321
  57.7 2.2 %copy-start.1 = (bf16[1,8,128,2,1024]{4,3,2,1,0:T(2,128)(2,1)S(1)}, bf16[1,8,128,2,1024]{4,3,2,1,0:T(2,128)(2,1)}, u32[]{:S(2)}) copy-start(bf16[1,8,128,2,1024]{4,3,2,1,0:T(2,128)(2,1)} %param.10) | copy-start | bytes 12582916

commit v10 on v8

--- a/solution.py
+++ b/solution.py
@@ -188,7 +188,7 @@
 
 
 def finish_kernel(tile_ref, came_ref, *refs):
-    own_refs, (out_ref, pool_ref, sems) = refs[:-3], refs[-3:]
+    own_refs, (to_ref, pool_ref, out_ref, sems) = refs[:-4], refs[-4:]
     senders = came_ref.shape[0]
     slots = pool_ref.shape[0]
     local = out_ref.shape[0]
@@ -251,6 +251,14 @@
                 value = (mine[0] * by[0] + mine[1] * by[1]) + mine[2] * by[2]
                 column = (head * GROUP + g + k) * HEAD_FEATURES
                 out_ref[:, column : column + HEAD_FEATURES] = value.astype(jnp.bfloat16)
+        if head % 4 == 3:
+            columns = slice((head - 3) * WIDTH, (head + 1) * WIDTH)
+            copies.append(
+                pltpu.make_async_copy(
+                    out_ref.at[:, columns], to_ref.at[:, columns], sems.at[senders + head]
+                )
+            )
+            copies[-1].start()
 
     for copy in copies:
         copy.wait()
@@ -272,8 +280,11 @@
             pl.BlockSpec(memory_space=pl.ANY),
         ]
         + [pl.BlockSpec(memory_space=pltpu.VMEM)] * (1 + len(own)),
-        out_specs=(pl.BlockSpec(memory_space=pltpu.VMEM), pl.BlockSpec(memory_space=pl.ANY)),
-        scratch_shapes=[pltpu.SemaphoreType.DMA((senders,))],
+        out_specs=(pl.BlockSpec(memory_space=pl.ANY), pl.BlockSpec(memory_space=pl.ANY)),
+        scratch_shapes=[
+            pltpu.VMEM((local, QUERY_HEADS * HEAD_FEATURES), jnp.bfloat16),
+            pltpu.SemaphoreType.DMA((senders + KEY_VALUE_HEADS,)),
+        ],
         compiler_params=pltpu.CompilerParams(vmem_limit_bytes=32 * 1024 * 1024),
         cost_estimate=pl.CostEstimate(
             flops=6 * local * QUERY_HEADS * HEAD_FEATURES,

time: 113 us -> 113 us (level)
  no operation moved by 1% of the time
where the time goes in v10:
time: 113 us
  starting transfers between devices  31.1 us (28%)
  Pallas kernels  29.5 us (26%)
  blocking collectives  25.9 us (23%)
  waiting for transfers between devices  20.3 us (18%)
  local copies, waits for them, and re-layouts  4.7 us (4%)
    all_to_all x1, blocking collectives, body(): came = lax.all_to_all(sent, 'samp', split_axis=0, concat_axis=0, tiled=True)  25.9 us
    pallas_call x2, Pallas kernels, partial_own(): pl.pallas_call(functools.partial(own_kernel, which * heads), grid=(1,), o...  21.7 us
    all_to_all x1, starting transfers between devices, body(): lax.all_to_all(chosen, ('inst', 'samp'), split_axis=0, concat_axis=0, til...  11.1 us
    all_to_all x1, waiting for transfers between devices, body(): lax.all_to_all(chosen, ('inst', 'samp'), split_axis=0, concat_axis=0, til...  10.3 us
    all_to_all x1, starting transfers between devices, body(): lax.all_to_all(prompt_key_values, 'inst', split_axis=1, concat_axis=0, ti...  10.3 us
    ppermute x4, starting transfers between devices, exchange(): lax.ppermute(sent, 'samp', [(i, i ^ 1 << place) for i in range(n_samp)])  9.71 us
    ppermute x4, waiting for transfers between devices, exchange(): lax.ppermute(sent, 'samp', [(i, i ^ 1 << place) for i in range(n_samp)])  5.86 us
    pallas_call x1, Pallas kernels, partial_shared(): pl.pallas_call(shared_kernel, out_shape=jax.ShapeDtypeStruct((owners, sen...  4.53 us
  transfers between devices with their start and end apart: 6, of which 4 were waited for; matrix products, arithmetic and copies ran while one was open for 1% of the time, Pallas kernels for 19%

profile of v10, /device:TPU:1, one launch (start us, length us, event | category | flops | bytes accessed | tf_op | source)
XLA Modules:
  0.0 112.7 jit_solution(10893523759128538371)
XLA Ops:
  0.6 0.0 copy-start.3
  0.6 0.0 copy-start.2
  0.6 10.3 %all-to-all-start = ((bf16[1,256,2,1024]{3,2,0,1:T(2,128)(2,1)}), bf16[1,256,2,1024]{3,2,0,1:T(2,128)(2,1)S(1)}, u32[]{:S(2)}, u32[]{:S(2)}) async-start(bf16[1,256,2,1024]{3,2,0,1:T(2,128)(2,1)} %bitcast.50), calls=%async_computation | async-start | bytes 2097152 | tf_op jit(solution)/shard_map/all_to_all | solution.py:370
  10.9 0.0 copy-done.3
  11.0 2.7 %collective-permute-start = (bf16[4,8,1536]{2,1,0:T(8,128)(2,1)S(1)}, bf16[4,8,1536]{2,1,0:T(8,128)(2,1)S(1)}, u32[]{:S(2)}, u32[]{:S(2)}) collective-permute-start(bf16[4,8,1536]{2,1,0:T(8,128)(2,1)S(1)} %dynamic-slice_bitcast_fusion), channel_id=1, source_target_pairs={{0,8},{1,9},{2,10},{3,11},{4,12},{5,13},{6,14},{7,15},{8,0},{9,1},... | collective-permute-start | bytes 294920 | tf_op jit(solution)/shard_map/ppermute | solution.py:357
  13.7 0.2 reshape_squeeze.10
  13.8 0.1 pad.4.query_ref
  13.9 0.0 copy-done.2
  13.9 0.0 copy-start
  13.9 2.2 %copy-done = bf16[1,8,128,2,1024]{4,3,2,1,0:T(2,128)(2,1)S(1)} copy-done((bf16[1,8,128,2,1024]{4,3,2,1,0:T(2,128)(2,1)S(1)}, bf16[1,8,128,2,1024]{4,3,2,1,0:T(2,128)(2,1)}, u32[]{:S(2)}) %copy-start) | copy-done | bytes 4194328
  16.1 0.0 copy-start.5
  16.1 10.9 %shard_map.78 = (f32[4,12,8,128]{3,2,1,0:T(8,128)S(1)}, f32[4,2,8,128]{3,2,1,0:T(8,128)S(1)}) custom-call(s32[8]{0:T(128)S(1)} %bitcast.48, bf16[8,8,16,128]{3,2,1,0:T(8,128)(2,1)S(1)} %pad.4.query_ref, bf16[8,128,2,1024]{3,2,1,0:T(2,128)(2,1)S(1)} %bitcast.43), custom_call_target="tpu_custom_call" | custom-call | bytes 65536 | tf_op jit(solution)/shard_map/pallas_call | solution.py:60
  27.0 0.0 collective-permute-done
  27.1 2.8 %collective-permute-start.1 = (bf16[2,2,8,1536]{3,2,1,0:T(8,128)(2,1)S(1)}, bf16[2,2,8,1536]{3,2,1,0:T(8,128)(2,1)S(1)}, u32[]{:S(2)}, u32[]{:S(2)}) collective-permute-start(bf16[2,2,8,1536]{3,2,1,0:T(8,128)(2,1)S(1)} %fusion), channel_id=1, source_target_pairs={{0,4},{1,5},{2,6},{3,7},{4,0},{5,1},{6,2},{7,3},{8,12},{9,13},{10,... | collective-permute-start | bytes 294920 | tf_op jit(solution)/shard_map/ppermute | solution.py:357
  29.9 0.0 copy-done.5
  29.9 0.1 select_reduce_fusion.listed_ref
  30.0 2.4 %collective-permute-done.1 = bf16[2,2,8,1536]{3,2,1,0:T(8,128)(2,1)S(1)} collective-permute-done((bf16[2,2,8,1536]{3,2,1,0:T(8,128)(2,1)S(1)}, bf16[2,2,8,1536]{3,2,1,0:T(8,128)(2,1)S(1)}, u32[]{:S(2)}, u32[]{:S(2)}) %collective-permute-start.1) | collective-permute-done | bytes 98336 | tf_op jit(solution)/shard_map/ppermute | solution.py:357
  32.5 4.2 %all-to-all-done = bf16[1,256,2,1024]{3,2,0,1:T(2,128)(2,1)S(1)} async-done(((bf16[1,256,2,1024]{3,2,0,1:T(2,128)(2,1)}), bf16[1,256,2,1024]{3,2,0,1:T(2,128)(2,1)S(1)}, u32[]{:S(2)}, u32[]{:S(2)}) %all-to-all-start) | async-done | bytes 1048608 | tf_op jit(solution)/shard_map/all_to_all | solution.py:370
  36.6 1.6 %shard_map.77 = bf16[16,8,16,2,128]{4,3,2,1,0:T(2,128)(2,1)} custom-call(s32[16]{0:T(128)S(1)} %select_reduce_fusion.listed_ref, bf16[16,16,2,1024]{3,2,1,0:T(2,128)(2,1)S(1)} %bitcast.46), custom_call_target="tpu_custom_call" | custom-call | bytes 4194304 | tf_op jit(solution)/shard_map/pallas_call | solution.py:328
  38.3 0.0 copy-start.4
  38.3 11.1 %all-to-all-start.1 = ((bf16[256,16,128]{2,1,0:T(8,128)(2,1)}), bf16[256,16,128]{2,1,0:T(8,128)(2,1)S(1)}, u32[]{:S(2)}, u32[]{:S(2)}) async-start(bf16[256,16,128]{2,1,0:T(8,128)(2,1)} %bitcast.2), calls=%async_computation.1 | async-start | bytes 2097152 | tf_op jit(solution)/shard_map/all_to_all | solution.py:386
  49.5 1.5 %collective-permute-start.2 = (bf16[1,2,2,8,1536]{4,3,2,1,0:T(8,128)(2,1)S(1)}, bf16[1,2,2,8,1536]{4,3,2,1,0:T(8,128)(2,1)S(1)}, u32[]{:S(2)}, u32[]{:S(2)}) collective-permute-start(bf16[1,2,2,8,1536]{4,3,2,1,0:T(8,128)(2,1)S(1)} %constant_dynamic-slice_fusion), channel_id=1, source_target_pairs={{0,2},{1,3},{2,0},{3,1},{4,6},{5,7},{6,4},{7,5},{8,10},{9,11},{10,... | collective-permute-start | bytes 294920 | tf_op jit(solution)/shard_map/ppermute | solution.py:357
  50.9 0.0 copy-done.4
  50.9 0.1 reshape_squeeze.11
  51.0 3.4 %collective-permute-done.2 = bf16[1,2,2,8,1536]{4,3,2,1,0:T(8,128)(2,1)S(1)} collective-permute-done((bf16[1,2,2,8,1536]{4,3,2,1,0:T(8,128)(2,1)S(1)}, bf16[1,2,2,8,1536]{4,3,2,1,0:T(8,128)(2,1)S(1)}, u32[]{:S(2)}, u32[]{:S(2)}) %collective-permute-start.2) | collective-permute-done | bytes 98336 | tf_op jit(solution)/shard_map/ppermute | solution.py:357
  54.5 2.7 %collective-permute-start.3 = (bf16[1,2,2,2,8,1536]{5,4,3,2,1,0:T(8,128)(2,1)S(1)}, bf16[1,2,2,2,8,1536]{5,4,3,2,1,0:T(8,128)(2,1)S(1)}, u32[]{:S(2)}, u32[]{:S(2)}) collective-permute-start(bf16[1,2,2,2,8,1536]{5,4,3,2,1,0:T(8,128)(2,1)S(1)} %pad_maximum_fusion.2), channel_id=1, source_target_pairs={{0,1},{1,0},{2,3},{3,2},{4,5},{5,4},{6,7},{7,6},{8,9},{9,8},{10,11... | collective-permute-start | bytes 589832 | tf_op jit(solution)/shard_map/ppermute | solution.py:357
  57.2 0.0 copy-start.1
  57.2 2.2 %copy-done.1 = bf16[1,8,128,2,1024]{4,3,2,1,0:T(2,128)(2,1)S(1)} copy-done((bf16[1,8,128,2,1024]{4,3,2,1,0:T(2,128)(2,1)S(1)}, bf16[1,8,128,2,1024]{4,3,2,1,0:T(2,128)(2,1)}, u32[]{:S(2)}) %copy-start.1) | copy-done | bytes 4194328
  59.4 10.9 %shard_map.79 = (f32[4,12,8,128]{3,2,1,0:T(8,128)S(1)}, f32[4,2,8,128]{3,2,1,0:T(8,128)S(1)}) custom-call(s32[8]{0:T(128)S(1)} %bitcast.49, bf16[8,8,16,128]{3,2,1,0:T(8,128)(2,1)S(1)} %pad.4.query_ref, bf16[8,128,2,1024]{3,2,1,0:T(2,128)(2,1)S(1)} %bitcast.44), custom_call_target="tpu_custom_call" | custom-call | bytes 65536 | tf_op jit(solution)/shard_map/pallas_call | solution.py:60
  70.3 0.0 collective-permute-done.3
  70.4 10.3 %all-to-all-done.1.pair_ref = bf16[256,16,128]{2,1,0:T(8,128)(2,1)S(1)} async-done(((bf16[256,16,128]{2,1,0:T(8,128)(2,1)}), bf16[256,16,128]{2,1,0:T(8,128)(2,1)S(1)}, u32[]{:S(2)}, u32[]{:S(2)}) %all-to-all-start.1) | async-done | bytes 1048608 | tf_op jit(solution)/shard_map/all_to_all | solution.py:386
  80.7 4.5 %shard_map.80 = bf16[16,368,128]{2,1,0:T(8,128)(2,1)S(1)} custom-call(s32[256]{0:T(256)S(1)} %fusion.5.listed_ref, bf16[128,1536]{1,0:T(8,128)(2,1)S(1)} %bitcast.47, bf16[256,16,128]{2,1,0:T(8,128)(2,1)S(1)} %all-to-all-done.1.pair_ref), custom_call_target="tpu_custom_call" | custom-call | flops 1610612736 | bytes 4194304 | tf_op jit(solution)/shard_map/pallas_call | solution.py:165
  85.2 25.9 %all_to_all.22.came_ref = bf16[16,368,128]{2,1,0:T(8,128)(2,1)S(1)} all-to-all(bf16[16,368,128]{2,1,0:T(8,128)(2,1)S(1)} %shard_map.80), channel_id=1, replica_groups=mesh['inst'=16,'samp'=16] {'samp'}, dimensions={0} | all-to-all | bytes 3014656 | tf_op jit(solution)/shard_map/all_to_all | solution.py:395
  111.1 1.6 %shard_map.81 = (bf16[8,12288]{1,0:T(8,128)(2,1)}, bf16[16,16,2,1024]{3,2,1,0:T(2,128)(2,1)}) custom-call(bf16[16,23,8,2,128]{4,3,2,1,0:T(2,128)(2,1)S(1)} %bitcast.45, bf16[16,368,128]{2,1,0:T(8,128)(2,1)S(1)} %all_to_all.22.came_ref, f32[4,12,8,128]{3,2,1,0:T(8,128)S(1)} %get-tuple-element.32.refs_0_, f32[4,2,8,128]{3,2,1,0:T(8,128)S(1)} %get-tuple-element.33.refs_1_, ...), custom_call_target="tpu_custom_call" | custom-call | flops 589824 | bytes 4194304 | tf_op jit(solution)/shard_map/pallas_call | solution.py:271
  (11 shorter events, 0.2 us)
Async XLA Ops:
  0.6 10.3 %copy-start.3 = (bf16[1,8,12288]{2,1,0:T(8,128)(2,1)S(1)}, bf16[1,8,12288]{2,1,0:T(8,128)(2,1)}, u32[]{:S(2)}) copy-start(bf16[1,8,12288]{2,1,0:T(8,128)(2,1)} %param.9) | copy-start | bytes 589828
  0.6 13.3 %copy-start.2 = (s32[1,8]{1,0:T(1,128)S(1)}, s32[1,8]{1,0:T(1,128)}, u32[]{:S(2)}) copy-start(s32[1,8]{1,0:T(1,128)} %param.11) | copy-start | bytes 100
  0.6 36.0 %all-to-all-start = ((bf16[1,256,2,1024]{3,2,0,1:T(2,128)(2,1)}), bf16[1,256,2,1024]{3,2,0,1:T(2,128)(2,1)S(1)}, u32[]{:S(2)}, u32[]{:S(2)}) async-start(bf16[1,256,2,1024]{3,2,0,1:T(2,128)(2,1)} %bitcast.50), calls=%async_computation | async-start | bytes 2097152 | tf_op jit(solution)/shard_map/all_to_all | solution.py:370
  11.0 16.0 %collective-permute-start = (bf16[4,8,1536]{2,1,0:T(8,128)(2,1)S(1)}, bf16[4,8,1536]{2,1,0:T(8,128)(2,1)S(1)}, u32[]{:S(2)}, u32[]{:S(2)}) collective-permute-start(bf16[4,8,1536]{2,1,0:T(8,128)(2,1)S(1)} %dynamic-slice_bitcast_fusion), channel_id=1, source_target_pairs={{0,8},{1,9},{2,10},{3,11},{4,12},{5,13},{6,14},{7,15},{8,0},{9,1},... | collective-permute-start | bytes 294920 | tf_op jit(solution)/shard_map/ppermute | solution.py:357
  13.9 2.2 %copy-start = (bf16[1,8,128,2,1024]{4,3,2,1,0:T(2,128)(2,1)S(1)}, bf16[1,8,128,2,1024]{4,3,2,1,0:T(2,128)(2,1)}, u32[]{:S(2)}) copy-start(bf16[1,8,128,2,1024]{4,3,2,1,0:T(2,128)(2,1)} %param.10) | copy-start | bytes 12582916
  16.1 13.8 %copy-start.5 = (s32[16]{0:T(128)S(1)}, s32[16]{0:T(128)}, u32[]{:S(2)}) copy-start(s32[16]{0:T(128)} %param.7) | copy-start | bytes 196
  27.1 5.4 %collective-permute-start.1 = (bf16[2,2,8,1536]{3,2,1,0:T(8,128)(2,1)S(1)}, bf16[2,2,8,1536]{3,2,1,0:T(8,128)(2,1)S(1)}, u32[]{:S(2)}, u32[]{:S(2)}) collective-permute-start(bf16[2,2,8,1536]{3,2,1,0:T(8,128)(2,1)S(1)} %fusion), channel_id=1, source_target_pairs={{0,4},{1,5},{2,6},{3,7},{4,0},{5,1},{6,2},{7,3},{8,12},{9,13},{10,... | collective-permute-start | bytes 294920 | tf_op jit(solution)/shard_map/ppermute | solution.py:357
  38.3 12.7 %copy-start.4 = (s32[1,16,16]{2,1,0:T(8,128)S(1)}, s32[1,16,16]{2,1,0:T(8,128)}, u32[]{:S(2)}) copy-start(s32[1,16,16]{2,1,0:T(8,128)} %param.8) | copy-start | bytes 3076
  38.3 42.4 %all-to-all-start.1 = ((bf16[256,16,128]{2,1,0:T(8,128)(2,1)}), bf16[256,16,128]{2,1,0:T(8,128)(2,1)S(1)}, u32[]{:S(2)}, u32[]{:S(2)}) async-start(bf16[256,16,128]{2,1,0:T(8,128)(2,1)} %bitcast.2), calls=%async_computation.1 | async-start | bytes 2097152 | tf_op jit(solution)/shard_map/all_to_all | solution.py:386
  49.5 5.0 %collective-permute-start.2 = (bf16[1,2,2,8,1536]{4,3,2,1,0:T(8,128)(2,1)S(1)}, bf16[1,2,2,8,1536]{4,3,2,1,0:T(8,128)(2,1)S(1)}, u32[]{:S(2)}, u32[]{:S(2)}) collective-permute-start(bf16[1,2,2,8,1536]{4,3,2,1,0:T(8,128)(2,1)S(1)} %constant_dynamic-slice_fusion), channel_id=1, source_target_pairs={{0,2},{1,3},{2,0},{3,1},{4,6},{5,7},{6,4},{7,5},{8,10},{9,11},{10,... | collective-permute-start | bytes 294920 | tf_op jit(solution)/shard_map/ppermute | solution.py:357
  54.5 15.8 %collective-permute-start.3 = (bf16[1,2,2,2,8,1536]{5,4,3,2,1,0:T(8,128)(2,1)S(1)}, bf16[1,2,2,2,8,1536]{5,4,3,2,1,0:T(8,128)(2,1)S(1)}, u32[]{:S(2)}, u32[]{:S(2)}) collective-permute-start(bf16[1,2,2,2,8,1536]{5,4,3,2,1,0:T(8,128)(2,1)S(1)} %pad_maximum_fusion.2), channel_id=1, source_target_pairs={{0,1},{1,0},{2,3},{3,2},{4,5},{5,4},{6,7},{7,6},{8,9},{9,8},{10,11... | collective-permute-start | bytes 589832 | tf_op jit(solution)/shard_map/ppermute | solution.py:357
  57.2 2.2 %copy-start.1 = (bf16[1,8,128,2,1024]{4,3,2,1,0:T(2,128)(2,1)S(1)}, bf16[1,8,128,2,1024]{4,3,2,1,0:T(2,128)(2,1)}, u32[]{:S(2)}) copy-start(bf16[1,8,128,2,1024]{4,3,2,1,0:T(2,128)(2,1)} %param.10) | copy-start | bytes 12582916

commit v11 on v10

--- a/solution.py
+++ b/solution.py
@@ -126,6 +126,11 @@
             query, key_ref[...], (((1,), (1,)), ((), ())), preferred_element_type=jnp.float32
         )
 
+    def send(g, weights):
+        numer = jnp.dot(weights, value_ref[...], preferred_element_type=jnp.float32)
+        first = slots * rows + g * local
+        out_ref[:, first : first + 2 * local, :] = side_by_side(numer[:samples], numer[samples:])
+
     later = scores_of(0)
     fetch.wait()
     for g in range(0, GROUP, 2):
@@ -138,11 +143,9 @@
         top = jnp.max(scores, axis=-1, keepdims=True)
         weights = jnp.exp2((scores - top) * factor)
         total = jnp.sum(weights, axis=-1, keepdims=True)
-        numer = jnp.dot(
-            weights.astype(jnp.bfloat16), value_ref[...], preferred_element_type=jnp.float32
-        )
-        first = slots * rows + g * local
-        out_ref[:, first : first + 2 * local, :] = side_by_side(numer[:samples], numer[samples:])
+        weights = weights.astype(jnp.bfloat16)
+        if g + 2 < GROUP:
+            send(g, weights)
         top = top * SCALE
         peaks = jnp.where(lane == g, top[:samples], peaks)
         peaks = jnp.where(lane == g + 1, top[samples:], peaks)
@@ -155,6 +158,7 @@
         stats = stats + (pltpu.roll(term, place * GROUP, 1) if place else term)
     first = slots * rows + GROUP * local
     out_ref[:, first:, :] = side_by_side(stats, jnp.zeros_like(stats))
+    send(GROUP - 2, weights)
 
 
 def partial_shared(place, query_rows, pairs, owners):
@@ -251,14 +255,13 @@
                 value = (mine[0] * by[0] + mine[1] * by[1]) + mine[2] * by[2]
                 column = (head * GROUP + g + k) * HEAD_FEATURES
                 out_ref[:, column : column + HEAD_FEATURES] = value.astype(jnp.bfloat16)
-        if head % 4 == 3:
-            columns = slice((head - 3) * WIDTH, (head + 1) * WIDTH)
-            copies.append(
-                pltpu.make_async_copy(
-                    out_ref.at[:, columns], to_ref.at[:, columns], sems.at[senders + head]
-                )
+        columns = slice(head * WIDTH, (head + 1) * WIDTH)
+        copies.append(
+            pltpu.make_async_copy(
+                out_ref.at[:, columns], to_ref.at[:, columns], sems.at[senders + head]
             )
-            copies[-1].start()
+        )
+        copies[-1].start()
 
     for copy in copies:
         copy.wait()

time: 113 us -> 113 us (level)
  no operation moved by 1% of the time
where the time goes in v11:
time: 113 us
  starting transfers between devices  31.1 us (28%)
  Pallas kernels  29.4 us (26%)
  blocking collectives  25.9 us (23%)
  waiting for transfers between devices  20.3 us (18%)
  local copies, waits for them, and re-layouts  4.7 us (4%)
    all_to_all x1, blocking collectives, body(): came = lax.all_to_all(sent, 'samp', split_axis=0, concat_axis=0, tiled=True)  25.9 us
    pallas_call x2, Pallas kernels, partial_own(): pl.pallas_call(functools.partial(own_kernel, which * heads), grid=(1,), o...  21.7 us
    all_to_all x1, starting transfers between devices, body(): lax.all_to_all(chosen, ('inst', 'samp'), split_axis=0, concat_axis=0, til...  11.1 us
    all_to_all x1, waiting for transfers between devices, body(): lax.all_to_all(chosen, ('inst', 'samp'), split_axis=0, concat_axis=0, til...  10.3 us
    all_to_all x1, starting transfers between devices, body(): lax.all_to_all(prompt_key_values, 'inst', split_axis=1, concat_axis=0, ti...  10.3 us
    ppermute x4, starting transfers between devices, exchange(): lax.ppermute(sent, 'samp', [(i, i ^ 1 << place) for i in range(n_samp)])  9.71 us
    ppermute x4, waiting for transfers between devices, exchange(): lax.ppermute(sent, 'samp', [(i, i ^ 1 << place) for i in range(n_samp)])  5.86 us
    pallas_call x1, Pallas kernels, partial_shared(): pl.pallas_call(shared_kernel, out_shape=jax.ShapeDtypeStruct((owners, sen...  4.53 us
  transfers between devices with their start and end apart: 6, of which 4 were waited for; matrix products, arithmetic and copies ran while one was open for 1% of the time, Pallas kernels for 19%

profile of v11, /device:TPU:1, one launch (start us, length us, event | category | flops | bytes accessed | tf_op | source)
XLA Modules:
  0.0 112.6 jit_solution(14245593941386665526)
XLA Ops:
  0.6 0.0 copy-start.3
  0.6 0.0 copy-start.2
  0.6 10.3 %all-to-all-start = ((bf16[1,256,2,1024]{3,2,0,1:T(2,128)(2,1)}), bf16[1,256,2,1024]{3,2,0,1:T(2,128)(2,1)S(1)}, u32[]{:S(2)}, u32[]{:S(2)}) async-start(bf16[1,256,2,1024]{3,2,0,1:T(2,128)(2,1)} %bitcast.50), calls=%async_computation | async-start | bytes 2097152 | tf_op jit(solution)/shard_map/all_to_all | solution.py:373
  10.9 0.0 copy-done.3
  11.0 2.7 %collective-permute-start = (bf16[4,8,1536]{2,1,0:T(8,128)(2,1)S(1)}, bf16[4,8,1536]{2,1,0:T(8,128)(2,1)S(1)}, u32[]{:S(2)}, u32[]{:S(2)}) collective-permute-start(bf16[4,8,1536]{2,1,0:T(8,128)(2,1)S(1)} %dynamic-slice_bitcast_fusion), channel_id=1, source_target_pairs={{0,8},{1,9},{2,10},{3,11},{4,12},{5,13},{6,14},{7,15},{8,0},{9,1},... | collective-permute-start | bytes 294920 | tf_op jit(solution)/shard_map/ppermute | solution.py:360
  13.7 0.2 reshape_squeeze.10
  13.8 0.1 pad.4.query_ref
  13.9 0.0 copy-done.2
  13.9 0.0 copy-start
  13.9 2.2 %copy-done = bf16[1,8,128,2,1024]{4,3,2,1,0:T(2,128)(2,1)S(1)} copy-done((bf16[1,8,128,2,1024]{4,3,2,1,0:T(2,128)(2,1)S(1)}, bf16[1,8,128,2,1024]{4,3,2,1,0:T(2,128)(2,1)}, u32[]{:S(2)}) %copy-start) | copy-done | bytes 4194328
  16.1 0.0 copy-start.5
  16.1 10.9 %shard_map.78 = (f32[4,12,8,128]{3,2,1,0:T(8,128)S(1)}, f32[4,2,8,128]{3,2,1,0:T(8,128)S(1)}) custom-call(s32[8]{0:T(128)S(1)} %bitcast.48, bf16[8,8,16,128]{3,2,1,0:T(8,128)(2,1)S(1)} %pad.4.query_ref, bf16[8,128,2,1024]{3,2,1,0:T(2,128)(2,1)S(1)} %bitcast.43), custom_call_target="tpu_custom_call" | custom-call | bytes 65536 | tf_op jit(solution)/shard_map/pallas_call | solution.py:60
  27.0 0.0 collective-permute-done
  27.1 2.8 %collective-permute-start.1 = (bf16[2,2,8,1536]{3,2,1,0:T(8,128)(2,1)S(1)}, bf16[2,2,8,1536]{3,2,1,0:T(8,128)(2,1)S(1)}, u32[]{:S(2)}, u32[]{:S(2)}) collective-permute-start(bf16[2,2,8,1536]{3,2,1,0:T(8,128)(2,1)S(1)} %fusion), channel_id=1, source_target_pairs={{0,4},{1,5},{2,6},{3,7},{4,0},{5,1},{6,2},{7,3},{8,12},{9,13},{10,... | collective-permute-start | bytes 294920 | tf_op jit(solution)/shard_map/ppermute | solution.py:360
  29.9 0.0 copy-done.5
  29.9 0.1 select_reduce_fusion.listed_ref
  30.0 2.4 %collective-permute-done.1 = bf16[2,2,8,1536]{3,2,1,0:T(8,128)(2,1)S(1)} collective-permute-done((bf16[2,2,8,1536]{3,2,1,0:T(8,128)(2,1)S(1)}, bf16[2,2,8,1536]{3,2,1,0:T(8,128)(2,1)S(1)}, u32[]{:S(2)}, u32[]{:S(2)}) %collective-permute-start.1) | collective-permute-done | bytes 98336 | tf_op jit(solution)/shard_map/ppermute | solution.py:360
  32.5 4.2 %all-to-all-done = bf16[1,256,2,1024]{3,2,0,1:T(2,128)(2,1)S(1)} async-done(((bf16[1,256,2,1024]{3,2,0,1:T(2,128)(2,1)}), bf16[1,256,2,1024]{3,2,0,1:T(2,128)(2,1)S(1)}, u32[]{:S(2)}, u32[]{:S(2)}) %all-to-all-start) | async-done | bytes 1048608 | tf_op jit(solution)/shard_map/all_to_all | solution.py:373
  36.6 1.6 %shard_map.77 = bf16[16,8,16,2,128]{4,3,2,1,0:T(2,128)(2,1)} custom-call(s32[16]{0:T(128)S(1)} %select_reduce_fusion.listed_ref, bf16[16,16,2,1024]{3,2,1,0:T(2,128)(2,1)S(1)} %bitcast.46), custom_call_target="tpu_custom_call" | custom-call | bytes 4194304 | tf_op jit(solution)/shard_map/pallas_call | solution.py:331
  38.3 0.0 copy-start.4
  38.3 11.1 %all-to-all-start.1 = ((bf16[256,16,128]{2,1,0:T(8,128)(2,1)}), bf16[256,16,128]{2,1,0:T(8,128)(2,1)S(1)}, u32[]{:S(2)}, u32[]{:S(2)}) async-start(bf16[256,16,128]{2,1,0:T(8,128)(2,1)} %bitcast.2), calls=%async_computation.1 | async-start | bytes 2097152 | tf_op jit(solution)/shard_map/all_to_all | solution.py:389
  49.5 1.5 %collective-permute-start.2 = (bf16[1,2,2,8,1536]{4,3,2,1,0:T(8,128)(2,1)S(1)}, bf16[1,2,2,8,1536]{4,3,2,1,0:T(8,128)(2,1)S(1)}, u32[]{:S(2)}, u32[]{:S(2)}) collective-permute-start(bf16[1,2,2,8,1536]{4,3,2,1,0:T(8,128)(2,1)S(1)} %constant_dynamic-slice_fusion), channel_id=1, source_target_pairs={{0,2},{1,3},{2,0},{3,1},{4,6},{5,7},{6,4},{7,5},{8,10},{9,11},{10,... | collective-permute-start | bytes 294920 | tf_op jit(solution)/shard_map/ppermute | solution.py:360
  50.9 0.0 copy-done.4
  50.9 0.1 reshape_squeeze.11
  51.0 3.4 %collective-permute-done.2 = bf16[1,2,2,8,1536]{4,3,2,1,0:T(8,128)(2,1)S(1)} collective-permute-done((bf16[1,2,2,8,1536]{4,3,2,1,0:T(8,128)(2,1)S(1)}, bf16[1,2,2,8,1536]{4,3,2,1,0:T(8,128)(2,1)S(1)}, u32[]{:S(2)}, u32[]{:S(2)}) %collective-permute-start.2) | collective-permute-done | bytes 98336 | tf_op jit(solution)/shard_map/ppermute | solution.py:360
  54.5 2.7 %collective-permute-start.3 = (bf16[1,2,2,2,8,1536]{5,4,3,2,1,0:T(8,128)(2,1)S(1)}, bf16[1,2,2,2,8,1536]{5,4,3,2,1,0:T(8,128)(2,1)S(1)}, u32[]{:S(2)}, u32[]{:S(2)}) collective-permute-start(bf16[1,2,2,2,8,1536]{5,4,3,2,1,0:T(8,128)(2,1)S(1)} %pad_maximum_fusion.2), channel_id=1, source_target_pairs={{0,1},{1,0},{2,3},{3,2},{4,5},{5,4},{6,7},{7,6},{8,9},{9,8},{10,11... | collective-permute-start | bytes 589832 | tf_op jit(solution)/shard_map/ppermute | solution.py:360
  57.2 0.0 copy-start.1
  57.2 2.2 %copy-done.1 = bf16[1,8,128,2,1024]{4,3,2,1,0:T(2,128)(2,1)S(1)} copy-done((bf16[1,8,128,2,1024]{4,3,2,1,0:T(2,128)(2,1)S(1)}, bf16[1,8,128,2,1024]{4,3,2,1,0:T(2,128)(2,1)}, u32[]{:S(2)}) %copy-start.1) | copy-done | bytes 4194328
  59.4 10.9 %shard_map.79 = (f32[4,12,8,128]{3,2,1,0:T(8,128)S(1)}, f32[4,2,8,128]{3,2,1,0:T(8,128)S(1)}) custom-call(s32[8]{0:T(128)S(1)} %bitcast.49, bf16[8,8,16,128]{3,2,1,0:T(8,128)(2,1)S(1)} %pad.4.query_ref, bf16[8,128,2,1024]{3,2,1,0:T(2,128)(2,1)S(1)} %bitcast.44), custom_call_target="tpu_custom_call" | custom-call | bytes 65536 | tf_op jit(solution)/shard_map/pallas_call | solution.py:60
  70.3 0.0 collective-permute-done.3
  70.4 10.3 %all-to-all-done.1.pair_ref = bf16[256,16,128]{2,1,0:T(8,128)(2,1)S(1)} async-done(((bf16[256,16,128]{2,1,0:T(8,128)(2,1)}), bf16[256,16,128]{2,1,0:T(8,128)(2,1)S(1)}, u32[]{:S(2)}, u32[]{:S(2)}) %all-to-all-start.1) | async-done | bytes 1048608 | tf_op jit(solution)/shard_map/all_to_all | solution.py:389
  80.7 4.5 %shard_map.80 = bf16[16,368,128]{2,1,0:T(8,128)(2,1)S(1)} custom-call(s32[256]{0:T(256)S(1)} %fusion.5.listed_ref, bf16[128,1536]{1,0:T(8,128)(2,1)S(1)} %bitcast.47, bf16[256,16,128]{2,1,0:T(8,128)(2,1)S(1)} %all-to-all-done.1.pair_ref), custom_call_target="tpu_custom_call" | custom-call | flops 1610612736 | bytes 4194304 | tf_op jit(solution)/shard_map/pallas_call | solution.py:169
  85.2 25.9 %all_to_all.22.came_ref = bf16[16,368,128]{2,1,0:T(8,128)(2,1)S(1)} all-to-all(bf16[16,368,128]{2,1,0:T(8,128)(2,1)S(1)} %shard_map.80), channel_id=1, replica_groups=mesh['inst'=16,'samp'=16] {'samp'}, dimensions={0} | all-to-all | bytes 3014656 | tf_op jit(solution)/shard_map/all_to_all | solution.py:398
  111.1 1.5 %shard_map.81 = (bf16[8,12288]{1,0:T(8,128)(2,1)}, bf16[16,16,2,1024]{3,2,1,0:T(2,128)(2,1)}) custom-call(bf16[16,23,8,2,128]{4,3,2,1,0:T(2,128)(2,1)S(1)} %bitcast.45, bf16[16,368,128]{2,1,0:T(8,128)(2,1)S(1)} %all_to_all.22.came_ref, f32[4,12,8,128]{3,2,1,0:T(8,128)S(1)} %get-tuple-element.32.refs_0_, f32[4,2,8,128]{3,2,1,0:T(8,128)S(1)} %get-tuple-element.33.refs_1_, ...), custom_call_target="tpu_custom_call" | custom-call | flops 589824 | bytes 4194304 | tf_op jit(solution)/shard_map/pallas_call | solution.py:274
  (11 shorter events, 0.2 us)
Async XLA Ops:
  0.6 10.3 %copy-start.3 = (bf16[1,8,12288]{2,1,0:T(8,128)(2,1)S(1)}, bf16[1,8,12288]{2,1,0:T(8,128)(2,1)}, u32[]{:S(2)}) copy-start(bf16[1,8,12288]{2,1,0:T(8,128)(2,1)} %param.9) | copy-start | bytes 589828
  0.6 13.3 %copy-start.2 = (s32[1,8]{1,0:T(1,128)S(1)}, s32[1,8]{1,0:T(1,128)}, u32[]{:S(2)}) copy-start(s32[1,8]{1,0:T(1,128)} %param.11) | copy-start | bytes 100
  0.6 36.0 %all-to-all-start = ((bf16[1,256,2,1024]{3,2,0,1:T(2,128)(2,1)}), bf16[1,256,2,1024]{3,2,0,1:T(2,128)(2,1)S(1)}, u32[]{:S(2)}, u32[]{:S(2)}) async-start(bf16[1,256,2,1024]{3,2,0,1:T(2,128)(2,1)} %bitcast.50), calls=%async_computation | async-start | bytes 2097152 | tf_op jit(solution)/shard_map/all_to_all | solution.py:373
  11.0 16.0 %collective-permute-start = (bf16[4,8,1536]{2,1,0:T(8,128)(2,1)S(1)}, bf16[4,8,1536]{2,1,0:T(8,128)(2,1)S(1)}, u32[]{:S(2)}, u32[]{:S(2)}) collective-permute-start(bf16[4,8,1536]{2,1,0:T(8,128)(2,1)S(1)} %dynamic-slice_bitcast_fusion), channel_id=1, source_target_pairs={{0,8},{1,9},{2,10},{3,11},{4,12},{5,13},{6,14},{7,15},{8,0},{9,1},... | collective-permute-start | bytes 294920 | tf_op jit(solution)/shard_map/ppermute | solution.py:360
  13.9 2.2 %copy-start = (bf16[1,8,128,2,1024]{4,3,2,1,0:T(2,128)(2,1)S(1)}, bf16[1,8,128,2,1024]{4,3,2,1,0:T(2,128)(2,1)}, u32[]{:S(2)}) copy-start(bf16[1,8,128,2,1024]{4,3,2,1,0:T(2,128)(2,1)} %param.10) | copy-start | bytes 12582916
  16.1 13.8 %copy-start.5 = (s32[16]{0:T(128)S(1)}, s32[16]{0:T(128)}, u32[]{:S(2)}) copy-start(s32[16]{0:T(128)} %param.7) | copy-start | bytes 196
  27.1 5.4 %collective-permute-start.1 = (bf16[2,2,8,1536]{3,2,1,0:T(8,128)(2,1)S(1)}, bf16[2,2,8,1536]{3,2,1,0:T(8,128)(2,1)S(1)}, u32[]{:S(2)}, u32[]{:S(2)}) collective-permute-start(bf16[2,2,8,1536]{3,2,1,0:T(8,128)(2,1)S(1)} %fusion), channel_id=1, source_target_pairs={{0,4},{1,5},{2,6},{3,7},{4,0},{5,1},{6,2},{7,3},{8,12},{9,13},{10,... | collective-permute-start | bytes 294920 | tf_op jit(solution)/shard_map/ppermute | solution.py:360
  38.3 12.7 %copy-start.4 = (s32[1,16,16]{2,1,0:T(8,128)S(1)}, s32[1,16,16]{2,1,0:T(8,128)}, u32[]{:S(2)}) copy-start(s32[1,16,16]{2,1,0:T(8,128)} %param.8) | copy-start | bytes 3076
  38.3 42.4 %all-to-all-start.1 = ((bf16[256,16,128]{2,1,0:T(8,128)(2,1)}), bf16[256,16,128]{2,1,0:T(8,128)(2,1)S(1)}, u32[]{:S(2)}, u32[]{:S(2)}) async-start(bf16[256,16,128]{2,1,0:T(8,128)(2,1)} %bitcast.2), calls=%async_computation.1 | async-start | bytes 2097152 | tf_op jit(solution)/shard_map/all_to_all | solution.py:389
  49.5 5.0 %collective-permute-start.2 = (bf16[1,2,2,8,1536]{4,3,2,1,0:T(8,128)(2,1)S(1)}, bf16[1,2,2,8,1536]{4,3,2,1,0:T(8,128)(2,1)S(1)}, u32[]{:S(2)}, u32[]{:S(2)}) collective-permute-start(bf16[1,2,2,8,1536]{4,3,2,1,0:T(8,128)(2,1)S(1)} %constant_dynamic-slice_fusion), channel_id=1, source_target_pairs={{0,2},{1,3},{2,0},{3,1},{4,6},{5,7},{6,4},{7,5},{8,10},{9,11},{10,... | collective-permute-start | bytes 294920 | tf_op jit(solution)/shard_map/ppermute | solution.py:360
  54.5 15.8 %collective-permute-start.3 = (bf16[1,2,2,2,8,1536]{5,4,3,2,1,0:T(8,128)(2,1)S(1)}, bf16[1,2,2,2,8,1536]{5,4,3,2,1,0:T(8,128)(2,1)S(1)}, u32[]{:S(2)}, u32[]{:S(2)}) collective-permute-start(bf16[1,2,2,2,8,1536]{5,4,3,2,1,0:T(8,128)(2,1)S(1)} %pad_maximum_fusion.2), channel_id=1, source_target_pairs={{0,1},{1,0},{2,3},{3,2},{4,5},{5,4},{6,7},{7,6},{8,9},{9,8},{10,11... | collective-permute-start | bytes 589832 | tf_op jit(solution)/shard_map/ppermute | solution.py:360
  57.2 2.2 %copy-start.1 = (bf16[1,8,128,2,1024]{4,3,2,1,0:T(2,128)(2,1)S(1)}, bf16[1,8,128,2,1024]{4,3,2,1,0:T(2,128)(2,1)}, u32[]{:S(2)}) copy-start(bf16[1,8,128,2,1024]{4,3,2,1,0:T(2,128)(2,1)} %param.10) | copy-start | bytes 12582916
